TPU v7x, 32 devices: a whole 2x2x4 slice. The times are simulated.
32 devices in a mesh: group: 4 (over y, core), pair: 8 (over z, x).
Axes of the slice: x: 2, y: 2, z: 4, core: 2. Of those that a mesh axis runs over, the one named last changes fastest.
Arguments:
- genotypes: int32 [4096, 16384], P(None, ('group', 'pair')), may hold values from 0 to 2, as said below
- dest_group: int32 [64], replicated, may hold values from 0 to 3, as said below
Outputs:
- rotated: bfloat16 [4096, 16384], P(None, ('group', 'pair'))
Inputs may be any that keep to these rules, and one draw needn't show every extreme that they name: For every pair index p and side k there is an offset s with dest_group[(g * 8 + p) * 2 + k] = (g + s) mod 4 for all g, and the two sides have different offsets; so every position (t, p, k) receives exactly one block. `genotypes`: allele counts of two alleles.
All inputs are finite; a program needn't handle non-finite values.
Results may differ from a plain program's by a relative error of at most 0.0077.
Values may be sent and summed in bfloat16 or wider, within the bound.
No kernel may reach another device: no remote copies, remote signals or barrier semaphores. Data moves between devices by JAX's collectives and lax.ppermute only.
A program may use at most 128 MiB of HBM per device.

v0:
```python
import jax
import jax.numpy as jnp
from jax import lax
from jax.sharding import PartitionSpec as P

ROUNDS = 3


epsilon = 1e-05


def passed_along(array, axis, by):
    size = lax.axis_size(axis)
    return lax.ppermute(array, axis, [(i, (i + by) % size) for i in range(size)])


def standardize(counts):
    values = counts.astype(jnp.float32)
    col_mean = jnp.mean(values, axis=0)
    centred = values - col_mean
    col_var = jnp.mean(centred * centred, axis=0)
    return (centred / jnp.sqrt(col_var + epsilon)).astype(jnp.bfloat16)


def rotation_for(top_block, low_block):
    blk_width = top_block.shape[1]
    top_wide = top_block.astype(jnp.float32)
    low_wide = low_block.astype(jnp.float32)
    norm_top = jnp.sum(top_wide * top_wide, axis=0)
    norm_low = jnp.sum(low_wide * low_wide, axis=0)
    cross_gram = lax.dot_general(
        top_block, low_block, (((0,), (0,)), ((), ())), preferred_element_type=jnp.float32
    )
    coupling = 2.0 * cross_gram / (norm_top[:, None] + norm_low[None, :] + epsilon)
    zero_block = jnp.zeros((blk_width, blk_width), jnp.float32)
    skew_part = jnp.concatenate(
        [
            jnp.concatenate([zero_block, coupling], axis=1),
            jnp.concatenate([-coupling.T, zero_block], axis=1),
        ],
        axis=0,
    )
    identity = jnp.eye(2 * blk_width, dtype=jnp.float32)
    gram_matrix = identity + jnp.dot(skew_part.T, skew_part, precision=lax.Precision.HIGHEST)
    factor = jnp.linalg.cholesky(gram_matrix)
    lifted = identity + skew_part
    rotation = jax.scipy.linalg.solve_triangular(factor, lifted.T, lower=True).T
    return rotation.astype(jnp.bfloat16)


def body(genotypes, dest_group):
    num_groups = lax.axis_size("group")
    num_pairs = lax.axis_size("pair")
    own_group = lax.axis_index("group")
    own_pair = lax.axis_index("pair")
    blk_width = genotypes.shape[1] // 2
    scaled = standardize(genotypes)
    first_block = scaled[:, :blk_width]
    second_block = scaled[:, blk_width:]
    dest_table = dest_group.reshape(num_groups, num_pairs, 2)
    column = lax.dynamic_index_in_dim(dest_table, own_pair, 1, keepdims=False)
    own_dest = lax.dynamic_index_in_dim(column, own_group, 0, keepdims=False)
    offset_zero = (own_dest[0] - own_group) % num_groups
    offset_one = (own_dest[1] - own_group) % num_groups
    top_block = jnp.where(offset_zero == 0, first_block, jnp.zeros_like(first_block))
    low_block = jnp.where(offset_one == 0, second_block, jnp.zeros_like(second_block))
    for distance in range(1, num_groups):
        outgoing = jnp.where(offset_zero == distance, first_block, second_block)
        incoming = passed_along(outgoing, "group", distance)
        top_block = jnp.where(offset_zero == distance, incoming, top_block)
        low_block = jnp.where(offset_one == distance, incoming, low_block)
    for cycle_round in range(ROUNDS):
        rotation = rotation_for(top_block, low_block)
        joined = jnp.concatenate([top_block, low_block], axis=1)
        result = jnp.dot(joined, rotation, preferred_element_type=jnp.float32).astype(jnp.bfloat16)
        top_block = result[:, :blk_width]
        low_block = passed_along(result[:, blk_width:], "pair", 1)
    return jnp.concatenate([top_block, low_block], axis=1)


def solution(mesh):
    in_specs = (P(None, ("group", "pair")), P())
    out_specs = P(None, ("group", "pair"))
    return jax.shard_map(body, mesh=mesh, in_specs=in_specs, out_specs=out_specs, check_vma=False)
```

profile of v0, /device:TPU:1, one launch (start us, length us, event | category | flops | bytes accessed | tf_op | source)
XLA Modules:
  0.0 720.1 jit_solution(12750321729995527971)
XLA Ops:
  19.6 44.1 %collective-permute-done = bf16[4096,256]{1,0:T(8,128)(2,1)} collective-permute-done((bf16[4096,256]{1,0:T(8,128)(2,1)}, bf16[4096,256]{1,0:T(8,128)(2,1)}, u32[]{:S(2)}, u32[]{:S(2)}) %collective-permute-start) | collective-permute-done | bytes 2097184 | tf_op jit(solution)/shard_map/ppermute | solution.py:14
  63.7 43.9 %collective-permute-done.2 = bf16[4096,256]{1,0:T(8,128)(2,1)} collective-permute-done((bf16[4096,256]{1,0:T(8,128)(2,1)}, bf16[4096,256]{1,0:T(8,128)(2,1)}, u32[]{:S(2)}, u32[]{:S(2)}) %collective-permute-start.2) | collective-permute-done | bytes 2097184 | tf_op jit(solution)/shard_map/ppermute | solution.py:14
  120.5 11.7 %cholesky.374 = f32[128,128]{1,0:T(8,128)S(1)} custom-call(f32[128,128]{1,0:T(8,128)S(1)} %cholesky.586), custom_call_target="Cholesky" | custom-call | tf_op jit(solution)/shard_map/jit(cholesky)/cholesky | solution.py:45
  132.4 9.8 %custom-call.31 = f32[1,128,128]{1,2,0:T(8,128)S(1)} custom-call(f32[1,128,128]{2,1,0:T(8,128)S(1)} %get-tuple-element.104), custom_call_target="InvertDiagBlocksLowerTriangular" | custom-call | tf_op jit(solution)/shard_map/jit(cholesky)/cholesky | solution.py:45
  144.7 11.9 %cholesky.393 = f32[128,128]{1,0:T(8,128)S(1)} custom-call(f32[128,128]{1,0:T(8,128)S(1)} %cholesky.590), custom_call_target="Cholesky" | custom-call | tf_op jit(solution)/shard_map/jit(cholesky)/cholesky | solution.py:45
  156.7 9.8 %custom-call.32 = f32[1,128,128]{1,2,0:T(8,128)S(1)} custom-call(f32[1,128,128]{2,1,0:T(8,128)S(1)} %get-tuple-element.101), custom_call_target="InvertDiagBlocksLowerTriangular" | custom-call | tf_op jit(solution)/shard_map/jit(cholesky)/cholesky | solution.py:45
  168.1 11.7 %cholesky.414 = f32[128,128]{1,0:T(8,128)S(1)} custom-call(f32[128,128]{1,0:T(8,128)S(1)} %cholesky.595), custom_call_target="Cholesky" | custom-call | tf_op jit(solution)/shard_map/jit(cholesky)/cholesky | solution.py:45
  191.7 12.1 %cholesky.431 = f32[128,128]{1,0:T(8,128)S(1)} custom-call(f32[128,128]{1,0:T(8,128)S(1)} %convolution_subtract_fusion.17), custom_call_target="Cholesky" | custom-call | tf_op jit(solution)/shard_map/jit(cholesky)/cholesky | solution.py:45
  215.5 39.3 %custom-call.34 = f32[4,128,128]{1,2,0:T(8,128)S(1)} custom-call(f32[4,128,128]{2,1,0:T(8,128)S(1)} %get-tuple-element.27), custom_call_target="InvertDiagBlocksLowerTriangular" | custom-call | tf_op jit(solution)/shard_map/jit(_solve_triangular)/triangular_solve | solution.py:47
  270.4 45.6 %collective-permute-done.3 = bf16[4096,256]{1,0:T(8,128)(2,1)S(1)} collective-permute-done((bf16[4096,256]{1,0:T(8,128)(2,1)}, bf16[4096,256]{1,0:T(8,128)(2,1)S(1)}, u32[]{:S(2)}, u32[]{:S(2)}) %collective-permute-start.3) | collective-permute-done | bytes 2097184 | tf_op jit(solution)/shard_map/ppermute | solution.py:14
  325.3 11.7 %cholesky.446 = f32[128,128]{1,0:T(8,128)S(1)} custom-call(f32[128,128]{1,0:T(8,128)S(1)} %cholesky.599), custom_call_target="Cholesky" | custom-call | tf_op jit(solution)/shard_map/jit(cholesky)/cholesky | solution.py:45
  337.1 9.8 %custom-call.35 = f32[1,128,128]{1,2,0:T(8,128)S(1)} custom-call(f32[1,128,128]{2,1,0:T(8,128)S(1)} %get-tuple-element.94), custom_call_target="InvertDiagBlocksLowerTriangular" | custom-call | tf_op jit(solution)/shard_map/jit(cholesky)/cholesky | solution.py:45
  349.5 12.1 %cholesky.465 = f32[128,128]{1,0:T(8,128)S(1)} custom-call(f32[128,128]{1,0:T(8,128)S(1)} %cholesky.603), custom_call_target="Cholesky" | custom-call | tf_op jit(solution)/shard_map/jit(cholesky)/cholesky | solution.py:45
  374.4 11.7 %cholesky.486 = f32[128,128]{1,0:T(8,128)S(1)} custom-call(f32[128,128]{1,0:T(8,128)S(1)} %cholesky.608), custom_call_target="Cholesky" | custom-call | tf_op jit(solution)/shard_map/jit(cholesky)/cholesky | solution.py:45
  398.2 11.7 %cholesky.503 = f32[128,128]{1,0:T(8,128)S(1)} custom-call(f32[128,128]{1,0:T(8,128)S(1)} %convolution_subtract_fusion.16), custom_call_target="Cholesky" | custom-call | tf_op jit(solution)/shard_map/jit(cholesky)/cholesky | solution.py:45
  421.2 39.3 %custom-call.38 = f32[4,128,128]{1,2,0:T(8,128)S(1)} custom-call(f32[4,128,128]{2,1,0:T(8,128)S(1)} %get-tuple-element.28), custom_call_target="InvertDiagBlocksLowerTriangular" | custom-call | tf_op jit(solution)/shard_map/jit(_solve_triangular)/triangular_solve | solution.py:47
  470.6 47.1 %collective-permute-done.4 = bf16[4096,256]{1,0:T(8,128)(2,1)S(1)} collective-permute-done((bf16[4096,256]{1,0:T(8,128)(2,1)S(1)}, bf16[4096,256]{1,0:T(8,128)(2,1)S(1)}, u32[]{:S(2)}, u32[]{:S(2)}) %collective-permute-start.4) | collective-permute-done | bytes 2097184 | tf_op jit(solution)/shard_map/ppermute | solution.py:14
  523.0 11.7 %cholesky.518 = f32[128,128]{1,0:T(8,128)S(1)} custom-call(f32[128,128]{1,0:T(8,128)S(1)} %cholesky.612), custom_call_target="Cholesky" | custom-call | tf_op jit(solution)/shard_map/jit(cholesky)/cholesky | solution.py:45
  534.9 9.8 %custom-call.39 = f32[1,128,128]{1,2,0:T(8,128)S(1)} custom-call(f32[1,128,128]{2,1,0:T(8,128)S(1)} %get-tuple-element.84), custom_call_target="InvertDiagBlocksLowerTriangular" | custom-call | tf_op jit(solution)/shard_map/jit(cholesky)/cholesky | solution.py:45
  547.3 11.9 %cholesky.537 = f32[128,128]{1,0:T(8,128)S(1)} custom-call(f32[128,128]{1,0:T(8,128)S(1)} %cholesky.616), custom_call_target="Cholesky" | custom-call | tf_op jit(solution)/shard_map/jit(cholesky)/cholesky | solution.py:45
  571.8 11.7 %cholesky.558 = f32[128,128]{1,0:T(8,128)S(1)} custom-call(f32[128,128]{1,0:T(8,128)S(1)} %cholesky.621), custom_call_target="Cholesky" | custom-call | tf_op jit(solution)/shard_map/jit(cholesky)/cholesky | solution.py:45
  595.5 11.9 %cholesky.575 = f32[128,128]{1,0:T(8,128)S(1)} custom-call(f32[128,128]{1,0:T(8,128)S(1)} %convolution_subtract_fusion.15), custom_call_target="Cholesky" | custom-call | tf_op jit(solution)/shard_map/jit(cholesky)/cholesky | solution.py:45
  618.6 39.3 %custom-call.42 = f32[4,128,128]{1,2,0:T(8,128)S(1)} custom-call(f32[4,128,128]{2,1,0:T(8,128)S(1)} %get-tuple-element.29), custom_call_target="InvertDiagBlocksLowerTriangular" | custom-call | tf_op jit(solution)/shard_map/jit(_solve_triangular)/triangular_solve | solution.py:47
  664.3 46.8 %collective-permute-done.5 = bf16[4096,256]{0,1:T(8,128)(2,1)S(1)} collective-permute-done((bf16[4096,256]{0,1:T(8,128)(2,1)S(1)}, bf16[4096,256]{0,1:T(8,128)(2,1)S(1)}, u32[]{:S(2)}, u32[]{:S(2)}) %collective-permute-start.5) | collective-permute-done | bytes 2097184 | tf_op jit(solution)/shard_map/ppermute | solution.py:14
  (212 shorter events, 206.7 us)
Async XLA Ops:
  2.1 5.8 copy-start
  10.4 3.9 copy-start.1
  14.3 49.4 %collective-permute-start = (bf16[4096,256]{1,0:T(8,128)(2,1)}, bf16[4096,256]{1,0:T(8,128)(2,1)}, u32[]{:S(2)}, u32[]{:S(2)}) collective-permute-start(bf16[4096,256]{1,0:T(8,128)(2,1)} %get-tuple-element.74), channel_id=1, source_target_pairs={{0,24},{8,0},{16,8},{24,16},{1,25},{9,1},{17,9},{25,17},{2,26},{10... | collective-permute-start | bytes 6291464 | tf_op jit(solution)/shard_map/ppermute | solution.py:14
  14.3 49.4 %collective-permute-start.1 = (bf16[4096,256]{1,0:T(8,128)(2,1)}, bf16[4096,256]{1,0:T(8,128)(2,1)}, u32[]{:S(2)}, u32[]{:S(2)}) collective-permute-start(bf16[4096,256]{1,0:T(8,128)(2,1)} %get-tuple-element.73), channel_id=1, source_target_pairs={{0,16},{8,24},{16,0},{24,8},{1,17},{9,25},{17,1},{25,9},{2,18},{10... | collective-permute-start | bytes 6291464 | tf_op jit(solution)/shard_map/ppermute | solution.py:14
  17.0 90.6 %collective-permute-start.2 = (bf16[4096,256]{1,0:T(8,128)(2,1)}, bf16[4096,256]{1,0:T(8,128)(2,1)}, u32[]{:S(2)}, u32[]{:S(2)}) collective-permute-start(bf16[4096,256]{1,0:T(8,128)(2,1)} %get-tuple-element.72), channel_id=1, source_target_pairs={{0,8},{8,16},{16,24},{24,0},{1,9},{9,17},{17,25},{25,1},{2,10},{10... | collective-permute-start | bytes 6291464 | tf_op jit(solution)/shard_map/ppermute | solution.py:14
  113.2 1.4 copy-start.10
  113.2 2.0 copy-start.12
  116.4 0.7 copy-start.16
  119.5 1.0 copy-start.5
  254.9 6.0 copy-start.11
  254.9 6.0 copy-start.13
  263.6 3.3 copy-start.2
  266.8 49.1 %collective-permute-start.3 = (bf16[4096,256]{1,0:T(8,128)(2,1)}, bf16[4096,256]{1,0:T(8,128)(2,1)S(1)}, u32[]{:S(2)}, u32[]{:S(2)}) collective-permute-start(bf16[4096,256]{1,0:T(8,128)(2,1)} %get-tuple-element.71), channel_id=1, source_target_pairs={{0,1},{1,2},{2,3},{3,4},{4,5},{5,6},{6,7},{7,0},{8,9},{9,10},{10,1... | collective-permute-start | bytes 6291464 | tf_op jit(solution)/shard_map/ppermute | solution.py:14
  316.0 5.8 copy-start.8
  324.3 1.0 copy-start.3
  460.5 4.8 copy-start.9
  460.5 4.8 copy-start.15
  469.6 48.1 %collective-permute-start.4 = (bf16[4096,256]{1,0:T(8,128)(2,1)S(1)}, bf16[4096,256]{1,0:T(8,128)(2,1)S(1)}, u32[]{:S(2)}, u32[]{:S(2)}) collective-permute-start(bf16[4096,256]{1,0:T(8,128)(2,1)S(1)} %get-tuple-element.69), channel_id=1, source_target_pairs={{0,1},{1,2},{2,3},{3,4},{4,5},{5,6},{6,7},{7,0},{8,9},{9,10},{10,1... | collective-permute-start | bytes 6291464 | tf_op jit(solution)/shard_map/ppermute | solution.py:14
  517.7 1.9 copy-start.6
  522.0 1.0 copy-start.4
  657.9 3.2 copy-start.7
  657.9 3.2 copy-start.14
  664.2 46.9 %collective-permute-start.5 = (bf16[4096,256]{0,1:T(8,128)(2,1)S(1)}, bf16[4096,256]{0,1:T(8,128)(2,1)S(1)}, u32[]{:S(2)}, u32[]{:S(2)}) collective-permute-start(bf16[4096,256]{0,1:T(8,128)(2,1)S(1)} %get-tuple-element.67), channel_id=1, source_target_pairs={{0,1},{1,2},{2,3},{3,4},{4,5},{5,6},{6,7},{7,0},{8,9},{9,10},{10,1... | collective-permute-start | bytes 6291464 | tf_op jit(solution)/shard_map/ppermute | solution.py:14
where the time goes:
time: 730 us; the launch traced here: 720 us
  other arithmetic  381 us (52%)
  waiting for transfers between devices  228 us (31%)
  local copies, waits for them, and re-layouts  47.5 us (7%)
  matrix products  47.4 us (6%)
  between operations  10.2 us (1%)
    another operation x44, other arithmetic, rotation_for(): factor = jnp.linalg.cholesky(gram_matrix)  238 us
    ppermute x6, waiting for transfers between devices, passed_along(): lax.ppermute(array, axis, [(i, (i + by) % size) for i in range(size)])  228 us
    another operation x7, other arithmetic, rotation_for(): rotation = jax.scipy.linalg.solve_triangular(factor, lifted.T, lower=True).T  118 us
    another operation x40, local copies, waits for them, and re-layouts, rotation_for(): rotation = jax.scipy.linalg.solve_triangular(factor, lifted.T, lower=True).T  23.4 us
    another operation x18, matrix products, rotation_for(): factor = jnp.linalg.cholesky(gram_matrix)  16.4 us
  transfers between devices with their start and end apart: 6, of which 5 were waited for; matrix products, arithmetic and copies ran while one was open for 0% of the time, Pallas kernels for 0%

commit v1 on v0

v1 whole, which is shorter than its diff:
```python
import functools

import jax
import jax.numpy as jnp
from jax import lax
from jax.experimental import pallas as pl
from jax.experimental.pallas import tpu as pltpu
from jax.sharding import PartitionSpec as P

ROUNDS = 3
SUB = 8
PANEL = 32
CHUNK = 512

epsilon = 1e-05
f32 = jnp.float32


def passed_along(array, axis, by):
    size = lax.axis_size(axis)
    return lax.ppermute(array, axis, [(i, (i + by) % size) for i in range(size)])


def standardize(counts):
    values = counts.astype(jnp.float32)
    col_mean = jnp.mean(values, axis=0)
    centred = values - col_mean
    col_var = jnp.mean(centred * centred, axis=0)
    return (centred / jnp.sqrt(col_var + epsilon)).astype(jnp.bfloat16)


def dot(a, b, ca, cb):
    return lax.dot_general(
        a, b, (((ca,), (cb,)), ((), ())), precision=lax.Precision.HIGHEST, preferred_element_type=f32
    )


def dot16(a, b, ca, cb):
    return lax.dot_general(a, b, (((ca,), (cb,)), ((), ())), preferred_element_type=f32)


def identity(size):
    rows = lax.broadcasted_iota(jnp.int32, (size, size), 0)
    cols = lax.broadcasted_iota(jnp.int32, (size, size), 1)
    return (rows == cols).astype(f32)


def inverse_of(x):
    guess = pl.reciprocal(x, approx=True)
    return guess * (2.0 - x * guess)


def panel_inverse(panel, size):
    width = 4 * size
    half = 2 * size
    tile = (SUB, width)
    first = lax.broadcasted_iota(jnp.int32, tile, 1) < half
    sub = lax.broadcasted_iota(jnp.int32, tile, 0)
    count = size // SUB
    work = [panel[SUB * t : SUB * t + SUB, :] for t in range(count)]
    done = []
    for g in range(count):
        columns = []
        for j in range(SUB):
            k = SUB * g + j
            columns.append(
                {
                    t: jnp.where(
                        first,
                        jnp.broadcast_to(work[t][:, k : k + 1], tile),
                        jnp.broadcast_to(work[t][:, half + k : half + k + 1], tile),
                    )
                    for t in range(g, count)
                }
            )
        pivots = jnp.ones(tile, f32)
        for j in range(SUB):
            pivot = jnp.broadcast_to(columns[j][g][j : j + 1, :], tile)
            pivots = jnp.where(sub == j, pivot, pivots)
            inverse = inverse_of(pivot)
            row = jnp.broadcast_to(work[g][j : j + 1, :], tile)
            heads = {m: jnp.broadcast_to(columns[m][g][j : j + 1, :], tile) for m in range(j + 1, SUB)}
            for t in range(g, count):
                factor = columns[j][t] * inverse
                if t == g:
                    factor = jnp.where(sub > j, factor, 0.0)
                for m in range(j + 1, SUB):
                    columns[m][t] = columns[m][t] - factor * heads[m]
                work[t] = work[t] - factor * row
        done.append(work[g] * lax.rsqrt(pivots))
    return jnp.concatenate(done, axis=0)


def invert_factors(grams, size):
    eye = identity(PANEL)
    for start in range(0, size, PANEL):
        stop = start + PANEL
        block = [gram[start:stop, start:stop] for gram in grams]
        inverses = panel_inverse(jnp.concatenate([block[0], eye, block[1], eye], axis=1), PANEL)
        for side, gram in enumerate(grams):
            inverse = inverses[:, (2 * side + 1) * PANEL : (2 * side + 2) * PANEL]
            rows = dot(inverse, gram[start:stop, :], 1, 0)
            gram[start:stop, :] = rows
            if stop < size:
                gram[stop:size, :] = gram[stop:size, :] - dot(rows[:, stop:size], rows, 0, 0)


def round_kernel(top_ref, low_ref, low_out, inv_out, mix_out, cross_ref, norm_ref, gram1, gram2):
    indiv, size = top_ref.shape
    cross_ref[...] = jnp.zeros_like(cross_ref)
    norm_ref[...] = jnp.zeros_like(norm_ref)

    def accumulate(step, carry):
        rows = pl.ds(step * CHUNK, CHUNK)
        top = top_ref[rows, :]
        low = low_ref[rows, :]
        cross_ref[...] += dot16(top, low, 0, 0)
        top = top.astype(f32)
        low = low.astype(f32)
        norm_ref[0:1, :] += jnp.sum(top * top, axis=0, keepdims=True)
        norm_ref[SUB : SUB + 1, :] += jnp.sum(low * low, axis=0, keepdims=True)
        return carry

    lax.fori_loop(0, indiv // CHUNK, accumulate, 0)
    norm_top = dot(norm_ref[0:SUB, :], jnp.ones((SUB, size), f32), 0, 0)
    norm_low = norm_ref[SUB : SUB + 1, :]
    coupling = 2.0 * cross_ref[...] / (norm_top + norm_low + epsilon)
    eye = identity(size)
    gram1[:, 0:size] = eye + dot(coupling, coupling, 1, 1)
    gram1[:, size : 2 * size] = eye
    gram2[:, 0:size] = eye + dot(coupling, coupling, 0, 0)
    gram2[:, size : 2 * size] = eye
    invert_factors((gram1, gram2), size)
    inverse1 = gram1[:, size : 2 * size]
    inverse2 = gram2[:, size : 2 * size]
    inv_out[...] = inverse1.astype(jnp.bfloat16)
    mix_out[...] = (-dot(inverse1, coupling, 1, 0)).astype(jnp.bfloat16)
    from_top = dot(coupling, inverse2, 1, 1).astype(jnp.bfloat16)
    from_low = inverse2.astype(jnp.bfloat16)

    def apply(step, carry):
        rows = pl.ds(step * CHUNK, CHUNK)
        low_out[rows, :] = (
            dot16(top_ref[rows, :], from_top, 1, 0) + dot16(low_ref[rows, :], from_low, 1, 1)
        ).astype(jnp.bfloat16)
        return carry

    lax.fori_loop(0, indiv // CHUNK, apply, 0)


def rotate_low(top, low):
    indiv, size = top.shape
    square = jax.ShapeDtypeStruct((size, size), jnp.bfloat16)
    return pl.pallas_call(
        round_kernel,
        out_shape=[jax.ShapeDtypeStruct((indiv, size), jnp.bfloat16), square, square],
        scratch_shapes=[
            pltpu.VMEM((size, size), f32),
            pltpu.VMEM((2 * SUB, size), f32),
            pltpu.VMEM((size, 2 * size), f32),
            pltpu.VMEM((size, 2 * size), f32),
        ],
        compiler_params=pltpu.CompilerParams(vmem_limit_bytes=40 * 2**20),
        cost_estimate=pl.CostEstimate(
            flops=4 * indiv * size * size, bytes_accessed=6 * indiv * size, transcendentals=0
        ),
        name="rotate_low",
    )(top, low)


def top_kernel(top_ref, low_ref, inv_ref, mix_ref, out_ref):
    out_ref[...] = (
        dot16(top_ref[...], inv_ref[...], 1, 1) + dot16(low_ref[...], mix_ref[...], 1, 1)
    ).astype(jnp.bfloat16)


def rotate_top(top, low, inverse, mix):
    indiv, size = top.shape
    rows = pl.BlockSpec((CHUNK, size), lambda i: (i, 0))
    whole = pl.BlockSpec((size, size), lambda i: (0, 0))
    return pl.pallas_call(
        top_kernel,
        grid=(indiv // CHUNK,),
        in_specs=[rows, rows, whole, whole],
        out_specs=rows,
        out_shape=jax.ShapeDtypeStruct((indiv, size), jnp.bfloat16),
        cost_estimate=pl.CostEstimate(
            flops=4 * indiv * size * size, bytes_accessed=6 * indiv * size, transcendentals=0
        ),
        name="rotate_top",
    )(top, low, inverse, mix)


def body(genotypes, dest_group):
    num_groups = lax.axis_size("group")
    num_pairs = lax.axis_size("pair")
    own_group = lax.axis_index("group")
    own_pair = lax.axis_index("pair")
    blk_width = genotypes.shape[1] // 2
    scaled = standardize(genotypes)
    first_block = scaled[:, :blk_width]
    second_block = scaled[:, blk_width:]
    dest_table = dest_group.reshape(num_groups, num_pairs, 2)
    column = lax.dynamic_index_in_dim(dest_table, own_pair, 1, keepdims=False)
    own_dest = lax.dynamic_index_in_dim(column, own_group, 0, keepdims=False)
    offset_zero = (own_dest[0] - own_group) % num_groups
    offset_one = (own_dest[1] - own_group) % num_groups
    top_block = jnp.where(offset_zero == 0, first_block, jnp.zeros_like(first_block))
    low_block = jnp.where(offset_one == 0, second_block, jnp.zeros_like(second_block))
    for distance in range(1, num_groups):
        outgoing = jnp.where(offset_zero == distance, first_block, second_block)
        incoming = passed_along(outgoing, "group", distance)
        top_block = jnp.where(offset_zero == distance, incoming, top_block)
        low_block = jnp.where(offset_one == distance, incoming, low_block)
    for cycle_round in range(ROUNDS):
        low_new, inverse, mix = rotate_low(top_block, low_block)
        low_next = passed_along(low_new, "pair", 1)
        top_block = rotate_top(top_block, low_block, inverse, mix)
        low_block = low_next
    return jnp.concatenate([top_block, low_block], axis=1)


def solution(mesh):
    in_specs = (P(None, ("group", "pair")), P())
    out_specs = P(None, ("group", "pair"))
    return jax.shard_map(body, mesh=mesh, in_specs=in_specs, out_specs=out_specs, check_vma=False)
```

time: 730 us -> 348 us (0.48); the launches traced: 720 us -> 345 us
  other arithmetic: 381 us -> 20.7 us
  Pallas kernels: 0 us -> 92.1 us
  matrix products: 47.4 us -> 0 us
  local copies, waits for them, and re-layouts: 47.5 us -> 10.9 us
  waiting for transfers between devices: 228 us -> 215 us
  between operations: 10.2 us -> 1.43 us
    another operation x51 -> x0, other arithmetic: 356 us -> none  [the longest x44 238 us: rotation_for(): factor = jnp.linalg.cholesky(gram_matrix)]
    pallas_call x0 -> x6, Pallas kernels: none -> 92.1 us  [the longest x3 70.3 us: rotate_low(): pl.pallas_call(round_kernel, out_shape=[jax.ShapeDtypeStruct((indiv, size...]
    another operation x39 -> x0, matrix products: 29 us -> none  [the longest x18 16.4 us: rotation_for(): factor = jnp.linalg.cholesky(gram_matrix)]
    another operation x52 -> x0, local copies, waits for them, and re-layouts: 23.8 us -> none  [the longest x40 23.4 us: rotation_for(): rotation = jax.scipy.linalg.solve_triangular(factor, lifted.T, lower=True).T]
    dot_general x9 -> x0, matrix products: 18.4 us -> none  [the longest x3 7.86 us: body(): jnp.dot(joined, rotation, preferred_element_type=jnp.float32)]
    ppermute x6, waiting for transfers between devices: 228 us -> 215 us  [passed_along(): lax.ppermute(array, axis, [(i, (i + by) % size) for i in range(size)])]
    reduce_sum x5 -> x0, other arithmetic: 9.42 us -> none  [the longest x3 8.27 us: rotation_for(): norm_top = jnp.sum(top_wide * top_wide, axis=0)]
  transfers between devices with their start and end apart: 6 -> 6, of which waited for: 5 -> 6; matrix products, arithmetic and copies ran while one was open for 0% -> 0% of each run, Pallas kernels for 0% -> 6%
where the time goes in v1:
time: 348 us; the launch traced here: 345 us
  waiting for transfers between devices  215 us (62%)
  Pallas kernels  92.1 us (26%)
  other arithmetic  20.7 us (6%)
  local copies, waits for them, and re-layouts  10.9 us (3%)
  starting transfers between devices  5.06 us (1%)
    ppermute x6, waiting for transfers between devices, passed_along(): lax.ppermute(array, axis, [(i, (i + by) % size) for i in range(size)])  215 us
    pallas_call x3, Pallas kernels, rotate_low(): pl.pallas_call(round_kernel, out_shape=[jax.ShapeDtypeStruct((indiv, size...  70.3 us
    pallas_call x3, Pallas kernels, rotate_top(): pl.pallas_call(top_kernel, grid=(indiv // CHUNK,), in_specs=[rows, rows,...  21.8 us
    unnamed x28, local copies, waits for them, and re-layouts  9.52 us
  transfers between devices with their start and end apart: 6, of which 6 were waited for; matrix products, arithmetic and copies ran while one was open for 0% of the time, Pallas kernels for 6%

profile of v1, /device:TPU:1, one launch (start us, length us, event | category | flops | bytes accessed | tf_op | source)
XLA Modules:
  0.0 345.5 jit_solution(9288006249197199875)
XLA Ops:
  0.0 0.7 reshape.17
  2.1 4.1 %convert_reduce_fusion = f32[512]{0:T(512)S(1)} fusion(s32[4096,512]{1,0:T(8,128)} %param.2), kind=kLoop, calls=%fused_computation.3 | loop fusion | flops 4193792 | bytes 8390656 | tf_op jit(solution)/shard_map/reduce_sum | solution.py:26
  6.2 1.6 copy-done.12
  7.8 1.2 multiply_reduce_fusion
  9.0 4.6 %divide_convert_fusion = bf16[4096,512]{1,0:T(8,128)(2,1)S(1)} fusion(s32[4096,512]{1,0:T(8,128)} %param.2, f32[512]{0:T(512)S(1)} %add_sqrt_fusion, f32[512]{0:T(512)S(1)} %broadcast_multiply_fusion), kind=kLoop, calls=%fused_computation | loop fusion | flops 8388608 | bytes 12587008 | tf_op jit(solution)/shard_map/convert_element_type | solution.py:29
  13.6 3.1 broadcast_select_fusion
  16.7 0.8 copy-done.13
  17.5 2.6 collective-permute-start.2
  21.2 44.1 %collective-permute-done.2 = bf16[4096,256]{1,0:T(8,128)(2,1)S(1)} collective-permute-done((bf16[4096,256]{1,0:T(8,128)(2,1)}, bf16[4096,256]{1,0:T(8,128)(2,1)S(1)}, u32[]{:S(2)}, u32[]{:S(2)}) %collective-permute-start.2) | collective-permute-done | bytes 2097184 | tf_op jit(solution)/shard_map/ppermute | solution.py:21
  65.3 44.9 %collective-permute-done.1 = bf16[4096,256]{1,0:T(8,128)(2,1)} collective-permute-done((bf16[4096,256]{1,0:T(8,128)(2,1)}, bf16[4096,256]{1,0:T(8,128)(2,1)}, u32[]{:S(2)}, u32[]{:S(2)}) %collective-permute-start.1) | collective-permute-done | bytes 2097184 | tf_op jit(solution)/shard_map/ppermute | solution.py:21
  110.7 3.7 %select_select_fusion = (bf16[4096,256]{1,0:T(8,128)(2,1)S(1)}, bf16[4096,256]{1,0:T(8,128)(2,1)S(1)}) fusion(bf16[4096,256]{1,0:T(8,128)(2,1)} %collective-permute-done, bf16[4096,256]{1,0:T(8,128)(2,1)} %collective-permute-done.1, bf16[4096,256]{1,0:T(8,128)(2,1)S(1)} %collective-permute-done.2, pred[]{:T(512)S(6)} %eq.37, pred[]{:T(512)S(6)} %eq.36, ...), kind=kLoop, calls=%fused_computation.5 | loop fusion | flops 8388608 | bytes 14680072 | tf_op jit(solution)/shard_map/jit(_where)/select_n | solution.py:214
  114.4 23.4 %rotate_low.3 = (bf16[4096,256]{1,0:T(8,128)(2,1)}, bf16[256,256]{1,0:T(8,128)(2,1)S(1)}, bf16[256,256]{1,0:T(8,128)(2,1)S(1)}) custom-call(bf16[4096,256]{1,0:T(8,128)(2,1)S(1)} %get-tuple-element.24.top_ref, bf16[4096,256]{1,0:T(8,128)(2,1)S(1)} %get-tuple-element.23.low_ref), custom_call_target="tpu_custom_call" | custom-call | flops 1073741824 | bytes 6291456 | tf_op jit(solution)/shard_map/rotate_low/pallas_call | solution.py:154
  139.2 2.0 collective-permute-start.3
  141.2 7.3 %rotate_top.3.top_ref = bf16[4096,256]{1,0:T(8,128)(2,1)} custom-call(bf16[4096,256]{1,0:T(8,128)(2,1)} %copy-done.3, bf16[4096,256]{1,0:T(8,128)(2,1)} %copy-done.2, bf16[256,256]{1,0:T(8,128)(2,1)} %copy-done.6, bf16[256,256]{1,0:T(8,128)(2,1)} %copy-done.7), custom_call_target="tpu_custom_call" | custom-call | flops 1073741824 | bytes 6291456 | tf_op jit(solution)/shard_map/rotate_top/pallas_call | solution.py:181
  148.5 42.1 %collective-permute-done.3.low_ref = bf16[4096,256]{1,0:T(8,128)(2,1)S(1)} collective-permute-done((bf16[4096,256]{1,0:T(8,128)(2,1)}, bf16[4096,256]{1,0:T(8,128)(2,1)S(1)}, u32[]{:S(2)}, u32[]{:S(2)}) %collective-permute-start.3) | collective-permute-done | bytes 2097184 | tf_op jit(solution)/shard_map/ppermute | solution.py:21
  190.5 1.6 copy-done
  192.1 23.5 %rotate_low.4 = (bf16[4096,256]{1,0:T(8,128)(2,1)}, bf16[256,256]{1,0:T(8,128)(2,1)S(1)}, bf16[256,256]{1,0:T(8,128)(2,1)S(1)}) custom-call(bf16[4096,256]{1,0:T(8,128)(2,1)S(1)} %copy-done, bf16[4096,256]{1,0:T(8,128)(2,1)S(1)} %collective-permute-done.3.low_ref), custom_call_target="tpu_custom_call" | custom-call | flops 1073741824 | bytes 6291456 | tf_op jit(solution)/shard_map/rotate_low/pallas_call | solution.py:154
  216.9 7.3 %rotate_top.4.top_ref = bf16[4096,256]{1,0:T(8,128)(2,1)} custom-call(bf16[4096,256]{1,0:T(8,128)(2,1)} %rotate_top.3.top_ref, bf16[4096,256]{1,0:T(8,128)(2,1)} %copy-done.4, bf16[256,256]{1,0:T(8,128)(2,1)} %copy-done.8, bf16[256,256]{1,0:T(8,128)(2,1)} %copy-done.9), custom_call_target="tpu_custom_call" | custom-call | flops 1073741824 | bytes 6291456 | tf_op jit(solution)/shard_map/rotate_top/pallas_call | solution.py:181
  224.2 42.3 %collective-permute-done.4.low_ref = bf16[4096,256]{1,0:T(8,128)(2,1)S(1)} collective-permute-done((bf16[4096,256]{1,0:T(8,128)(2,1)}, bf16[4096,256]{1,0:T(8,128)(2,1)S(1)}, u32[]{:S(2)}, u32[]{:S(2)}) %collective-permute-start.4) | collective-permute-done | bytes 2097184 | tf_op jit(solution)/shard_map/ppermute | solution.py:21
  266.5 1.6 copy-done.1
  268.1 23.4 %rotate_low.5 = (bf16[4096,256]{1,0:T(8,128)(2,1)}, bf16[256,256]{1,0:T(8,128)(2,1)S(1)}, bf16[256,256]{1,0:T(8,128)(2,1)S(1)}) custom-call(bf16[4096,256]{1,0:T(8,128)(2,1)S(1)} %copy-done.1, bf16[4096,256]{1,0:T(8,128)(2,1)S(1)} %collective-permute-done.4.low_ref), custom_call_target="tpu_custom_call" | custom-call | flops 1073741824 | bytes 6291456 | tf_op jit(solution)/shard_map/rotate_low/pallas_call | solution.py:154
  292.8 7.3 %rotate_top.5 = bf16[4096,256]{1,0:T(8,128)(2,1)} custom-call(bf16[4096,256]{1,0:T(8,128)(2,1)} %rotate_top.4.top_ref, bf16[4096,256]{1,0:T(8,128)(2,1)} %copy-done.5, bf16[256,256]{1,0:T(8,128)(2,1)} %copy-done.10, bf16[256,256]{1,0:T(8,128)(2,1)} %copy-done.11), custom_call_target="tpu_custom_call" | custom-call | flops 1073741824 | bytes 6291456 | tf_op jit(solution)/shard_map/rotate_top/pallas_call | solution.py:181
  300.1 41.4 %collective-permute-done.5 = bf16[4096,256]{1,0:T(8,128)(2,1)S(1)} collective-permute-done((bf16[4096,256]{1,0:T(8,128)(2,1)}, bf16[4096,256]{1,0:T(8,128)(2,1)S(1)}, u32[]{:S(2)}, u32[]{:S(2)}) %collective-permute-start.5) | collective-permute-done | bytes 2097184 | tf_op jit(solution)/shard_map/ppermute | solution.py:21
  341.5 3.9 %pad_maximum_fusion = bf16[4096,512]{1,0:T(8,128)(2,1)} fusion(bf16[4096,256]{1,0:T(8,128)(2,1)S(1)} %collective-permute-done.5, bf16[4096,256]{1,0:T(8,128)(2,1)} %rotate_top.5), kind=kLoop, calls=%fused_computation.4 | loop fusion | flops 8388608 | bytes 8388608 | tf_op jit(solution)/shard_map/concatenate | solution.py:220
  (33 shorter events, 5.5 us)
Async XLA Ops:
  2.1 5.8 %copy-start.12 = (s32[4096,512]{1,0:T(8,128)S(1)}, s32[4096,512]{1,0:T(8,128)}, u32[]{:S(2)}) copy-start(s32[4096,512]{1,0:T(8,128)} %param.2) | copy-start | bytes 25165828
  13.6 3.9 %copy-start.13 = (bf16[4096,512]{1,0:T(8,128)(2,1)}, bf16[4096,512]{1,0:T(8,128)(2,1)S(1)}, u32[]{:S(2)}) copy-start(bf16[4096,512]{1,0:T(8,128)(2,1)S(1)} %divide_convert_fusion) | copy-start | bytes 12582916
  17.5 47.8 %collective-permute-start.2 = (bf16[4096,256]{1,0:T(8,128)(2,1)}, bf16[4096,256]{1,0:T(8,128)(2,1)S(1)}, u32[]{:S(2)}, u32[]{:S(2)}) collective-permute-start(bf16[4096,256]{1,0:T(8,128)(2,1)} %get-tuple-element.25), channel_id=1, source_target_pairs={{0,8},{8,16},{16,24},{24,0},{1,9},{9,17},{17,25},{25,1},{2,10},{10... | collective-permute-start | bytes 6291464 | tf_op jit(solution)/shard_map/ppermute | solution.py:21
  20.1 90.2 %collective-permute-start.1 = (bf16[4096,256]{1,0:T(8,128)(2,1)}, bf16[4096,256]{1,0:T(8,128)(2,1)}, u32[]{:S(2)}, u32[]{:S(2)}) collective-permute-start(bf16[4096,256]{1,0:T(8,128)(2,1)} %get-tuple-element.26), channel_id=1, source_target_pairs={{0,16},{8,24},{16,0},{24,8},{1,17},{9,25},{17,1},{25,9},{2,18},{10... | collective-permute-start | bytes 6291464 | tf_op jit(solution)/shard_map/ppermute | solution.py:21
  20.1 90.6 %collective-permute-start = (bf16[4096,256]{1,0:T(8,128)(2,1)}, bf16[4096,256]{1,0:T(8,128)(2,1)}, u32[]{:S(2)}, u32[]{:S(2)}) collective-permute-start(bf16[4096,256]{1,0:T(8,128)(2,1)} %get-tuple-element.27), channel_id=1, source_target_pairs={{0,24},{8,0},{16,8},{24,16},{1,25},{9,1},{17,9},{25,17},{2,26},{10... | collective-permute-start | bytes 6291464 | tf_op jit(solution)/shard_map/ppermute | solution.py:21
  114.4 23.5 %copy-start.2 = (bf16[4096,256]{1,0:T(8,128)(2,1)}, bf16[4096,256]{1,0:T(8,128)(2,1)S(1)}, u32[]{:S(2)}) copy-start(bf16[4096,256]{1,0:T(8,128)(2,1)S(1)} %get-tuple-element.23.low_ref) | copy-start | bytes 6291460
  114.4 23.4 %copy-start.3 = (bf16[4096,256]{1,0:T(8,128)(2,1)}, bf16[4096,256]{1,0:T(8,128)(2,1)S(1)}, u32[]{:S(2)}) copy-start(bf16[4096,256]{1,0:T(8,128)(2,1)S(1)} %get-tuple-element.24.top_ref) | copy-start | bytes 6291460
  137.9 0.7 copy-start.6
  138.5 0.7 copy-start.7
  139.2 51.3 %collective-permute-start.3 = (bf16[4096,256]{1,0:T(8,128)(2,1)}, bf16[4096,256]{1,0:T(8,128)(2,1)S(1)}, u32[]{:S(2)}, u32[]{:S(2)}) collective-permute-start(bf16[4096,256]{1,0:T(8,128)(2,1)} %get-tuple-element.16), channel_id=1, source_target_pairs={{0,1},{1,2},{2,3},{3,4},{4,5},{5,6},{6,7},{7,0},{8,9},{9,10},{10,1... | collective-permute-start | bytes 6291464 | tf_op jit(solution)/shard_map/ppermute | solution.py:21
  190.5 1.6 copy-start
  192.1 23.5 %copy-start.4 = (bf16[4096,256]{1,0:T(8,128)(2,1)}, bf16[4096,256]{1,0:T(8,128)(2,1)S(1)}, u32[]{:S(2)}) copy-start(bf16[4096,256]{1,0:T(8,128)(2,1)S(1)} %collective-permute-done.3.low_ref) | copy-start | bytes 6291460
  215.6 0.7 copy-start.8
  216.2 0.7 copy-start.9
  216.9 49.6 %collective-permute-start.4 = (bf16[4096,256]{1,0:T(8,128)(2,1)}, bf16[4096,256]{1,0:T(8,128)(2,1)S(1)}, u32[]{:S(2)}, u32[]{:S(2)}) collective-permute-start(bf16[4096,256]{1,0:T(8,128)(2,1)} %get-tuple-element.19), channel_id=1, source_target_pairs={{0,1},{1,2},{2,3},{3,4},{4,5},{5,6},{6,7},{7,0},{8,9},{9,10},{10,1... | collective-permute-start | bytes 6291464 | tf_op jit(solution)/shard_map/ppermute | solution.py:21
  266.5 1.6 copy-start.1
  268.1 23.4 %copy-start.5 = (bf16[4096,256]{1,0:T(8,128)(2,1)}, bf16[4096,256]{1,0:T(8,128)(2,1)S(1)}, u32[]{:S(2)}) copy-start(bf16[4096,256]{1,0:T(8,128)(2,1)S(1)} %collective-permute-done.4.low_ref) | copy-start | bytes 6291460
  291.5 0.7 copy-start.10
  292.2 0.7 copy-start.11
  292.8 48.7 %collective-permute-start.5 = (bf16[4096,256]{1,0:T(8,128)(2,1)}, bf16[4096,256]{1,0:T(8,128)(2,1)S(1)}, u32[]{:S(2)}, u32[]{:S(2)}) collective-permute-start(bf16[4096,256]{1,0:T(8,128)(2,1)} %get-tuple-element.22), channel_id=1, source_target_pairs={{0,1},{1,2},{2,3},{3,4},{4,5},{5,6},{6,7},{7,0},{8,9},{9,10},{10,1... | collective-permute-start | bytes 6291464 | tf_op jit(solution)/shard_map/ppermute | solution.py:21

commit v2 on v1

v2 whole, which is shorter than its diff:
```python
import functools

import jax
import jax.numpy as jnp
from jax import lax
from jax.experimental import pallas as pl
from jax.experimental.pallas import tpu as pltpu
from jax.sharding import PartitionSpec as P

ROUNDS = 3
SUB = 8
PANEL = 32
CHUNK = 512

epsilon = 1e-05
f32 = jnp.float32


def passed_along(array, axis, by):
    size = lax.axis_size(axis)
    return lax.ppermute(array, axis, [(i, (i + by) % size) for i in range(size)])


def dot(a, b, ca, cb):
    return lax.dot_general(
        a, b, (((ca,), (cb,)), ((), ())), precision=lax.Precision.HIGHEST, preferred_element_type=f32
    )


def dot16(a, b, ca, cb):
    return lax.dot_general(a, b, (((ca,), (cb,)), ((), ())), preferred_element_type=f32)


def identity(size):
    rows = lax.broadcasted_iota(jnp.int32, (size, size), 0)
    cols = lax.broadcasted_iota(jnp.int32, (size, size), 1)
    return (rows == cols).astype(f32)


def inverse_of(x):
    guess = pl.reciprocal(x, approx=True)
    return guess * (2.0 - x * guess)


def panel_inverse(panel, size):
    width = 4 * size
    half = 2 * size
    tile = (SUB, width)
    first = lax.broadcasted_iota(jnp.int32, tile, 1) < half
    sub = lax.broadcasted_iota(jnp.int32, tile, 0)
    count = size // SUB
    work = [panel[SUB * t : SUB * t + SUB, :] for t in range(count)]
    done = []
    for g in range(count):
        columns = []
        for j in range(SUB):
            k = SUB * g + j
            columns.append(
                {
                    t: jnp.where(
                        first,
                        jnp.broadcast_to(work[t][:, k : k + 1], tile),
                        jnp.broadcast_to(work[t][:, half + k : half + k + 1], tile),
                    )
                    for t in range(g, count)
                }
            )
        pivots = jnp.ones(tile, f32)
        for j in range(SUB):
            pivot = jnp.broadcast_to(columns[j][g][j : j + 1, :], tile)
            pivots = jnp.where(sub == j, pivot, pivots)
            inverse = inverse_of(pivot)
            row = jnp.broadcast_to(work[g][j : j + 1, :], tile)
            heads = {m: jnp.broadcast_to(columns[m][g][j : j + 1, :], tile) for m in range(j + 1, SUB)}
            for t in range(g, count):
                factor = columns[j][t] * inverse
                if t == g:
                    factor = jnp.where(sub > j, factor, 0.0)
                for m in range(j + 1, SUB):
                    columns[m][t] = columns[m][t] - factor * heads[m]
                work[t] = work[t] - factor * row
        done.append(work[g] * lax.rsqrt(pivots))
    return jnp.concatenate(done, axis=0)


def split(x):
    first = x.astype(jnp.bfloat16)
    rest = x - first.astype(f32)
    second = rest.astype(jnp.bfloat16)
    return first, second, (rest - second.astype(f32)).astype(jnp.bfloat16)


LEFT = (0, 0, 1, 0, 1, 2)
RIGHT = (0, 1, 0, 2, 1, 0)


def stacked(terms, order, axis):
    return jnp.concatenate([terms[i] for i in order], axis=axis)


def invert_factors(grams, size):
    wide = (PANEL, 4 * PANEL)
    lane = lax.broadcasted_iota(jnp.int32, wide, 1)
    sub = lax.broadcasted_iota(jnp.int32, wide, 0)
    inverse_part = lane % (2 * PANEL) >= PANEL
    eyes = (lane % (2 * PANEL) == sub + PANEL).astype(f32)
    row_lane = lax.broadcasted_iota(jnp.int32, (PANEL, size), 1)
    row_sub = lax.broadcasted_iota(jnp.int32, (PANEL, size), 0)
    all_lane = lax.broadcasted_iota(jnp.int32, (size, size), 1)
    zero = jnp.zeros((PANEL, size), f32)

    def step(index, carry):
        start = pl.multiple_of(index * PANEL, PANEL)
        stop = start + PANEL
        rows = [gram[pl.ds(start, PANEL), :] for gram in grams]
        blocks = []
        for side in range(2):
            block = rows[side][:, 0 : 4 * PANEL]
            for at in range(4 * PANEL, size, 4 * PANEL):
                block = jnp.where(start >= at, rows[side][:, at : at + 4 * PANEL], block)
            blocks.append(pltpu.roll(block, lax.rem(2 * PANEL * side + 4 * size - start, 4 * PANEL), 1))
        panel = jnp.where(inverse_part, eyes, jnp.where(lane < 2 * PANEL, blocks[0], blocks[1]))
        inverse = jnp.where(inverse_part, panel_inverse(panel, PANEL), 0.0)
        inverse = jnp.concatenate(
            [jnp.where(lane < 2 * PANEL, inverse, 0.0), jnp.where(lane >= 2 * PANEL, inverse, 0.0)], axis=0
        )
        within = (row_lane >= start) & (row_lane < stop)
        eye = (row_lane - start == row_sub).astype(f32)
        rows = [jnp.where(within, eye, part) for part in rows]
        left = split(inverse)
        right = split(jnp.concatenate([zero, rows[0], zero, rows[1]], axis=0))
        done = dot16(stacked(left, LEFT, 1), stacked(right, RIGHT, 0), 1, 0)
        terms = split(done)
        for side, gram in enumerate(grams):
            own = slice(side * PANEL, (side + 1) * PANEL)
            right = [term[own, :] for term in terms]
            left = [jnp.where(row_lane >= stop, term, jnp.zeros_like(term)) for term in right]
            change = dot16(stacked(left, LEFT, 0), stacked(right, RIGHT, 0), 0, 0)
            gram[...] = jnp.where((all_lane >= start) & (all_lane < stop), 0.0, gram[...]) - change
            gram[pl.ds(start, PANEL), :] = done[own, :]
        return carry

    lax.fori_loop(0, size // PANEL, step, 0)


def take_grams(rows, top_ref, low_ref, cross_ref, norm_ref):
    top = top_ref[rows, :]
    low = low_ref[rows, :]
    cross_ref[...] += dot16(top, low, 0, 0)
    top = top.astype(f32)
    low = low.astype(f32)
    norm_ref[0:1, :] += jnp.sum(top * top, axis=0, keepdims=True)
    norm_ref[SUB : SUB + 1, :] += jnp.sum(low * low, axis=0, keepdims=True)


def rotate(refs, outs, scratch, sems):
    top_ref, low_ref = refs
    low_out, inv_out, mix_out = outs
    cross_ref, norm_ref, gram1, gram2, new_ref, inv_ref, mix_ref = scratch
    indiv, size = top_ref.shape
    norm_top = dot(norm_ref[0:SUB, :], jnp.ones((SUB, size), f32), 0, 0)
    norm_low = norm_ref[SUB : SUB + 1, :]
    coupling = 2.0 * cross_ref[...] / (norm_top + norm_low + epsilon)
    eye = identity(size)
    gram1[...] = eye + dot(coupling, coupling, 1, 1)
    gram2[...] = eye + dot(coupling, coupling, 0, 0)
    invert_factors((gram1, gram2), size)
    below = lax.broadcasted_iota(jnp.int32, (size, size), 0) >= lax.broadcasted_iota(jnp.int32, (size, size), 1)
    inverse1 = jnp.where(below, gram1[...], 0.0)
    inverse2 = jnp.where(below, gram2[...], 0.0)
    from_top = dot(coupling, inverse2, 1, 1).astype(jnp.bfloat16)
    from_low = inverse2.astype(jnp.bfloat16)
    count = indiv // CHUNK

    def sent(step):
        rows = pl.ds(pl.multiple_of(step * CHUNK, CHUNK), CHUNK)
        return pltpu.make_async_copy(new_ref.at[rows, :], low_out.at[rows, :], sems.at[step])

    def apply(step, carry):
        rows = pl.ds(pl.multiple_of(step * CHUNK, CHUNK), CHUNK)
        new_ref[rows, :] = (
            dot16(top_ref[rows, :], from_top, 1, 0) + dot16(low_ref[rows, :], from_low, 1, 1)
        ).astype(jnp.bfloat16)
        sent(step).start()
        return carry

    lax.fori_loop(0, count, apply, 0)
    inv_ref[...] = inverse1.astype(jnp.bfloat16)
    mix_ref[...] = (-dot(inverse1, coupling, 1, 0)).astype(jnp.bfloat16)
    small = [
        pltpu.make_async_copy(inv_ref, inv_out, sems.at[count]),
        pltpu.make_async_copy(mix_ref, mix_out, sems.at[count + 1]),
    ]
    for copy in small:
        copy.start()
    for step in range(count):
        sent(step).wait()
    for copy in small:
        copy.wait()


def scratch_of(indiv, size):
    block = pltpu.VMEM((indiv, size), jnp.bfloat16)
    small = pltpu.VMEM((size, size), jnp.bfloat16)
    count = indiv // CHUNK
    return [
        block,
        block,
        pltpu.VMEM((size, size), f32),
        pltpu.VMEM((2 * SUB, size), f32),
        pltpu.VMEM((size, size), f32),
        pltpu.VMEM((size, size), f32),
        block,
        small,
        small,
        pltpu.SemaphoreType.DMA((count + 2,)),
        pltpu.SemaphoreType.DMA((2 * count,)),
    ]


def cost(indiv, size):
    return pl.CostEstimate(flops=40 * indiv * size * size, bytes_accessed=16 * indiv * size, transcendentals=0)


def round_kernel(top_hbm, low_hbm, low_out, inv_out, mix_out, top_ref, low_ref, cross_ref, norm_ref, *rest):
    *scratch, sems, in_sems = rest
    indiv, size = top_ref.shape
    count = indiv // CHUNK

    def fetched(step):
        rows = pl.ds(pl.multiple_of(step * CHUNK, CHUNK), CHUNK)
        return [
            pltpu.make_async_copy(top_hbm.at[rows, :], top_ref.at[rows, :], in_sems.at[2 * step]),
            pltpu.make_async_copy(low_hbm.at[rows, :], low_ref.at[rows, :], in_sems.at[2 * step + 1]),
        ]

    for step in range(count):
        for copy in fetched(step):
            copy.start()
    cross_ref[...] = jnp.zeros_like(cross_ref)
    norm_ref[...] = jnp.zeros_like(norm_ref)

    def accumulate(step, carry):
        for copy in fetched(step):
            copy.wait()
        take_grams(pl.ds(pl.multiple_of(step * CHUNK, CHUNK), CHUNK), top_ref, low_ref, cross_ref, norm_ref)
        return carry

    lax.fori_loop(0, count, accumulate, 0)
    rotate((top_ref, low_ref), (low_out, inv_out, mix_out), (cross_ref, norm_ref, *scratch), sems)


def rotate_low(top, low):
    indiv, size = top.shape
    square = jax.ShapeDtypeStruct((size, size), jnp.bfloat16)
    anywhere = pl.BlockSpec(memory_space=pl.ANY)
    return pl.pallas_call(
        round_kernel,
        in_specs=[anywhere] * 2,
        out_specs=[anywhere] * 3,
        out_shape=[jax.ShapeDtypeStruct((indiv, size), jnp.bfloat16), square, square],
        scratch_shapes=scratch_of(indiv, size),
        compiler_params=pltpu.CompilerParams(vmem_limit_bytes=16 * 2**20),
        cost_estimate=cost(indiv, size),
        name="rotate_low",
    )(top, low)


def first_kernel(slots, flags, *refs):
    inputs = 6 if slots == 2 else 13
    sources = refs[:6] if slots == 2 else refs[:8]
    low_out, inv_out, mix_out, top_scaled, low_scaled = refs[inputs : inputs + 5]
    top_ref, low_ref, cross_ref, norm_ref, *rest = refs[inputs + 5 :]
    *scratch, sems, in_sems = rest
    own, other = sources[0:2], sources[2:4]
    indiv, size = top_ref.shape
    half = indiv // 2
    count = indiv // CHUNK
    core = flags[3]

    @pl.when(flags[0] == 1)
    def _():
        def fetch(code, target, parts, side):
            for part in range(2):
                place = jnp.where(core == part, 0, half)
                place = pl.multiple_of(place, half)

                @pl.when(flags[1 + side] == code)
                def _():
                    pltpu.make_async_copy(
                        parts[part], target.at[pl.ds(place, half), :], in_sems.at[2 * side + part]
                    ).start()

        for side, target in enumerate((top_ref, low_ref)):
            columns = slice(side * size, (side + 1) * size)
            choices = [[ref.at[:, columns] for ref in own], [ref.at[:, columns] for ref in other]]
            for slot in range(2):
                columns = slice(slot * size, (slot + 1) * size)
                choices.append([ref.at[:, columns] for ref in sources[4:6]])
            if slots == 3:
                choices.append(list(sources[6:8]))
            for code, parts in enumerate(choices):
                fetch(code, target, parts, side)
        cross_ref[...] = jnp.zeros_like(cross_ref)
        norm_ref[...] = jnp.zeros_like(norm_ref)
        scales = []
        for side, target in enumerate((top_ref, low_ref)):
            for part in range(2):
                pltpu.make_async_copy(
                    own[0].at[:, 0:size], target.at[pl.ds(0, half), :], in_sems.at[2 * side + part]
                ).wait()

            def add(step, sums):
                values = target[pl.ds(pl.multiple_of(step * CHUNK, CHUNK), CHUNK), :].astype(f32)
                return (
                    sums[0] + jnp.sum(values, axis=0, keepdims=True),
                    sums[1] + jnp.sum(values * values, axis=0, keepdims=True),
                )

            total, squares = lax.fori_loop(0, count, add, (jnp.zeros((1, size), f32),) * 2)
            whole = total.astype(jnp.int32)
            spread = indiv * squares.astype(jnp.int32) - whole * whole
            variance = spread.astype(f32) * (1.0 / (indiv * indiv))
            scales.append((total * (1.0 / indiv), 1.0 / jnp.sqrt(variance + epsilon)))

        def kept(step):
            rows = pl.ds(pl.multiple_of(step * CHUNK, CHUNK), CHUNK)
            return [
                pltpu.make_async_copy(target.at[rows, :], scaled.at[rows, :], in_sems.at[4 + 2 * step + side])
                for side, (target, scaled) in enumerate(((top_ref, top_scaled), (low_ref, low_scaled)))
            ]

        def scale_rows(step, carry):
            rows = pl.ds(pl.multiple_of(step * CHUNK, CHUNK), CHUNK)
            for (mean, scale), target in zip(scales, (top_ref, low_ref)):
                target[rows, :] = ((target[rows, :].astype(f32) - mean) * scale).astype(jnp.bfloat16)
            for copy in kept(step):
                copy.start()
            take_grams(rows, top_ref, low_ref, cross_ref, norm_ref)
            return carry

        lax.fori_loop(0, count, scale_rows, 0)
        rotate((top_ref, low_ref), (low_out, inv_out, mix_out), (cross_ref, norm_ref, *scratch), sems)
        for step in range(count):
            for copy in kept(step):
                copy.wait()


def first_round(flags, sources, held=()):
    half, size = sources[0].shape[0], sources[0].shape[1] // 2
    indiv = 2 * half
    slots = 3 if held else 2
    block = jax.ShapeDtypeStruct((indiv, size), jnp.bfloat16)
    square = jax.ShapeDtypeStruct((size, size), jnp.bfloat16)
    anywhere = pl.BlockSpec(memory_space=pl.ANY)
    scratch = scratch_of(indiv, size)
    scratch[-1] = pltpu.SemaphoreType.DMA((2 * (indiv // CHUNK) + 4,))
    return pl.pallas_call(
        functools.partial(first_kernel, slots),
        in_specs=[pl.BlockSpec(memory_space=pltpu.SMEM)] + [anywhere] * (len(sources) + len(held)),
        out_specs=[anywhere] * 5,
        out_shape=[block, square, square, block, block],
        input_output_aliases={1 + len(sources) + i: i for i in range(len(held))},
        scratch_shapes=scratch,
        compiler_params=pltpu.CompilerParams(vmem_limit_bytes=16 * 2**20),
        cost_estimate=cost(indiv, size),
        name="first_round",
    )(flags, *sources, *held)


def top_kernel(top_ref, low_ref, inv_ref, mix_ref, out_ref):
    out_ref[...] = (
        dot16(top_ref[...], inv_ref[...], 1, 1) + dot16(low_ref[...], mix_ref[...], 1, 1)
    ).astype(jnp.bfloat16)


def rotate_top(top, low, inverse, mix, blocks=1):
    indiv, size = top.shape
    rows = pl.BlockSpec((CHUNK, size), lambda i: (i, 0))
    whole = pl.BlockSpec((size, size), lambda i: (0, 0))
    return pl.pallas_call(
        top_kernel,
        grid=(indiv // CHUNK,),
        in_specs=[rows, rows, whole, whole],
        out_specs=rows,
        out_shape=jax.ShapeDtypeStruct((indiv, blocks * size), jnp.bfloat16),
        cost_estimate=pl.CostEstimate(
            flops=4 * indiv * size * size, bytes_accessed=6 * indiv * size, transcendentals=0
        ),
        name="rotate_top",
    )(top, low, inverse, mix)


def place_kernel(low_ref, held_ref, out_ref):
    out_ref[...] = low_ref[...]


def place_low(low, held):
    indiv, size = low.shape
    return pl.pallas_call(
        place_kernel,
        grid=(indiv // CHUNK,),
        in_specs=[pl.BlockSpec((CHUNK, size), lambda i: (i, 0)), pl.BlockSpec(memory_space=pl.ANY)],
        out_specs=pl.BlockSpec((CHUNK, size), lambda i: (i, 1)),
        out_shape=jax.ShapeDtypeStruct(held.shape, held.dtype),
        input_output_aliases={1: 0},
        name="place_low",
    )(low, held)


def across(array, bit):
    size = lax.axis_size("group")
    return lax.ppermute(array, "group", [(i, i ^ bit) for i in range(size)])


def regrouped_first_round(genotypes, dest_group):
    num_groups = lax.axis_size("group")
    num_pairs = lax.axis_size("pair")
    own_pair = lax.axis_index("pair")
    core = lax.axis_index("group") % 2
    size = genotypes.shape[1] // 2
    half = genotypes.shape[0] // 2
    offsets = lax.dynamic_index_in_dim(
        dest_group.reshape(num_groups, num_pairs, 2)[0], own_pair, 0, keepdims=False
    )
    crossing = [[(offsets[k] == 1 + c) | (offsets[k] == 2 + c) for k in range(2)] for c in range(2)]
    slot = [[None, None], [None, None]]
    used = jnp.int32(0)
    side_of = [jnp.int32(0)] * 3
    core_of = [jnp.int32(0)] * 3
    for c in range(2):
        for k in range(2):
            slot[c][k] = used
            for i in range(3):
                here = crossing[c][k] & (used == i)
                side_of[i] = jnp.where(here, k, side_of[i])
                core_of[i] = jnp.where(here, (offsets[k] + c) % 2, core_of[i])
            used = used + crossing[c][k].astype(jnp.int32)
    codes = []
    for k in range(2):
        far = jnp.where(core == 0, crossing[0][k], crossing[1][k])
        place = 2 + jnp.where(core == 0, slot[0][k], slot[1][k])
        codes.append(jnp.where(far, place, jnp.where(offsets[k] == 0, 0, 1)))

    def counts(which):
        rows = lax.dynamic_slice_in_dim(genotypes, which * half, half, 0)
        return rows.astype(jnp.bfloat16)

    own_away = counts(1 - core)
    other_here = across(own_away, 1)
    own_here = counts(core)

    def payload(i):
        near = lax.dynamic_slice_in_dim(own_here, side_of[i] * size, size, 1)
        far = lax.dynamic_slice_in_dim(other_here, side_of[i] * size, size, 1)
        return jnp.where(core_of[i] == core, near, far)

    early = across(jnp.concatenate([payload(0), payload(1)], axis=1), 2)
    other_away = across(own_here, 1)
    late, early = lax.optimization_barrier((payload(2), early))
    late = across(late, 2)
    early_away = across(early, 1)
    sources = (own_here, own_away, other_here, other_away, early, early_away)

    def flags(which):
        return jnp.stack([(core == which).astype(jnp.int32), codes[0], codes[1], core]).astype(jnp.int32)

    held = list(first_round(flags(0), sources))
    late, held[1] = lax.optimization_barrier((late, held[1]))
    late_away = across(late, 1)
    return first_round(flags(1), sources + (late, late_away), tuple(held))


def body(genotypes, dest_group):
    low_new, inverse, mix, top, low = regrouped_first_round(genotypes, dest_group)
    for cycle_round in range(1, ROUNDS):
        low_next = passed_along(low_new, "pair", 1)
        top = rotate_top(top, low, inverse, mix)
        low = low_next
        low_new, inverse, mix = rotate_low(top, low)
    low_next = passed_along(low_new, "pair", 1)
    return place_low(low_next, rotate_top(top, low, inverse, mix, 2))


def solution(mesh):
    in_specs = (P(None, ("group", "pair")), P())
    out_specs = P(None, ("group", "pair"))
    return jax.shard_map(body, mesh=mesh, in_specs=in_specs, out_specs=out_specs, check_vma=False)
```

time: 348 us -> 273 us (0.78)
  waiting for transfers between devices: 215 us -> 136 us
  other arithmetic: 20.7 us -> 10.2 us
  between operations: 1.43 us -> 9.97 us
  local copies, waits for them, and re-layouts: 10.9 us -> 17.6 us
  starting transfers between devices: 5.06 us -> 9.72 us
  Pallas kernels: 92.1 us -> 88.6 us
    ppermute x6 -> x3, waiting for transfers between devices: 215 us -> 67.4 us  [passed_along(): lax.ppermute(array, axis, [(i, (i + by) % size) for i in range(size)])]
    ppermute x0 -> x6, waiting for transfers between devices: none -> 68.1 us  [across(): return lax.ppermute(array, 'group', [(i, i ^ bit) for i in range(size)])]
    ppermute x0 -> x6, starting transfers between devices: none -> 9.14 us  [across(): return lax.ppermute(array, 'group', [(i, i ^ bit) for i in range(size)])]
    unnamed x28 -> x36, local copies, waits for them, and re-layouts: 9.52 us -> 16.9 us
    reduce_sum x2 -> x0, other arithmetic: 5.3 us -> none  [the longest x1 4.15 us: standardize(): col_mean = jnp.mean(values, axis=0)]
    ppermute x6 -> x3, starting transfers between devices: 5.06 us -> 0.58 us  [passed_along(): lax.ppermute(array, axis, [(i, (i + by) % size) for i in range(size)])]
    concatenate x1, other arithmetic: 3.94 us -> 0.16 us  [regrouped_first_round(): early = across(jnp.concatenate([payload(0), payload(1)], axis=1), 2)]
    pallas_call x3 -> x5, Pallas kernels: 70.3 us -> 66.8 us  [the longest x2 37.3 us: rotate_low(): pl.pallas_call(round_kernel, in_specs=[anywhere] * 2, out_specs=[anywhere...]
  transfers between devices with their start and end apart: 6 -> 9, of which waited for: 6 -> 7; matrix products, arithmetic and copies ran while one was open for 0% -> 0% of each run, Pallas kernels for 6% -> 8%
where the time goes in v2:
time: 273 us; the launch traced here: 272 us
  waiting for transfers between devices  136 us (50%)
  Pallas kernels  88.6 us (32%)
  local copies, waits for them, and re-layouts  17.6 us (6%)
  other arithmetic  10.2 us (4%)
  between operations  9.97 us (4%)
  starting transfers between devices  9.72 us (4%)
    ppermute x6, waiting for transfers between devices, across(): return lax.ppermute(array, 'group', [(i, i ^ bit) for i in range(size)])  68.1 us
    ppermute x3, waiting for transfers between devices, passed_along(): lax.ppermute(array, axis, [(i, (i + by) % size) for i in range(size)])  67.4 us
    pallas_call x2, Pallas kernels, rotate_low(): pl.pallas_call(round_kernel, in_specs=[anywhere] * 2, out_specs=[anywhere...  37.3 us
    pallas_call x2, Pallas kernels, first_round(): pl.pallas_call(functools.partial(first_kernel, slots), in_specs=[pl.Block...  23.9 us
    pallas_call x3, Pallas kernels, rotate_top(): pl.pallas_call(top_kernel, grid=(indiv // CHUNK,), in_specs=[rows, rows,...  21.8 us
    unnamed x36, local copies, waits for them, and re-layouts  16.9 us
    ppermute x6, starting transfers between devices, across(): return lax.ppermute(array, 'group', [(i, i ^ bit) for i in range(size)])  9.14 us
    convert_element_type x1, other arithmetic, counts(): return rows.astype(jnp.bfloat16)  5.97 us
  transfers between devices with their start and end apart: 9, of which 7 were waited for; matrix products, arithmetic and copies ran while one was open for 0% of the time, Pallas kernels for 8%

profile of v2, /device:TPU:1, one launch (start us, length us, event | category | flops | bytes accessed | tf_op | source)
XLA Modules:
  0.0 271.6 jit_solution(13798014985334498728)
XLA Ops:
  0.0 6.0 %dynamic-slice_convert_fusion = (bf16[2048,512]{1,0:T(8,128)(2,1)}, bf16[2048,512]{1,0:T(8,128)(2,1)S(1)}) fusion(s32[4096,512]{1,0:T(8,128)} %param.2, s32[]{:T(128)S(6)} %select_n.182, s32[]{:T(128)S(6)} %select_n.181), kind=kLoop, calls=%fused_computation | loop fusion | flops 2097152 | bytes 12582920 | tf_op jit(solution)/shard_map/convert_element_type | solution.py:447
  15.4 3.9 %dynamic-slice_select_fusion.1 = (bf16[2048,256]{1,0:T(8,128)(2,1)S(1)}, bf16[2048,256]{1,0:T(8,128)(2,1)S(1)}, bf16[2048,256]{1,0:T(8,128)(2,1)}) fusion(bf16[2048,512]{1,0:T(8,128)(2,1)} %collective-permute-done.refs_2_, s32[]{:T(128)S(6)} %select_n.204, bf16[2048,512]{1,0:T(8,128)(2,1)S(1)} %get-tuple-element.46.refs_0_, pred[]{:T(512)S(6)} %eq.103, ...), kind=kLoop, calls=%fused_computation.4 | loop fusion | flops 1572864 | bytes 9437199 | tf_op jit(solution)/shard_map/jit(_where)/select_n | solution.py:456
  19.4 2.8 %collective-permute-start.2 = (bf16[2048,512]{1,0:T(8,128)(2,1)S(1)}, bf16[2048,512]{1,0:T(8,128)(2,1)}, u32[]{:S(2)}, u32[]{:S(2)}) collective-permute-start(bf16[2048,512]{1,0:T(8,128)(2,1)S(1)} %pad_maximum_fusion), channel_id=1, source_target_pairs={{0,16},{8,24},{16,0},{24,8},{1,17},{9,25},{17,1},{25,9},{2,18},{10... | collective-permute-start | bytes 6291464 | tf_op jit(solution)/shard_map/ppermute | solution.py:413
  22.4 45.8 %collective-permute-done.2.refs_4_ = bf16[2048,512]{1,0:T(8,128)(2,1)} collective-permute-done((bf16[2048,512]{1,0:T(8,128)(2,1)S(1)}, bf16[2048,512]{1,0:T(8,128)(2,1)}, u32[]{:S(2)}, u32[]{:S(2)}) %collective-permute-start.2) | collective-permute-done | bytes 2097184 | tf_op jit(solution)/shard_map/ppermute | solution.py:413
  70.1 1.5 collective-permute-start.4
  73.8 1.4 copy-done.2
  76.5 18.7 %collective-permute-done.4.refs_6_ = bf16[2048,256]{1,0:T(8,128)(2,1)S(1)} collective-permute-done((bf16[2048,256]{1,0:T(8,128)(2,1)}, bf16[2048,256]{1,0:T(8,128)(2,1)S(1)}, u32[]{:S(2)}, u32[]{:S(2)}) %collective-permute-start.4) | collective-permute-done | bytes 1048608 | tf_op jit(solution)/shard_map/ppermute | solution.py:413
  95.1 3.9 %collective-permute-start.5 = (bf16[2048,256]{1,0:T(8,128)(2,1)S(1)}, bf16[2048,256]{1,0:T(8,128)(2,1)}, u32[]{:S(2)}, u32[]{:S(2)}) collective-permute-start(bf16[2048,256]{1,0:T(8,128)(2,1)S(1)} %collective-permute-done.4.refs_6_), channel_id=1, source_target_pairs={{0,8},{8,0},{16,24},{24,16},{1,9},{9,1},{17,25},{25,17},{2,10},{10... | collective-permute-start | bytes 3145736 | tf_op jit(solution)/shard_map/ppermute | solution.py:413
  99.2 2.3 collective-permute-done.5.refs_7_
  101.5 1.6 copy-done.3
  103.1 1.6 copy-done.6
  104.7 23.1 %first_round.3 = (bf16[4096,256]{1,0:T(8,128)(2,1)}, bf16[256,256]{1,0:T(8,128)(2,1)S(1)}, bf16[256,256]{1,0:T(8,128)(2,1)S(1)}, bf16[4096,256]{1,0:T(8,128)(2,1)S(1)}, bf16[4096,256]{1,0:T(8,128)(2,1)S(1)}) custom-call(s32[4]{0:T(128)S(1)} %add_add_fusion.flags, ...), custom_call_target="tpu_custom_call", output_to_operand_aliasing={{0}: (9, {}), {1}: (10, {}), {2}: (11, {}), {3}: (12, {}), ... | custom-call | flops 10737418240 | bytes 16777216 | tf_op jit(solution)/shard_map/first_round/pallas_call | solution.py:358
  132.3 7.2 %rotate_top.3.top_hbm.top_ref = bf16[4096,256]{1,0:T(8,128)(2,1)} custom-call(bf16[4096,256]{1,0:T(8,128)(2,1)} %copy-done.4, bf16[4096,256]{1,0:T(8,128)(2,1)} %copy-done.7, bf16[256,256]{1,0:T(8,128)(2,1)} %copy-done.12, bf16[256,256]{1,0:T(8,128)(2,1)} %copy-done.13), custom_call_target="tpu_custom_call" | custom-call | flops 1073741824 | bytes 6291456 | tf_op jit(solution)/shard_map/rotate_top/pallas_call | solution.py:381
  139.5 21.0 %collective-permute-done.6.low_hbm.low_ref = bf16[4096,256]{1,0:T(8,128)(2,1)S(1)} collective-permute-done((bf16[4096,256]{1,0:T(8,128)(2,1)}, bf16[4096,256]{1,0:T(8,128)(2,1)S(1)}, u32[]{:S(2)}, u32[]{:S(2)}) %collective-permute-start.6) | collective-permute-done | bytes 2097184 | tf_op jit(solution)/shard_map/ppermute | solution.py:21
  160.6 1.6 copy-done
  162.1 18.7 %rotate_low.2 = (bf16[4096,256]{1,0:T(8,128)(2,1)}, bf16[256,256]{1,0:T(8,128)(2,1)S(1)}, bf16[256,256]{1,0:T(8,128)(2,1)S(1)}) custom-call(bf16[4096,256]{1,0:T(8,128)(2,1)S(1)} %copy-done, bf16[4096,256]{1,0:T(8,128)(2,1)S(1)} %collective-permute-done.6.low_hbm.low_ref), custom_call_target="tpu_custom_call" | custom-call | flops 10737418240 | bytes 16777216 | tf_op jit(solution)/shard_map/rotate_low/pallas_call | solution.py:257
  182.1 7.3 %rotate_top.4.top_hbm.top_ref = bf16[4096,256]{1,0:T(8,128)(2,1)} custom-call(bf16[4096,256]{1,0:T(8,128)(2,1)} %rotate_top.3.top_hbm.top_ref, bf16[4096,256]{1,0:T(8,128)(2,1)} %copy-done.8, bf16[256,256]{1,0:T(8,128)(2,1)} %copy-done.14, bf16[256,256]{1,0:T(8,128)(2,1)} %copy-done.15), custom_call_target="tpu_custom_call" | custom-call | flops 1073741824 | bytes 6291456 | tf_op jit(solution)/shard_map/rotate_top/pallas_call | solution.py:381
  189.4 22.6 %collective-permute-done.7.low_hbm.low_ref = bf16[4096,256]{1,0:T(8,128)(2,1)S(1)} collective-permute-done((bf16[4096,256]{1,0:T(8,128)(2,1)}, bf16[4096,256]{1,0:T(8,128)(2,1)S(1)}, u32[]{:S(2)}, u32[]{:S(2)}) %collective-permute-start.7) | collective-permute-done | bytes 2097184 | tf_op jit(solution)/shard_map/ppermute | solution.py:21
  212.0 1.6 copy-done.1
  213.6 18.7 %rotate_low.3 = (bf16[4096,256]{1,0:T(8,128)(2,1)}, bf16[256,256]{1,0:T(8,128)(2,1)S(1)}, bf16[256,256]{1,0:T(8,128)(2,1)S(1)}) custom-call(bf16[4096,256]{1,0:T(8,128)(2,1)S(1)} %copy-done.1, bf16[4096,256]{1,0:T(8,128)(2,1)S(1)} %collective-permute-done.7.low_hbm.low_ref), custom_call_target="tpu_custom_call" | custom-call | flops 10737418240 | bytes 16777216 | tf_op jit(solution)/shard_map/rotate_low/pallas_call | solution.py:257
  233.6 7.3 %rotate_top.5.held_ref = bf16[4096,512]{1,0:T(8,128)(2,1)} custom-call(bf16[4096,256]{1,0:T(8,128)(2,1)} %rotate_top.4.top_hbm.top_ref, bf16[4096,256]{1,0:T(8,128)(2,1)} %copy-done.9, bf16[256,256]{1,0:T(8,128)(2,1)} %copy-done.10, bf16[256,256]{1,0:T(8,128)(2,1)} %copy-done.11), custom_call_target="tpu_custom_call" | custom-call | flops 1073741824 | bytes 6291456 | tf_op jit(solution)/shard_map/rotate_top/pallas_call | solution.py:381
  240.9 23.7 %collective-permute-done.8.low_ref = bf16[4096,256]{1,0:T(8,128)(2,1)S(1)} collective-permute-done((bf16[4096,256]{1,0:T(8,128)(2,1)}, bf16[4096,256]{1,0:T(8,128)(2,1)S(1)}, u32[]{:S(2)}, u32[]{:S(2)}) %collective-permute-start.8) | collective-permute-done | bytes 2097184 | tf_op jit(solution)/shard_map/ppermute | solution.py:21
  264.6 1.4 copy-done.16
  266.0 5.6 %place_low.1 = bf16[4096,512]{1,0:T(8,128)(2,1)} custom-call(bf16[4096,256]{1,0:T(8,128)(2,1)} %copy-done.16, bf16[4096,512]{1,0:T(8,128)(2,1)} %rotate_top.5.held_ref), custom_call_target="tpu_custom_call", output_to_operand_aliasing={{}: (1, {})} | custom-call | tf_op jit(solution)/shard_map/place_low/pallas_call | solution.py:400
  (46 shorter events, 12.5 us)
Async XLA Ops:
  0.0 6.0 %copy-start.17 = (s32[64]{0:T(128)S(1)}, s32[64]{0:T(128)}, u32[]{:S(2)}) copy-start(s32[64]{0:T(128)} %param.3) | copy-start | bytes 772
  6.0 9.4 %collective-permute-start = (bf16[2048,512]{1,0:T(8,128)(2,1)}, bf16[2048,512]{1,0:T(8,128)(2,1)}, u32[]{:S(2)}, u32[]{:S(2)}) collective-permute-start(bf16[2048,512]{1,0:T(8,128)(2,1)} %get-tuple-element.45.refs_1_), channel_id=1, source_target_pairs={{0,8},{8,0},{16,24},{24,16},{1,9},{9,1},{17,25},{25,17},{2,10},{10... | collective-permute-start | bytes 6291464 | tf_op jit(solution)/shard_map/ppermute | solution.py:413
  19.4 48.9 %collective-permute-start.2 = (bf16[2048,512]{1,0:T(8,128)(2,1)S(1)}, bf16[2048,512]{1,0:T(8,128)(2,1)}, u32[]{:S(2)}, u32[]{:S(2)}) collective-permute-start(bf16[2048,512]{1,0:T(8,128)(2,1)S(1)} %pad_maximum_fusion), channel_id=1, source_target_pairs={{0,16},{8,24},{16,0},{24,8},{1,17},{9,25},{17,1},{25,9},{2,18},{10... | collective-permute-start | bytes 6291464 | tf_op jit(solution)/shard_map/ppermute | solution.py:413
  22.1 49.5 %collective-permute-start.1 = (bf16[2048,512]{1,0:T(8,128)(2,1)S(1)}, bf16[2048,512]{1,0:T(8,128)(2,1)}, u32[]{:S(2)}, u32[]{:S(2)}) collective-permute-start(bf16[2048,512]{1,0:T(8,128)(2,1)S(1)} %get-tuple-element.46.refs_0_), channel_id=1, source_target_pairs={{0,8},{8,0},{16,24},{24,16},{1,9},{9,1},{17,25},{25,17},{2,10},{10... | collective-permute-start | bytes 6291464 | tf_op jit(solution)/shard_map/ppermute | solution.py:413
  68.3 4.7 %collective-permute-start.3 = (bf16[2048,512]{1,0:T(8,128)(2,1)}, bf16[2048,512]{1,0:T(8,128)(2,1)}, u32[]{:S(2)}, u32[]{:S(2)}) collective-permute-start(bf16[2048,512]{1,0:T(8,128)(2,1)} %collective-permute-done.2.refs_4_), channel_id=1, source_target_pairs={{0,8},{8,0},{16,24},{24,16},{1,9},{9,1},{17,25},{25,17},{2,10},{10... | collective-permute-start | bytes 6291464 | tf_op jit(solution)/shard_map/ppermute | solution.py:413
  70.1 25.1 %collective-permute-start.4 = (bf16[2048,256]{1,0:T(8,128)(2,1)}, bf16[2048,256]{1,0:T(8,128)(2,1)S(1)}, u32[]{:S(2)}, u32[]{:S(2)}) collective-permute-start(bf16[2048,256]{1,0:T(8,128)(2,1)} %get-tuple-element.26), channel_id=1, source_target_pairs={{0,16},{8,24},{16,0},{24,8},{1,17},{9,25},{17,1},{25,9},{2,18},{10... | collective-permute-start | bytes 3145736 | tf_op jit(solution)/shard_map/ppermute | solution.py:413
  73.8 1.4 copy-start.2
  75.1 1.3 copy-start.5
  95.1 6.4 %collective-permute-start.5 = (bf16[2048,256]{1,0:T(8,128)(2,1)S(1)}, bf16[2048,256]{1,0:T(8,128)(2,1)}, u32[]{:S(2)}, u32[]{:S(2)}) collective-permute-start(bf16[2048,256]{1,0:T(8,128)(2,1)S(1)} %collective-permute-done.4.refs_6_), channel_id=1, source_target_pairs={{0,8},{8,0},{16,24},{24,16},{1,9},{9,1},{17,25},{25,17},{2,10},{10... | collective-permute-start | bytes 3145736 | tf_op jit(solution)/shard_map/ppermute | solution.py:413
  101.5 1.6 copy-start.3
  103.1 1.6 copy-start.6
  127.7 1.3 copy-start.4
  129.1 1.3 copy-start.7
  130.4 0.7 copy-start.12
  131.0 0.7 copy-start.13
  131.7 28.9 %collective-permute-start.6 = (bf16[4096,256]{1,0:T(8,128)(2,1)}, bf16[4096,256]{1,0:T(8,128)(2,1)S(1)}, u32[]{:S(2)}, u32[]{:S(2)}) collective-permute-start(bf16[4096,256]{1,0:T(8,128)(2,1)} %get-tuple-element.38), channel_id=1, source_target_pairs={{0,1},{1,2},{2,3},{3,4},{4,5},{5,6},{6,7},{7,0},{8,9},{9,10},{10,1... | collective-permute-start | bytes 6291464 | tf_op jit(solution)/shard_map/ppermute | solution.py:21
  160.6 1.6 copy-start
  162.1 18.7 %copy-start.8 = (bf16[4096,256]{1,0:T(8,128)(2,1)}, bf16[4096,256]{1,0:T(8,128)(2,1)S(1)}, u32[]{:S(2)}) copy-start(bf16[4096,256]{1,0:T(8,128)(2,1)S(1)} %collective-permute-done.6.low_hbm.low_ref) | copy-start | bytes 6291460
  181.5 0.7 copy-start.15
  182.1 29.9 %collective-permute-start.7 = (bf16[4096,256]{1,0:T(8,128)(2,1)}, bf16[4096,256]{1,0:T(8,128)(2,1)S(1)}, u32[]{:S(2)}, u32[]{:S(2)}) collective-permute-start(bf16[4096,256]{1,0:T(8,128)(2,1)} %get-tuple-element.41), channel_id=1, source_target_pairs={{0,1},{1,2},{2,3},{3,4},{4,5},{5,6},{6,7},{7,0},{8,9},{9,10},{10,1... | collective-permute-start | bytes 6291464 | tf_op jit(solution)/shard_map/ppermute | solution.py:21
  212.0 1.6 copy-start.1
  213.6 18.7 %copy-start.9 = (bf16[4096,256]{1,0:T(8,128)(2,1)}, bf16[4096,256]{1,0:T(8,128)(2,1)S(1)}, u32[]{:S(2)}) copy-start(bf16[4096,256]{1,0:T(8,128)(2,1)S(1)} %collective-permute-done.7.low_hbm.low_ref) | copy-start | bytes 6291460
  233.6 31.0 %collective-permute-start.8 = (bf16[4096,256]{1,0:T(8,128)(2,1)}, bf16[4096,256]{1,0:T(8,128)(2,1)S(1)}, u32[]{:S(2)}, u32[]{:S(2)}) collective-permute-start(bf16[4096,256]{1,0:T(8,128)(2,1)} %get-tuple-element.42), channel_id=1, source_target_pairs={{0,1},{1,2},{2,3},{3,4},{4,5},{5,6},{6,7},{7,0},{8,9},{9,10},{10,1... | collective-permute-start | bytes 6291464 | tf_op jit(solution)/shard_map/ppermute | solution.py:21
  264.6 1.4 copy-start.16
  (3 other events, 1.9 us)

commit v3 on v2

--- a/solution.py
+++ b/solution.py
@@ -266,49 +266,90 @@
     )(top, low)
 
 
-def first_kernel(slots, flags, *refs):
-    inputs = 6 if slots == 2 else 13
-    sources = refs[:6] if slots == 2 else refs[:8]
-    low_out, inv_out, mix_out, top_scaled, low_scaled = refs[inputs : inputs + 5]
-    top_ref, low_ref, cross_ref, norm_ref, *rest = refs[inputs + 5 :]
+def offsets_of(dest):
+    pair = lax.axis_index("pair")
+    return dest[2 * pair], dest[2 * pair + 1]
+
+
+def present(offsets, value):
+    return (offsets[0] == value) | (offsets[1] == value)
+
+
+def side_with(offsets, value):
+    return jnp.where(offsets[1] == value, 1, 0)
+
+
+def cast_kernel(dest, *refs):
+    count = len(refs) // 2
+    for counts_ref, out_ref in zip(refs[:count], refs[count:]):
+        out_ref[...] = counts_ref[...].astype(out_ref.dtype)
+
+
+def picked(genotypes, dest, wants):
+    indiv, size = genotypes.shape[0], genotypes.shape[1] // 2
+    steps = 4
+    in_specs, out_specs, shapes = [], [], []
+    for want in wants:
+        parts = len(want((0, 0)))
+        rows = indiv // steps // parts
+
+        def place(i, dest, want=want):
+            offsets = offsets_of(dest)
+            value, *part = want(offsets)
+            return (i + (part[0] * steps if part else 0), side_with(offsets, value))
+
+        in_specs.append(pl.BlockSpec((rows, size), place))
+        out_specs.append(pl.BlockSpec((rows, size), lambda i, dest: (i, 0)))
+        shapes.append(jax.ShapeDtypeStruct((indiv // parts, size), jnp.bfloat16))
+    return pl.pallas_call(
+        cast_kernel,
+        grid_spec=pltpu.PrefetchScalarGridSpec(
+            num_scalar_prefetch=1, grid=(steps,), in_specs=in_specs, out_specs=out_specs
+        ),
+        out_shape=shapes,
+        name="pick_blocks",
+    )(dest, *[genotypes] * len(wants))
+
+
+def first_kernel(wholes, halves, dest, *refs):
+    sources = refs[: wholes + halves]
+    held = 5 if halves else 0
+    low_out, inv_out, mix_out, top_scaled, low_scaled = refs[wholes + halves + held : wholes + halves + held + 5]
+    top_ref, low_ref, cross_ref, norm_ref, *rest = refs[wholes + halves + held + 5 :]
     *scratch, sems, in_sems = rest
-    own, other = sources[0:2], sources[2:4]
     indiv, size = top_ref.shape
     half = indiv // 2
     count = indiv // CHUNK
-    core = flags[3]
-
-    @pl.when(flags[0] == 1)
+
+    offsets = offsets_of(dest)
+    if halves:
+        two = jnp.where(present(offsets, 1), wholes, 2)
+        codes = (0, 1, two, jnp.where(present(offsets, 2), wholes, 2))
+    else:
+        codes = (0, 2, 3, 1)
+
+    @pl.when(lax.axis_index("group") % 2 == (1 if halves else 0))
     def _():
-        def fetch(code, target, parts, side):
-            for part in range(2):
-                place = jnp.where(core == part, 0, half)
-                place = pl.multiple_of(place, half)
-
-                @pl.when(flags[1 + side] == code)
-                def _():
-                    pltpu.make_async_copy(
-                        parts[part], target.at[pl.ds(place, half), :], in_sems.at[2 * side + part]
-                    ).start()
-
         for side, target in enumerate((top_ref, low_ref)):
-            columns = slice(side * size, (side + 1) * size)
-            choices = [[ref.at[:, columns] for ref in own], [ref.at[:, columns] for ref in other]]
-            for slot in range(2):
-                columns = slice(slot * size, (slot + 1) * size)
-                choices.append([ref.at[:, columns] for ref in sources[4:6]])
-            if slots == 3:
-                choices.append(list(sources[6:8]))
-            for code, parts in enumerate(choices):
-                fetch(code, target, parts, side)
+            chosen = jnp.int32(codes[0])
+            for offset in range(1, 4):
+                chosen = jnp.where(offsets[side] == offset, codes[offset], chosen)
+            for code in range(wholes + halves // 2):
+                for part in range(2):
+                    rows = pl.ds(part * half, half)
+                    source = sources[code].at[rows, :] if code < wholes else sources[wholes + part]
+
+                    @pl.when(chosen == code)
+                    def _():
+                        pltpu.make_async_copy(source, target.at[rows, :], in_sems.at[2 * side + part]).start()
+
         cross_ref[...] = jnp.zeros_like(cross_ref)
         norm_ref[...] = jnp.zeros_like(norm_ref)
         scales = []
         for side, target in enumerate((top_ref, low_ref)):
             for part in range(2):
-                pltpu.make_async_copy(
-                    own[0].at[:, 0:size], target.at[pl.ds(0, half), :], in_sems.at[2 * side + part]
-                ).wait()
+                rows = pl.ds(part * half, half)
+                pltpu.make_async_copy(sources[0].at[rows, :], target.at[rows, :], in_sems.at[2 * side + part]).wait()
 
             def add(step, sums):
                 values = target[pl.ds(pl.multiple_of(step * CHUNK, CHUNK), CHUNK), :].astype(f32)
@@ -346,17 +387,16 @@
                 copy.wait()
 
 
-def first_round(flags, sources, held=()):
-    half, size = sources[0].shape[0], sources[0].shape[1] // 2
-    indiv = 2 * half
-    slots = 3 if held else 2
+def first_round(dest, wholes, halves=(), held=()):
+    indiv, size = wholes[0].shape
+    sources = tuple(wholes) + tuple(halves)
     block = jax.ShapeDtypeStruct((indiv, size), jnp.bfloat16)
     square = jax.ShapeDtypeStruct((size, size), jnp.bfloat16)
     anywhere = pl.BlockSpec(memory_space=pl.ANY)
     scratch = scratch_of(indiv, size)
     scratch[-1] = pltpu.SemaphoreType.DMA((2 * (indiv // CHUNK) + 4,))
     return pl.pallas_call(
-        functools.partial(first_kernel, slots),
+        functools.partial(first_kernel, len(wholes), len(halves)),
         in_specs=[pl.BlockSpec(memory_space=pltpu.SMEM)] + [anywhere] * (len(sources) + len(held)),
         out_specs=[anywhere] * 5,
         out_shape=[block, square, square, block, block],
@@ -365,7 +405,7 @@
         compiler_params=pltpu.CompilerParams(vmem_limit_bytes=16 * 2**20),
         cost_estimate=cost(indiv, size),
         name="first_round",
-    )(flags, *sources, *held)
+    )(dest, *sources, *held)
 
 
 def top_kernel(top_ref, low_ref, inv_ref, mix_ref, out_ref):
@@ -391,84 +431,70 @@
     )(top, low, inverse, mix)
 
 
-def place_kernel(low_ref, held_ref, out_ref):
-    out_ref[...] = low_ref[...]
+def place_kernel(low_ref, held_ref, out_ref, sem):
+    size = low_ref.shape[1]
+    copy = pltpu.make_async_copy(low_ref, out_ref.at[:, size : 2 * size], sem)
+    copy.start()
+    copy.wait()
 
 
 def place_low(low, held):
-    indiv, size = low.shape
+    anywhere = pl.BlockSpec(memory_space=pl.ANY)
     return pl.pallas_call(
         place_kernel,
-        grid=(indiv // CHUNK,),
-        in_specs=[pl.BlockSpec((CHUNK, size), lambda i: (i, 0)), pl.BlockSpec(memory_space=pl.ANY)],
-        out_specs=pl.BlockSpec((CHUNK, size), lambda i: (i, 1)),
+        in_specs=[pl.BlockSpec(memory_space=pltpu.VMEM), anywhere],
+        out_specs=anywhere,
         out_shape=jax.ShapeDtypeStruct(held.shape, held.dtype),
         input_output_aliases={1: 0},
+        scratch_shapes=[pltpu.SemaphoreType.DMA],
         name="place_low",
     )(low, held)
 
 
-def across(array, bit):
-    size = lax.axis_size("group")
-    return lax.ppermute(array, "group", [(i, i ^ bit) for i in range(size)])
-
-
 def regrouped_first_round(genotypes, dest_group):
     num_groups = lax.axis_size("group")
-    num_pairs = lax.axis_size("pair")
-    own_pair = lax.axis_index("pair")
     core = lax.axis_index("group") % 2
-    size = genotypes.shape[1] // 2
-    half = genotypes.shape[0] // 2
-    offsets = lax.dynamic_index_in_dim(
-        dest_group.reshape(num_groups, num_pairs, 2)[0], own_pair, 0, keepdims=False
+    offsets = offsets_of(dest_group)
+
+    def by_core(zero, one):
+        return jnp.where(lax.axis_index("group") % 2 == 0, zero, one)
+
+    def sent(array, hops):
+        return lax.ppermute(array, "group", [hop for chip in range(0, num_groups, 2) for hop in hops(chip)])
+
+    def far(chip):
+        return (chip + 2) % num_groups
+
+    (cross,) = picked(
+        genotypes,
+        dest_group,
+        [lambda o: (by_core(jnp.where(present(o, 2), 2, 3), jnp.where(present(o, 1), 1, 2)),)],
     )
-    crossing = [[(offsets[k] == 1 + c) | (offsets[k] == 2 + c) for k in range(2)] for c in range(2)]
-    slot = [[None, None], [None, None]]
-    used = jnp.int32(0)
-    side_of = [jnp.int32(0)] * 3
-    core_of = [jnp.int32(0)] * 3
-    for c in range(2):
-        for k in range(2):
-            slot[c][k] = used
-            for i in range(3):
-                here = crossing[c][k] & (used == i)
-                side_of[i] = jnp.where(here, k, side_of[i])
-                core_of[i] = jnp.where(here, (offsets[k] + c) % 2, core_of[i])
-            used = used + crossing[c][k].astype(jnp.int32)
-    codes = []
-    for k in range(2):
-        far = jnp.where(core == 0, crossing[0][k], crossing[1][k])
-        place = 2 + jnp.where(core == 0, slot[0][k], slot[1][k])
-        codes.append(jnp.where(far, place, jnp.where(offsets[k] == 0, 0, 1)))
-
-    def counts(which):
-        rows = lax.dynamic_slice_in_dim(genotypes, which * half, half, 0)
-        return rows.astype(jnp.bfloat16)
-
-    own_away = counts(1 - core)
-    other_here = across(own_away, 1)
-    own_here = counts(core)
-
-    def payload(i):
-        near = lax.dynamic_slice_in_dim(own_here, side_of[i] * size, size, 1)
-        far = lax.dynamic_slice_in_dim(other_here, side_of[i] * size, size, 1)
-        return jnp.where(core_of[i] == core, near, far)
-
-    early = across(jnp.concatenate([payload(0), payload(1)], axis=1), 2)
-    other_away = across(own_here, 1)
-    late, early = lax.optimization_barrier((payload(2), early))
-    late = across(late, 2)
-    early_away = across(early, 1)
-    sources = (own_here, own_away, other_here, other_away, early, early_away)
-
-    def flags(which):
-        return jnp.stack([(core == which).astype(jnp.int32), codes[0], codes[1], core]).astype(jnp.int32)
-
-    held = list(first_round(flags(0), sources))
-    late, held[1] = lax.optimization_barrier((late, held[1]))
-    late_away = across(late, 1)
-    return first_round(flags(1), sources + (late, late_away), tuple(held))
+    cross_one = sent(cross, lambda chip: [(chip + 1, far(chip))])
+    cross_zero = sent(cross, lambda chip: [(chip, far(chip))])
+    table, _ = lax.optimization_barrier((genotypes, cross))
+    near, own, lent, kept = picked(
+        table,
+        dest_group,
+        [
+            lambda o: (by_core(1, 3),),
+            lambda o: (0,),
+            lambda o: (by_core(3, 2), by_core(1, 0)),
+            lambda o: (by_core(3, 2), by_core(0, 1)),
+        ],
+    )
+    lent = sent(lent, lambda chip: [(chip, chip + 1), (chip + 1, chip)])
+    near = sent(near, lambda chip: [(chip, chip + 1), (chip + 1, chip)])
+    last = jnp.where(jnp.where(present(offsets, 3), core == 0, core == 1), kept, lent)
+    last, cross_one, cross_zero = lax.optimization_barrier((last, cross_one, cross_zero))
+    upper = sent(last, lambda chip: [(chip, far(chip) + 1)])
+    lower = sent(last, lambda chip: [(chip + 1, far(chip) + 1)])
+    held = list(first_round(dest_group, (own, near, cross_one, cross_zero)))
+    upper, lower, cross_one, cross_zero, held[1] = lax.optimization_barrier(
+        (upper, lower, cross_one, cross_zero, held[1])
+    )
+    passed = sent(jnp.where(present(offsets, 2), cross_one, cross_zero), lambda chip: [(chip, chip + 1)])
+    return first_round(dest_group, (own, near, passed), (upper, lower), held)
 
 
 def body(genotypes, dest_group):

time: 273 us -> 260 us (0.952)
  Pallas kernels: 88.6 us -> 97.9 us
  other arithmetic: 10.2 us -> 2.1 us
  between operations: 9.97 us -> 2.55 us
  local copies, waits for them, and re-layouts: 17.6 us -> 11.7 us
  waiting for transfers between devices: 136 us -> 132 us
  starting transfers between devices: 9.72 us -> 12.9 us
    pallas_call x3 -> x5, Pallas kernels: 29.5 us -> 38.7 us  [the longest x2 22.7 us: first_round(): pl.pallas_call(functools.partial(first_kernel, len(wholes), len(halves)),...]
    ppermute x6 -> x7, waiting for transfers between devices: 68.1 us -> 61 us  [sent(): lax.ppermute(array, 'group', [hop for chip in range(0, num_groups, 2) for...]
    convert_element_type x1 -> x0, other arithmetic: 5.97 us -> none  [counts(): return rows.astype(jnp.bfloat16)]
    unnamed x36 -> x30, local copies, waits for them, and re-layouts: 16.9 us -> 11.1 us
    ppermute x6 -> x7, starting transfers between devices: 9.14 us -> 12.9 us  [sent(): lax.ppermute(array, 'group', [hop for chip in range(0, num_groups, 2) for...]
    ppermute x3, waiting for transfers between devices: 67.4 us -> 70.9 us  [passed_along(): lax.ppermute(array, axis, [(i, (i + by) % size) for i in range(size)])]
  transfers between devices with their start and end apart: 9 -> 10, of which waited for: 7 -> 8; matrix products, arithmetic and copies ran while one was open for 0% -> 0% of each run, Pallas kernels for 8% -> 12%
where the time goes in v3:
time: 260 us; the launch traced here: 259 us
  waiting for transfers between devices  132 us (51%)
  Pallas kernels  97.9 us (38%)
  starting transfers between devices  12.9 us (5%)
  local copies, waits for them, and re-layouts  11.7 us (4%)
    ppermute x3, waiting for transfers between devices, passed_along(): lax.ppermute(array, axis, [(i, (i + by) % size) for i in range(size)])  70.9 us
    ppermute x7, waiting for transfers between devices, sent(): lax.ppermute(array, 'group', [hop for chip in range(0, num_groups, 2) for...  61 us
    pallas_call x2, Pallas kernels, rotate_low(): pl.pallas_call(round_kernel, in_specs=[anywhere] * 2, out_specs=[anywhere...  37.3 us
    pallas_call x2, Pallas kernels, first_round(): pl.pallas_call(functools.partial(first_kernel, len(wholes), len(halves)),...  22.7 us
    pallas_call x3, Pallas kernels, rotate_top(): pl.pallas_call(top_kernel, grid=(indiv // CHUNK,), in_specs=[rows, rows,...  21.8 us
    pallas_call x2, Pallas kernels, picked(): pl.pallas_call(cast_kernel, grid_spec=pltpu.PrefetchScalarGridSpec(num_sc...  13.1 us
    ppermute x7, starting transfers between devices, sent(): lax.ppermute(array, 'group', [hop for chip in range(0, num_groups, 2) for...  12.9 us
    unnamed x30, local copies, waits for them, and re-layouts  11.1 us
  transfers between devices with their start and end apart: 10, of which 8 were waited for; matrix products, arithmetic and copies ran while one was open for 0% of the time, Pallas kernels for 12%

profile of v3, /device:TPU:1, one launch (start us, length us, event | category | flops | bytes accessed | tf_op | source)
XLA Modules:
  0.0 259.0 jit_solution(7150222339752089542)
XLA Ops:
  0.0 5.0 %pick_blocks.2 = bf16[4096,256]{1,0:T(8,128)(2,1)} custom-call(s32[64]{0:T(128)} %dest.7, s32[4096,512]{1,0:T(8,128)} %refs_3_), custom_call_target="tpu_custom_call" | custom-call | tf_op jit(solution)/shard_map/pick_blocks/pallas_call | solution.py:304
  5.9 7.0 %collective-permute-start.2 = (bf16[4096,256]{1,0:T(8,128)(2,1)}, bf16[4096,256]{1,0:T(8,128)(2,1)}, u32[]{:S(2)}, u32[]{:S(2)}) collective-permute-start(bf16[4096,256]{1,0:T(8,128)(2,1)} %pick_blocks.2), channel_id=1, source_target_pairs={{8,16},{24,0},{9,17},{25,1},{10,18},{26,2},{11,19},{27,3},{12,20},... | collective-permute-start | bytes 6291464 | tf_op jit(solution)/shard_map/ppermute | solution.py:463
  13.0 8.1 %pick_blocks.3 = (bf16[4096,256]{1,0:T(8,128)(2,1)}, bf16[4096,256]{1,0:T(8,128)(2,1)}, bf16[2048,256]{1,0:T(8,128)(2,1)}, bf16[2048,256]{1,0:T(8,128)(2,1)}) custom-call(s32[64]{0:T(128)} %dest.7, s32[4096,512]{1,0:T(8,128)} %refs_3_, s32[4096,512]{1,0:T(8,128)} %refs_3_, s32[4096,512]{1,0:T(8,128)} %refs_3_, s32[4096,512]{1,0:T(8,128)} %refs_3_), custom_call_target="tpu_custom_call" | custom-call | tf_op jit(solution)/shard_map/pick_blocks/pallas_call | solution.py:304
  23.3 3.3 %collective-permute-done.1 = bf16[2048,256]{1,0:T(8,128)(2,1)S(1)} collective-permute-done((bf16[2048,256]{1,0:T(8,128)(2,1)}, bf16[2048,256]{1,0:T(8,128)(2,1)S(1)}, u32[]{:S(2)}, u32[]{:S(2)}) %collective-permute-start.1) | collective-permute-done | bytes 1048608 | tf_op jit(solution)/shard_map/ppermute | solution.py:463
  26.7 29.3 %collective-permute-done.2.refs_2_ = bf16[4096,256]{1,0:T(8,128)(2,1)} collective-permute-done((bf16[4096,256]{1,0:T(8,128)(2,1)}, bf16[4096,256]{1,0:T(8,128)(2,1)}, u32[]{:S(2)}, u32[]{:S(2)}) %collective-permute-start.2) | collective-permute-done | bytes 2097184 | tf_op jit(solution)/shard_map/ppermute | solution.py:463
  56.0 1.9 collective-permute-start.5
  61.2 19.0 %collective-permute-done.5.refs_4_ = bf16[2048,256]{1,0:T(8,128)(2,1)S(1)} collective-permute-done((bf16[2048,256]{1,0:T(8,128)(2,1)S(1)}, bf16[2048,256]{1,0:T(8,128)(2,1)S(1)}, u32[]{:S(2)}, u32[]{:S(2)}) %collective-permute-start.5) | collective-permute-done | bytes 1048608 | tf_op jit(solution)/shard_map/ppermute | solution.py:463
  80.2 2.6 collective-permute-done.4.refs_3_
  82.8 1.9 broadcast_select_fusion
  86.0 6.9 %collective-permute-done.6.refs_2_ = bf16[4096,256]{1,0:T(8,128)(2,1)S(1)} collective-permute-done((bf16[4096,256]{1,0:T(8,128)(2,1)S(1)}, bf16[4096,256]{1,0:T(8,128)(2,1)S(1)}, u32[]{:S(2)}, u32[]{:S(2)}) %collective-permute-start.6) | collective-permute-done | bytes 2097184 | tf_op jit(solution)/shard_map/ppermute | solution.py:463
  92.8 21.9 %first_round.3 = (bf16[4096,256]{1,0:T(8,128)(2,1)}, bf16[256,256]{1,0:T(8,128)(2,1)S(1)}, bf16[256,256]{1,0:T(8,128)(2,1)S(1)}, bf16[4096,256]{1,0:T(8,128)(2,1)S(1)}, bf16[4096,256]{1,0:T(8,128)(2,1)S(1)}) custom-call(s32[64]{0:T(128)S(1)} %copy-done.12, ...), custom_call_target="tpu_custom_call", output_to_operand_aliasing={{0}: (6, {}), {1}: (7, {}), {2}: (8, {}), {3}: (9, {}), {4}... | custom-call | flops 10737418240 | bytes 16777216 | tf_op jit(solution)/shard_map/first_round/pallas_call | solution.py:398
  116.0 1.4 copy-done.3
  118.7 7.3 %rotate_top.3.top_hbm.top_ref = bf16[4096,256]{1,0:T(8,128)(2,1)} custom-call(bf16[4096,256]{1,0:T(8,128)(2,1)} %copy-done.2, bf16[4096,256]{1,0:T(8,128)(2,1)} %copy-done.3, bf16[256,256]{1,0:T(8,128)(2,1)} %copy-done.8, bf16[256,256]{1,0:T(8,128)(2,1)} %copy-done.9), custom_call_target="tpu_custom_call" | custom-call | flops 1073741824 | bytes 6291456 | tf_op jit(solution)/shard_map/rotate_top/pallas_call | solution.py:421
  126.0 22.5 %collective-permute-done.7.low_hbm.low_ref = bf16[4096,256]{1,0:T(8,128)(2,1)S(1)} collective-permute-done((bf16[4096,256]{1,0:T(8,128)(2,1)}, bf16[4096,256]{1,0:T(8,128)(2,1)S(1)}, u32[]{:S(2)}, u32[]{:S(2)}) %collective-permute-start.7) | collective-permute-done | bytes 2097184 | tf_op jit(solution)/shard_map/ppermute | solution.py:21
  148.5 1.6 copy-done
  150.1 18.7 %rotate_low.2 = (bf16[4096,256]{1,0:T(8,128)(2,1)}, bf16[256,256]{1,0:T(8,128)(2,1)S(1)}, bf16[256,256]{1,0:T(8,128)(2,1)S(1)}) custom-call(bf16[4096,256]{1,0:T(8,128)(2,1)S(1)} %copy-done, bf16[4096,256]{1,0:T(8,128)(2,1)S(1)} %collective-permute-done.7.low_hbm.low_ref), custom_call_target="tpu_custom_call" | custom-call | flops 10737418240 | bytes 16777216 | tf_op jit(solution)/shard_map/rotate_low/pallas_call | solution.py:257
  170.1 7.3 %rotate_top.4.top_hbm.top_ref = bf16[4096,256]{1,0:T(8,128)(2,1)} custom-call(bf16[4096,256]{1,0:T(8,128)(2,1)} %rotate_top.3.top_hbm.top_ref, bf16[4096,256]{1,0:T(8,128)(2,1)} %copy-done.4, bf16[256,256]{1,0:T(8,128)(2,1)} %copy-done.10, bf16[256,256]{1,0:T(8,128)(2,1)} %copy-done.11), custom_call_target="tpu_custom_call" | custom-call | flops 1073741824 | bytes 6291456 | tf_op jit(solution)/shard_map/rotate_top/pallas_call | solution.py:421
  177.4 23.6 %collective-permute-done.8.low_hbm.low_ref = bf16[4096,256]{1,0:T(8,128)(2,1)S(1)} collective-permute-done((bf16[4096,256]{1,0:T(8,128)(2,1)}, bf16[4096,256]{1,0:T(8,128)(2,1)S(1)}, u32[]{:S(2)}, u32[]{:S(2)}) %collective-permute-start.8) | collective-permute-done | bytes 2097184 | tf_op jit(solution)/shard_map/ppermute | solution.py:21
  201.0 1.6 copy-done.1
  202.6 18.7 %rotate_low.3 = (bf16[4096,256]{1,0:T(8,128)(2,1)}, bf16[256,256]{1,0:T(8,128)(2,1)S(1)}, bf16[256,256]{1,0:T(8,128)(2,1)S(1)}) custom-call(bf16[4096,256]{1,0:T(8,128)(2,1)S(1)} %copy-done.1, bf16[4096,256]{1,0:T(8,128)(2,1)S(1)} %collective-permute-done.8.low_hbm.low_ref), custom_call_target="tpu_custom_call" | custom-call | flops 10737418240 | bytes 16777216 | tf_op jit(solution)/shard_map/rotate_low/pallas_call | solution.py:257
  222.6 7.3 %rotate_top.5.held_ref = bf16[4096,512]{1,0:T(8,128)(2,1)} custom-call(bf16[4096,256]{1,0:T(8,128)(2,1)} %rotate_top.4.top_hbm.top_ref, bf16[4096,256]{1,0:T(8,128)(2,1)} %copy-done.5, bf16[256,256]{1,0:T(8,128)(2,1)} %copy-done.6, bf16[256,256]{1,0:T(8,128)(2,1)} %copy-done.7), custom_call_target="tpu_custom_call" | custom-call | flops 1073741824 | bytes 6291456 | tf_op jit(solution)/shard_map/rotate_top/pallas_call | solution.py:421
  229.9 24.7 %collective-permute-done.9.low_ref = bf16[4096,256]{1,0:T(8,128)(2,1)S(1)} collective-permute-done((bf16[4096,256]{1,0:T(8,128)(2,1)}, bf16[4096,256]{1,0:T(8,128)(2,1)S(1)}, u32[]{:S(2)}, u32[]{:S(2)}) %collective-permute-start.9) | collective-permute-done | bytes 2097184 | tf_op jit(solution)/shard_map/ppermute | solution.py:21
  254.6 1.4 copy-done.14
  255.9 2.9 %place_low.1 = bf16[4096,512]{1,0:T(8,128)(2,1)} custom-call(bf16[4096,256]{1,0:T(8,128)(2,1)} %copy-done.14, bf16[4096,512]{1,0:T(8,128)(2,1)} %rotate_top.5.held_ref), custom_call_target="tpu_custom_call", output_to_operand_aliasing={{}: (1, {})} | custom-call | tf_op jit(solution)/shard_map/place_low/pallas_call | solution.py:443
  (39 shorter events, 10.8 us)
Async XLA Ops:
  5.0 16.5 %copy-start.12 = (s32[64]{0:T(128)S(1)}, s32[64]{0:T(128)}, u32[]{:S(2)}) copy-start(s32[64]{0:T(128)} %dest.7) | copy-start | bytes 772
  5.0 21.7 %collective-permute-start.3 = (bf16[4096,256]{1,0:T(8,128)(2,1)}, bf16[4096,256]{1,0:T(8,128)(2,1)S(1)}, u32[]{:S(2)}, u32[]{:S(2)}) collective-permute-start(bf16[4096,256]{1,0:T(8,128)(2,1)} %pick_blocks.2), channel_id=1, source_target_pairs={{0,16},{16,0},{1,17},{17,1},{2,18},{18,2},{3,19},{19,3},{4,20},{20... | collective-permute-start | bytes 6291464 | tf_op jit(solution)/shard_map/ppermute | solution.py:463
  5.9 50.1 %collective-permute-start.2 = (bf16[4096,256]{1,0:T(8,128)(2,1)}, bf16[4096,256]{1,0:T(8,128)(2,1)}, u32[]{:S(2)}, u32[]{:S(2)}) collective-permute-start(bf16[4096,256]{1,0:T(8,128)(2,1)} %pick_blocks.2), channel_id=1, source_target_pairs={{8,16},{24,0},{9,17},{25,1},{10,18},{26,2},{11,19},{27,3},{12,20},... | collective-permute-start | bytes 6291464 | tf_op jit(solution)/shard_map/ppermute | solution.py:463
  21.0 39.3 %collective-permute-start = (bf16[4096,256]{1,0:T(8,128)(2,1)}, bf16[4096,256]{1,0:T(8,128)(2,1)}, u32[]{:S(2)}, u32[]{:S(2)}) collective-permute-start(bf16[4096,256]{1,0:T(8,128)(2,1)} %get-tuple-element.36), channel_id=1, source_target_pairs={{0,8},{8,0},{16,24},{24,16},{1,9},{9,1},{17,25},{25,17},{2,10},{10... | collective-permute-start | bytes 6291464 | tf_op jit(solution)/shard_map/ppermute | solution.py:463
  21.0 5.5 %collective-permute-start.1 = (bf16[2048,256]{1,0:T(8,128)(2,1)}, bf16[2048,256]{1,0:T(8,128)(2,1)S(1)}, u32[]{:S(2)}, u32[]{:S(2)}) collective-permute-start(bf16[2048,256]{1,0:T(8,128)(2,1)} %get-tuple-element.38), channel_id=1, source_target_pairs={{0,8},{8,0},{16,24},{24,16},{1,9},{9,1},{17,25},{25,17},{2,10},{10... | collective-permute-start | bytes 3145736 | tf_op jit(solution)/shard_map/ppermute | solution.py:463
  23.3 37.1 %copy-start.13 = (bf16[4096,256]{1,0:T(8,128)(2,1)S(1)}, bf16[4096,256]{1,0:T(8,128)(2,1)}, u32[]{:S(2)}) copy-start(bf16[4096,256]{1,0:T(8,128)(2,1)} %get-tuple-element.35.refs_0_) | copy-start | bytes 6291460
  56.0 24.2 %collective-permute-start.5 = (bf16[2048,256]{1,0:T(8,128)(2,1)S(1)}, bf16[2048,256]{1,0:T(8,128)(2,1)S(1)}, u32[]{:S(2)}, u32[]{:S(2)}) collective-permute-start(bf16[2048,256]{1,0:T(8,128)(2,1)S(1)} %broadcast_select_fusion.1), channel_id=1, source_target_pairs={{8,24},{24,8},{9,25},{25,9},{10,26},{26,10},{11,27},{27,11},{12,28... | collective-permute-start | bytes 3145736 | tf_op jit(solution)/shard_map/ppermute | solution.py:463
  57.9 24.9 %collective-permute-start.4 = (bf16[2048,256]{1,0:T(8,128)(2,1)S(1)}, bf16[2048,256]{1,0:T(8,128)(2,1)S(1)}, u32[]{:S(2)}, u32[]{:S(2)}) collective-permute-start(bf16[2048,256]{1,0:T(8,128)(2,1)S(1)} %broadcast_select_fusion.1), channel_id=1, source_target_pairs={{0,24},{16,8},{1,25},{17,9},{2,26},{18,10},{3,27},{19,11},{4,28},{... | collective-permute-start | bytes 3145736 | tf_op jit(solution)/shard_map/ppermute | solution.py:463
  84.7 8.2 %collective-permute-start.6 = (bf16[4096,256]{1,0:T(8,128)(2,1)S(1)}, bf16[4096,256]{1,0:T(8,128)(2,1)S(1)}, u32[]{:S(2)}, u32[]{:S(2)}) collective-permute-start(bf16[4096,256]{1,0:T(8,128)(2,1)S(1)} %broadcast_select_fusion), channel_id=1, source_target_pairs={{0,8},{16,24},{1,9},{17,25},{2,10},{18,26},{3,11},{19,27},{4,12},{... | collective-permute-start | bytes 6291464 | tf_op jit(solution)/shard_map/ppermute | solution.py:463
  114.7 1.3 copy-start.2
  116.0 1.4 copy-start.3
  117.4 0.7 copy-start.8
  118.1 0.7 copy-start.9
  118.7 29.8 %collective-permute-start.7 = (bf16[4096,256]{1,0:T(8,128)(2,1)}, bf16[4096,256]{1,0:T(8,128)(2,1)S(1)}, u32[]{:S(2)}, u32[]{:S(2)}) collective-permute-start(bf16[4096,256]{1,0:T(8,128)(2,1)} %get-tuple-element.56), channel_id=1, source_target_pairs={{0,1},{1,2},{2,3},{3,4},{4,5},{5,6},{6,7},{7,0},{8,9},{9,10},{10,1... | collective-permute-start | bytes 6291464 | tf_op jit(solution)/shard_map/ppermute | solution.py:21
  148.5 1.6 copy-start
  150.1 18.7 %copy-start.4 = (bf16[4096,256]{1,0:T(8,128)(2,1)}, bf16[4096,256]{1,0:T(8,128)(2,1)S(1)}, u32[]{:S(2)}) copy-start(bf16[4096,256]{1,0:T(8,128)(2,1)S(1)} %collective-permute-done.7.low_hbm.low_ref) | copy-start | bytes 6291460
  168.8 0.7 copy-start.10
  169.5 0.7 copy-start.11
  170.1 30.9 %collective-permute-start.8 = (bf16[4096,256]{1,0:T(8,128)(2,1)}, bf16[4096,256]{1,0:T(8,128)(2,1)S(1)}, u32[]{:S(2)}, u32[]{:S(2)}) collective-permute-start(bf16[4096,256]{1,0:T(8,128)(2,1)} %get-tuple-element.59), channel_id=1, source_target_pairs={{0,1},{1,2},{2,3},{3,4},{4,5},{5,6},{6,7},{7,0},{8,9},{9,10},{10,1... | collective-permute-start | bytes 6291464 | tf_op jit(solution)/shard_map/ppermute | solution.py:21
  201.0 1.6 copy-start.1
  202.6 18.7 %copy-start.5 = (bf16[4096,256]{1,0:T(8,128)(2,1)}, bf16[4096,256]{1,0:T(8,128)(2,1)S(1)}, u32[]{:S(2)}) copy-start(bf16[4096,256]{1,0:T(8,128)(2,1)S(1)} %collective-permute-done.8.low_hbm.low_ref) | copy-start | bytes 6291460
  221.3 0.7 copy-start.6
  222.6 32.0 %collective-permute-start.9 = (bf16[4096,256]{1,0:T(8,128)(2,1)}, bf16[4096,256]{1,0:T(8,128)(2,1)S(1)}, u32[]{:S(2)}, u32[]{:S(2)}) collective-permute-start(bf16[4096,256]{1,0:T(8,128)(2,1)} %get-tuple-element.60), channel_id=1, source_target_pairs={{0,1},{1,2},{2,3},{3,4},{4,5},{5,6},{6,7},{7,0},{8,9},{9,10},{10,1... | collective-permute-start | bytes 6291464 | tf_op jit(solution)/shard_map/ppermute | solution.py:21
  254.6 1.4 copy-start.14
  (1 other events, 0.7 us)

commit v4 on v3

--- a/solution.py
+++ b/solution.py
@@ -307,6 +307,7 @@
             num_scalar_prefetch=1, grid=(steps,), in_specs=in_specs, out_specs=out_specs
         ),
         out_shape=shapes,
+        compiler_params=pltpu.CompilerParams(vmem_limit_bytes=16 * 2**20),
         name="pick_blocks",
     )(dest, *[genotypes] * len(wants))
 
@@ -408,22 +409,60 @@
     )(dest, *sources, *held)
 
 
-def top_kernel(top_ref, low_ref, inv_ref, mix_ref, out_ref):
-    out_ref[...] = (
-        dot16(top_ref[...], inv_ref[...], 1, 1) + dot16(low_ref[...], mix_ref[...], 1, 1)
-    ).astype(jnp.bfloat16)
+def top_kernel(top_hbm, low_hbm, inv_hbm, mix_hbm, out_hbm, top_ref, low_ref, inv_ref, mix_ref, new_ref, sems):
+    indiv, size = top_ref.shape
+    count = indiv // CHUNK
+    small = [
+        pltpu.make_async_copy(inv_hbm, inv_ref, sems.at[3 * count]),
+        pltpu.make_async_copy(mix_hbm, mix_ref, sems.at[3 * count + 1]),
+    ]
+    for copy in small:
+        copy.start()
+
+    def fetched(step):
+        rows = pl.ds(pl.multiple_of(step * CHUNK, CHUNK), CHUNK)
+        return [
+            pltpu.make_async_copy(top_hbm.at[rows, :], top_ref.at[rows, :], sems.at[3 * step]),
+            pltpu.make_async_copy(low_hbm.at[rows, :], low_ref.at[rows, :], sems.at[3 * step + 1]),
+        ]
+
+    def sent(step):
+        rows = pl.ds(pl.multiple_of(step * CHUNK, CHUNK), CHUNK)
+        return pltpu.make_async_copy(new_ref.at[rows, :], out_hbm.at[rows, 0:size], sems.at[3 * step + 2])
+
+    for step in range(count):
+        for copy in fetched(step):
+            copy.start()
+    for copy in small:
+        copy.wait()
+
+    def apply(step, carry):
+        for copy in fetched(step):
+            copy.wait()
+        rows = pl.ds(pl.multiple_of(step * CHUNK, CHUNK), CHUNK)
+        new_ref[rows, :] = (
+            dot16(top_ref[rows, :], inv_ref[...], 1, 1) + dot16(low_ref[rows, :], mix_ref[...], 1, 1)
+        ).astype(jnp.bfloat16)
+        sent(step).start()
+        return carry
+
+    lax.fori_loop(0, count, apply, 0)
+    for step in range(count):
+        sent(step).wait()
 
 
 def rotate_top(top, low, inverse, mix, blocks=1):
     indiv, size = top.shape
-    rows = pl.BlockSpec((CHUNK, size), lambda i: (i, 0))
-    whole = pl.BlockSpec((size, size), lambda i: (0, 0))
+    anywhere = pl.BlockSpec(memory_space=pl.ANY)
+    block = pltpu.VMEM((indiv, size), jnp.bfloat16)
+    small = pltpu.VMEM((size, size), jnp.bfloat16)
     return pl.pallas_call(
         top_kernel,
-        grid=(indiv // CHUNK,),
-        in_specs=[rows, rows, whole, whole],
-        out_specs=rows,
+        in_specs=[anywhere] * 4,
+        out_specs=anywhere,
         out_shape=jax.ShapeDtypeStruct((indiv, blocks * size), jnp.bfloat16),
+        scratch_shapes=[block, block, small, small, block, pltpu.SemaphoreType.DMA((3 * (indiv // CHUNK) + 2,))],
+        compiler_params=pltpu.CompilerParams(vmem_limit_bytes=12 * 2**20),
         cost_estimate=pl.CostEstimate(
             flops=4 * indiv * size * size, bytes_accessed=6 * indiv * size, transcendentals=0
         ),
@@ -431,22 +470,38 @@
     )(top, low, inverse, mix)
 
 
-def place_kernel(low_ref, held_ref, out_ref, sem):
-    size = low_ref.shape[1]
-    copy = pltpu.make_async_copy(low_ref, out_ref.at[:, size : 2 * size], sem)
-    copy.start()
-    copy.wait()
+def place_kernel(low_hbm, held_ref, out_hbm, low_ref, sems):
+    indiv, size = low_ref.shape
+    count = indiv // CHUNK
+    into, out = [], []
+    for step in range(count):
+        rows = pl.ds(step * CHUNK, CHUNK)
+        into.append(pltpu.make_async_copy(low_hbm.at[rows, :], low_ref.at[rows, :], sems.at[2 * step]))
+        out.append(
+            pltpu.make_async_copy(low_ref.at[rows, :], out_hbm.at[rows, size : 2 * size], sems.at[2 * step + 1])
+        )
+        into[-1].start()
+    for step in range(count):
+        into[step].wait()
+        out[step].start()
+    for copy in out:
+        copy.wait()
 
 
 def place_low(low, held):
+    indiv, size = low.shape
     anywhere = pl.BlockSpec(memory_space=pl.ANY)
     return pl.pallas_call(
         place_kernel,
-        in_specs=[pl.BlockSpec(memory_space=pltpu.VMEM), anywhere],
+        in_specs=[anywhere] * 2,
         out_specs=anywhere,
         out_shape=jax.ShapeDtypeStruct(held.shape, held.dtype),
         input_output_aliases={1: 0},
-        scratch_shapes=[pltpu.SemaphoreType.DMA],
+        scratch_shapes=[
+            pltpu.VMEM((indiv, size), jnp.bfloat16),
+            pltpu.SemaphoreType.DMA((2 * (indiv // CHUNK),)),
+        ],
+        compiler_params=pltpu.CompilerParams(vmem_limit_bytes=4 * 2**20),
         name="place_low",
     )(low, held)
 
@@ -470,8 +525,8 @@
         dest_group,
         [lambda o: (by_core(jnp.where(present(o, 2), 2, 3), jnp.where(present(o, 1), 1, 2)),)],
     )
-    cross_one = sent(cross, lambda chip: [(chip + 1, far(chip))])
-    cross_zero = sent(cross, lambda chip: [(chip, far(chip))])
+    cross_one = sent(cross, lambda chip: [(chip + 1, far(chip)), (chip, chip + 1)])
+    cross_zero = sent(cross, lambda chip: [(chip, far(chip)), (chip + 1, chip + 1)])
     table, _ = lax.optimization_barrier((genotypes, cross))
     near, own, lent, kept = picked(
         table,
@@ -487,13 +542,12 @@
     near = sent(near, lambda chip: [(chip, chip + 1), (chip + 1, chip)])
     last = jnp.where(jnp.where(present(offsets, 3), core == 0, core == 1), kept, lent)
     last, cross_one, cross_zero = lax.optimization_barrier((last, cross_one, cross_zero))
-    upper = sent(last, lambda chip: [(chip, far(chip) + 1)])
-    lower = sent(last, lambda chip: [(chip + 1, far(chip) + 1)])
+    upper = sent(last, lambda chip: [(chip, far(chip) + 1), (chip + 1, chip)])
+    lower = sent(last, lambda chip: [(chip + 1, far(chip) + 1), (chip, chip)])
+    passed = jnp.where(present(offsets, 2), cross_one, cross_zero)
+    passed = sent(passed, lambda chip: [(chip, chip + 1), (chip + 1, chip)])
     held = list(first_round(dest_group, (own, near, cross_one, cross_zero)))
-    upper, lower, cross_one, cross_zero, held[1] = lax.optimization_barrier(
-        (upper, lower, cross_one, cross_zero, held[1])
-    )
-    passed = sent(jnp.where(present(offsets, 2), cross_one, cross_zero), lambda chip: [(chip, chip + 1)])
+    upper, lower, held[1] = lax.optimization_barrier((upper, lower, held[1]))
     return first_round(dest_group, (own, near, passed), (upper, lower), held)
 
 

time: 260 us -> 237 us (0.912)
  Pallas kernels: 97.9 us -> 80.9 us
  local copies, waits for them, and re-layouts: 11.7 us -> 6.06 us
    pallas_call x4, Pallas kernels: 24.7 us -> 13.2 us  [the longest x3 11.6 us: rotate_top(): pl.pallas_call(top_kernel, in_specs=[anywhere] * 4, out_specs=anywhere, o...]
    pallas_call x2, Pallas kernels: 13.1 us -> 6.5 us  [picked(): pl.pallas_call(cast_kernel, grid_spec=pltpu.PrefetchScalarGridSpec(num_sc...]
    unnamed x30 -> x10, local copies, waits for them, and re-layouts: 11.1 us -> 5.4 us
    ppermute x3, starting transfers between devices: 0.01 us -> 3.97 us  [passed_along(): lax.ppermute(array, axis, [(i, (i + by) % size) for i in range(size)])]
    ppermute x7, starting transfers between devices: 12.9 us -> 10.2 us  [sent(): lax.ppermute(array, 'group', [hop for chip in range(0, num_groups, 2) for...]
  transfers between devices with their start and end apart: 10 -> 10, of which waited for: 8 -> 6; matrix products, arithmetic and copies ran while one was open for 0% -> 0% of each run, Pallas kernels for 12% -> 7%
where the time goes in v4:
time: 237 us
  waiting for transfers between devices  133 us (56%)
  Pallas kernels  80.9 us (34%)
  starting transfers between devices  14.1 us (6%)
  local copies, waits for them, and re-layouts  6.06 us (3%)
  between operations  2.96 us (1%)
    ppermute x3, waiting for transfers between devices, passed_along(): lax.ppermute(array, axis, [(i, (i + by) % size) for i in range(size)])  73.5 us
    ppermute x7, waiting for transfers between devices, sent(): lax.ppermute(array, 'group', [hop for chip in range(0, num_groups, 2) for...  59.1 us
    pallas_call x2, Pallas kernels, rotate_low(): pl.pallas_call(round_kernel, in_specs=[anywhere] * 2, out_specs=[anywhere...  37.6 us
    pallas_call x2, Pallas kernels, first_round(): pl.pallas_call(functools.partial(first_kernel, len(wholes), len(halves)),...  23.6 us
    pallas_call x3, Pallas kernels, rotate_top(): pl.pallas_call(top_kernel, in_specs=[anywhere] * 4, out_specs=anywhere, o...  11.6 us
    ppermute x7, starting transfers between devices, sent(): lax.ppermute(array, 'group', [hop for chip in range(0, num_groups, 2) for...  10.2 us
    pallas_call x2, Pallas kernels, picked(): pl.pallas_call(cast_kernel, grid_spec=pltpu.PrefetchScalarGridSpec(num_sc...  6.5 us
    unnamed x10, local copies, waits for them, and re-layouts  5.4 us
  transfers between devices with their start and end apart: 10, of which 6 were waited for; matrix products, arithmetic and copies ran while one was open for 0% of the time, Pallas kernels for 7%

profile of v4, /device:TPU:1, one launch (start us, length us, event | category | flops | bytes accessed | tf_op | source)
XLA Modules:
  0.0 236.9 jit_solution(8254244370748079229)
XLA Ops:
  0.0 3.4 %copy-done = s32[4096,512]{1,0:T(8,128)S(1)} copy-done((s32[4096,512]{1,0:T(8,128)S(1)}, s32[4096,512]{1,0:T(8,128)}, u32[]{:S(2)}) %copy-start) | copy-done | bytes 8388632
  4.0 2.7 %pick_blocks.2 = bf16[4096,256]{1,0:T(8,128)(2,1)} custom-call(s32[64]{0:T(128)S(1)} %copy-done.1, s32[4096,512]{1,0:T(8,128)S(1)} %copy-done), custom_call_target="tpu_custom_call" | custom-call | tf_op jit(solution)/shard_map/pick_blocks/pallas_call | solution.py:304
  6.8 2.4 collective-permute-start.3
  9.2 2.4 collective-permute-start.2
  11.5 3.8 %pick_blocks.3 = (bf16[4096,256]{1,0:T(8,128)(2,1)}, bf16[4096,256]{1,0:T(8,128)(2,1)S(1)}, bf16[2048,256]{1,0:T(8,128)(2,1)}, bf16[2048,256]{1,0:T(8,128)(2,1)S(1)}) custom-call(s32[64]{0:T(128)S(1)} %copy-done.1, s32[4096,512]{1,0:T(8,128)S(1)} %copy-done, s32[4096,512]{1,0:T(8,128)S(1)} %copy-done, s32[4096,512]{1,0:T(8,128)S(1)} %copy-done, ...), custom_call_target="tpu_custom_call" | custom-call | tf_op jit(solution)/shard_map/pick_blocks/pallas_call | solution.py:304
  15.3 1.4 copy-done.3
  20.6 36.3 %collective-permute-done.2.refs_2_ = bf16[4096,256]{1,0:T(8,128)(2,1)} collective-permute-done((bf16[4096,256]{1,0:T(8,128)(2,1)}, bf16[4096,256]{1,0:T(8,128)(2,1)}, u32[]{:S(2)}, u32[]{:S(2)}) %collective-permute-start.2) | collective-permute-done | bytes 2097184 | tf_op jit(solution)/shard_map/ppermute | solution.py:518
  57.1 1.8 collective-permute-start.4
  58.9 3.0 %collective-permute-start.6 = (bf16[2048,256]{1,0:T(8,128)(2,1)S(1)}, bf16[2048,256]{1,0:T(8,128)(2,1)S(1)}, u32[]{:S(2)}, u32[]{:S(2)}) collective-permute-start(bf16[2048,256]{1,0:T(8,128)(2,1)S(1)} %broadcast_select_fusion.1), channel_id=1, source_target_pairs={{8,24},{0,0},{24,8},{16,16},{9,25},{1,1},{25,9},{17,17},{10,26},{2... | collective-permute-start | bytes 3145736 | tf_op jit(solution)/shard_map/ppermute | solution.py:518
  62.1 0.8 first_round.2
  62.9 21.1 %collective-permute-done.6.refs_4_ = bf16[2048,256]{1,0:T(8,128)(2,1)S(1)} collective-permute-done((bf16[2048,256]{1,0:T(8,128)(2,1)S(1)}, bf16[2048,256]{1,0:T(8,128)(2,1)S(1)}, u32[]{:S(2)}, u32[]{:S(2)}) %collective-permute-start.6) | collective-permute-done | bytes 1048608 | tf_op jit(solution)/shard_map/ppermute | solution.py:518
  84.0 1.7 collective-permute-done.5.refs_3_
  85.7 22.7 %first_round.3 = (bf16[4096,256]{1,0:T(8,128)(2,1)S(1)}, bf16[256,256]{1,0:T(8,128)(2,1)S(1)}, bf16[256,256]{1,0:T(8,128)(2,1)S(1)}, bf16[4096,256]{1,0:T(8,128)(2,1)S(1)}, bf16[4096,256]{1,0:T(8,128)(2,1)S(1)}) custom-call(s32[64]{0:T(128)S(1)} %copy-done.2, ...), custom_call_target="tpu_custom_call", output_to_operand_aliasing={{0}: (6, {}), {1}: (7, {}), {2}: (8, {}), {3}: (9, {}), {4}... | custom-call | flops 10737418240 | bytes 16777216 | tf_op jit(solution)/shard_map/first_round/pallas_call | solution.py:399
  108.4 2.9 %collective-permute-start.7 = (bf16[4096,256]{1,0:T(8,128)(2,1)S(1)}, bf16[4096,256]{1,0:T(8,128)(2,1)S(1)}, u32[]{:S(2)}, u32[]{:S(2)}) collective-permute-start(bf16[4096,256]{1,0:T(8,128)(2,1)S(1)} %get-tuple-element.52), channel_id=1, source_target_pairs={{0,1},{1,2},{2,3},{3,4},{4,5},{5,6},{6,7},{7,0},{8,9},{9,10},{10,1... | collective-permute-start | bytes 6291464 | tf_op jit(solution)/shard_map/ppermute | solution.py:21
  111.4 3.7 %rotate_top.3.top_hbm = bf16[4096,256]{1,0:T(8,128)(2,1)S(1)} custom-call(bf16[4096,256]{1,0:T(8,128)(2,1)S(1)} %get-tuple-element.48.top_hbm, bf16[4096,256]{1,0:T(8,128)(2,1)S(1)} %get-tuple-element.49.low_hbm, bf16[256,256]{1,0:T(8,128)(2,1)S(1)} %get-tuple-element.50.inv_hbm, bf16[256,256]{1,0:T(8,128)(2,1)S(1)} %get-tuple-element.51.mix_hbm), custom_call_target="tpu_custom_call" | custom-call | flops 1073741824 | bytes 6291456 | tf_op jit(solution)/shard_map/rotate_top/pallas_call | solution.py:459
  115.1 22.4 %collective-permute-done.7.low_hbm = bf16[4096,256]{1,0:T(8,128)(2,1)S(1)} collective-permute-done((bf16[4096,256]{1,0:T(8,128)(2,1)S(1)}, bf16[4096,256]{1,0:T(8,128)(2,1)S(1)}, u32[]{:S(2)}, u32[]{:S(2)}) %collective-permute-start.7) | collective-permute-done | bytes 2097184 | tf_op jit(solution)/shard_map/ppermute | solution.py:21
  137.4 18.8 %rotate_low.2 = (bf16[4096,256]{1,0:T(8,128)(2,1)S(1)}, bf16[256,256]{1,0:T(8,128)(2,1)S(1)}, bf16[256,256]{1,0:T(8,128)(2,1)S(1)}) custom-call(bf16[4096,256]{1,0:T(8,128)(2,1)S(1)} %rotate_top.3.top_hbm, bf16[4096,256]{1,0:T(8,128)(2,1)S(1)} %collective-permute-done.7.low_hbm), custom_call_target="tpu_custom_call" | custom-call | flops 10737418240 | bytes 16777216 | tf_op jit(solution)/shard_map/rotate_low/pallas_call | solution.py:257
  156.3 1.0 collective-permute-start.8
  157.2 3.7 %rotate_top.4.top_hbm = bf16[4096,256]{1,0:T(8,128)(2,1)S(1)} custom-call(bf16[4096,256]{1,0:T(8,128)(2,1)S(1)} %rotate_top.3.top_hbm, bf16[4096,256]{1,0:T(8,128)(2,1)S(1)} %collective-permute-done.7.low_hbm, bf16[256,256]{1,0:T(8,128)(2,1)S(1)} %get-tuple-element.53.inv_hbm, bf16[256,256]{1,0:T(8,128)(2,1)S(1)} %get-tuple-element.54.mix_hbm), custom_call_target="tpu_custom_call" | custom-call | flops 1073741824 | bytes 6291456 | tf_op jit(solution)/shard_map/rotate_top/pallas_call | solution.py:459
  160.9 24.9 %collective-permute-done.8.low_hbm = bf16[4096,256]{1,0:T(8,128)(2,1)S(1)} collective-permute-done((bf16[4096,256]{1,0:T(8,128)(2,1)S(1)}, bf16[4096,256]{1,0:T(8,128)(2,1)S(1)}, u32[]{:S(2)}, u32[]{:S(2)}) %collective-permute-start.8) | collective-permute-done | bytes 2097184 | tf_op jit(solution)/shard_map/ppermute | solution.py:21
  185.8 18.8 %rotate_low.3 = (bf16[4096,256]{1,0:T(8,128)(2,1)S(1)}, bf16[256,256]{1,0:T(8,128)(2,1)S(1)}, bf16[256,256]{1,0:T(8,128)(2,1)S(1)}) custom-call(bf16[4096,256]{1,0:T(8,128)(2,1)S(1)} %rotate_top.4.top_hbm, bf16[4096,256]{1,0:T(8,128)(2,1)S(1)} %collective-permute-done.8.low_hbm), custom_call_target="tpu_custom_call" | custom-call | flops 10737418240 | bytes 16777216 | tf_op jit(solution)/shard_map/rotate_low/pallas_call | solution.py:257
  204.7 4.3 %rotate_top.5.held_ref = bf16[4096,512]{1,0:T(8,128)(2,1)} custom-call(bf16[4096,256]{1,0:T(8,128)(2,1)S(1)} %rotate_top.4.top_hbm, bf16[4096,256]{1,0:T(8,128)(2,1)S(1)} %collective-permute-done.8.low_hbm, bf16[256,256]{1,0:T(8,128)(2,1)S(1)} %get-tuple-element.57.inv_hbm, bf16[256,256]{1,0:T(8,128)(2,1)S(1)} %get-tuple-element.58.mix_hbm), custom_call_target="tpu_custom_call" | custom-call | flops 1073741824 | bytes 6291456 | tf_op jit(solution)/shard_map/rotate_top/pallas_call | solution.py:459
  208.9 26.3 %collective-permute-done.9.low_hbm = bf16[4096,256]{1,0:T(8,128)(2,1)S(1)} collective-permute-done((bf16[4096,256]{1,0:T(8,128)(2,1)S(1)}, bf16[4096,256]{1,0:T(8,128)(2,1)S(1)}, u32[]{:S(2)}, u32[]{:S(2)}) %collective-permute-start.9) | collective-permute-done | bytes 2097184 | tf_op jit(solution)/shard_map/ppermute | solution.py:21
  235.2 1.6 place_low.1
  (19 shorter events, 2.3 us)
Async XLA Ops:
  0.0 3.4 %copy-start = (s32[4096,512]{1,0:T(8,128)S(1)}, s32[4096,512]{1,0:T(8,128)}, u32[]{:S(2)}) copy-start(s32[4096,512]{1,0:T(8,128)} %refs_3_) | copy-start | bytes 25165828
  3.4 0.7 copy-start.1
  6.8 10.4 %copy-start.2 = (s32[64]{0:T(128)S(1)}, s32[64]{0:T(128)}, u32[]{:S(2)}) copy-start(s32[64]{0:T(128)} %dest.7) | copy-start | bytes 772
  6.8 13.8 %collective-permute-start.3 = (bf16[4096,256]{1,0:T(8,128)(2,1)}, bf16[4096,256]{1,0:T(8,128)(2,1)S(1)}, u32[]{:S(2)}, u32[]{:S(2)}) collective-permute-start(bf16[4096,256]{1,0:T(8,128)(2,1)} %pick_blocks.2), channel_id=1, source_target_pairs={{0,16},{8,8},{16,0},{24,24},{1,17},{9,9},{17,1},{25,25},{2,18},{10... | collective-permute-start | bytes 6291464 | tf_op jit(solution)/shard_map/ppermute | solution.py:518
  9.2 47.7 %collective-permute-start.2 = (bf16[4096,256]{1,0:T(8,128)(2,1)}, bf16[4096,256]{1,0:T(8,128)(2,1)}, u32[]{:S(2)}, u32[]{:S(2)}) collective-permute-start(bf16[4096,256]{1,0:T(8,128)(2,1)} %pick_blocks.2), channel_id=1, source_target_pairs={{8,16},{0,8},{24,0},{16,24},{9,17},{1,9},{25,1},{17,25},{10,18},{2... | collective-permute-start | bytes 6291464 | tf_op jit(solution)/shard_map/ppermute | solution.py:518
  15.3 1.4 copy-start.3
  16.6 3.8 %collective-permute-start.1 = (bf16[2048,256]{1,0:T(8,128)(2,1)}, bf16[2048,256]{1,0:T(8,128)(2,1)}, u32[]{:S(2)}, u32[]{:S(2)}) collective-permute-start(bf16[2048,256]{1,0:T(8,128)(2,1)} %get-tuple-element.36), channel_id=1, source_target_pairs={{0,8},{8,0},{16,24},{24,16},{1,9},{9,1},{17,25},{25,17},{2,10},{10... | collective-permute-start | bytes 3145736 | tf_op jit(solution)/shard_map/ppermute | solution.py:518
  17.0 45.0 %collective-permute-start = (bf16[4096,256]{1,0:T(8,128)(2,1)}, bf16[4096,256]{1,0:T(8,128)(2,1)}, u32[]{:S(2)}, u32[]{:S(2)}) collective-permute-start(bf16[4096,256]{1,0:T(8,128)(2,1)} %get-tuple-element.34), channel_id=1, source_target_pairs={{0,8},{8,0},{16,24},{24,16},{1,9},{9,1},{17,25},{25,17},{2,10},{10... | collective-permute-start | bytes 6291464 | tf_op jit(solution)/shard_map/ppermute | solution.py:518
  56.9 5.2 %copy-start.4 = (bf16[4096,256]{1,0:T(8,128)(2,1)S(1)}, bf16[4096,256]{1,0:T(8,128)(2,1)}, u32[]{:S(2)}) copy-start(bf16[4096,256]{1,0:T(8,128)(2,1)} %copy-done.3) | copy-start | bytes 6291460
  57.1 28.6 %collective-permute-start.4 = (bf16[4096,256]{1,0:T(8,128)(2,1)S(1)}, bf16[4096,256]{1,0:T(8,128)(2,1)S(1)}, u32[]{:S(2)}, u32[]{:S(2)}) collective-permute-start(bf16[4096,256]{1,0:T(8,128)(2,1)S(1)} %broadcast_select_fusion), channel_id=1, source_target_pairs={{0,8},{8,0},{16,24},{24,16},{1,9},{9,1},{17,25},{25,17},{2,10},{10... | collective-permute-start | bytes 6291464 | tf_op jit(solution)/shard_map/ppermute | solution.py:518
  58.9 25.0 %collective-permute-start.6 = (bf16[2048,256]{1,0:T(8,128)(2,1)S(1)}, bf16[2048,256]{1,0:T(8,128)(2,1)S(1)}, u32[]{:S(2)}, u32[]{:S(2)}) collective-permute-start(bf16[2048,256]{1,0:T(8,128)(2,1)S(1)} %broadcast_select_fusion.1), channel_id=1, source_target_pairs={{8,24},{0,0},{24,8},{16,16},{9,25},{1,1},{25,9},{17,17},{10,26},{2... | collective-permute-start | bytes 3145736 | tf_op jit(solution)/shard_map/ppermute | solution.py:518
  62.0 23.7 %collective-permute-start.5 = (bf16[2048,256]{1,0:T(8,128)(2,1)S(1)}, bf16[2048,256]{1,0:T(8,128)(2,1)S(1)}, u32[]{:S(2)}, u32[]{:S(2)}) collective-permute-start(bf16[2048,256]{1,0:T(8,128)(2,1)S(1)} %broadcast_select_fusion.1), channel_id=1, source_target_pairs={{0,24},{8,0},{16,8},{24,16},{1,25},{9,1},{17,9},{25,17},{2,26},{10... | collective-permute-start | bytes 3145736 | tf_op jit(solution)/shard_map/ppermute | solution.py:518
  108.4 29.0 %collective-permute-start.7 = (bf16[4096,256]{1,0:T(8,128)(2,1)S(1)}, bf16[4096,256]{1,0:T(8,128)(2,1)S(1)}, u32[]{:S(2)}, u32[]{:S(2)}) collective-permute-start(bf16[4096,256]{1,0:T(8,128)(2,1)S(1)} %get-tuple-element.52), channel_id=1, source_target_pairs={{0,1},{1,2},{2,3},{3,4},{4,5},{5,6},{6,7},{7,0},{8,9},{9,10},{10,1... | collective-permute-start | bytes 6291464 | tf_op jit(solution)/shard_map/ppermute | solution.py:21
  156.3 29.5 %collective-permute-start.8 = (bf16[4096,256]{1,0:T(8,128)(2,1)S(1)}, bf16[4096,256]{1,0:T(8,128)(2,1)S(1)}, u32[]{:S(2)}, u32[]{:S(2)}) collective-permute-start(bf16[4096,256]{1,0:T(8,128)(2,1)S(1)} %get-tuple-element.55), channel_id=1, source_target_pairs={{0,1},{1,2},{2,3},{3,4},{4,5},{5,6},{6,7},{7,0},{8,9},{9,10},{10,1... | collective-permute-start | bytes 6291464 | tf_op jit(solution)/shard_map/ppermute | solution.py:21
  204.6 30.6 %collective-permute-start.9 = (bf16[4096,256]{1,0:T(8,128)(2,1)S(1)}, bf16[4096,256]{1,0:T(8,128)(2,1)S(1)}, u32[]{:S(2)}, u32[]{:S(2)}) collective-permute-start(bf16[4096,256]{1,0:T(8,128)(2,1)S(1)} %get-tuple-element.56), channel_id=1, source_target_pairs={{0,1},{1,2},{2,3},{3,4},{4,5},{5,6},{6,7},{7,0},{8,9},{9,10},{10,1... | collective-permute-start | bytes 6291464 | tf_op jit(solution)/shard_map/ppermute | solution.py:21

commit v5 on v4

--- a/solution.py
+++ b/solution.py
@@ -10,7 +10,10 @@
 ROUNDS = 3
 SUB = 8
 PANEL = 32
-CHUNK = 512
+LANES = 128
+HALF = LANES // 2
+CHUNK = 2048
+PIECE = 512
 
 epsilon = 1e-05
 f32 = jnp.float32
@@ -37,49 +40,62 @@
     return (rows == cols).astype(f32)
 
 
-def inverse_of(x):
-    guess = pl.reciprocal(x, approx=True)
-    return guess * (2.0 - x * guess)
-
-
-def panel_inverse(panel, size):
-    width = 4 * size
-    half = 2 * size
-    tile = (SUB, width)
-    first = lax.broadcasted_iota(jnp.int32, tile, 1) < half
+def eliminate(block, rows):
+    tile = (SUB, LANES)
+    count = PANEL // SUB
+    wide = rows.shape[1] // LANES
+    first = lax.broadcasted_iota(jnp.int32, tile, 1) < HALF
     sub = lax.broadcasted_iota(jnp.int32, tile, 0)
-    count = size // SUB
-    work = [panel[SUB * t : SUB * t + SUB, :] for t in range(count)]
+
+    def down(value, j):
+        return jnp.broadcast_to(value[j : j + 1, :], tile)
+
+    def along(value, k):
+        return jnp.where(
+            first,
+            jnp.broadcast_to(value[:, k : k + 1], tile),
+            jnp.broadcast_to(value[:, HALF + k : HALF + k + 1], tile),
+        )
+
+    block = [block[SUB * t : SUB * t + SUB, :] for t in range(count)]
+    work = [
+        [rows[SUB * t : SUB * t + SUB, LANES * w : LANES * w + LANES] for w in range(wide)] for t in range(count)
+    ]
     done = []
+    ready = [[along(part, k) for part in block] for k in range(SUB)]
     for g in range(count):
-        columns = []
+        later = SUB * (g + 1)
+        ahead = []
+        if g + 1 < count:
+            ahead = [[None] * (g + 1) + [along(part, later + k) for part in block[g + 1 :]] for k in range(SUB)]
+        head = {(m, l): down(ready[l][g], m) for l in range(SUB) for m in range(l, SUB)}
+        pivots = head[0, 0]
         for j in range(SUB):
-            k = SUB * g + j
-            columns.append(
-                {
-                    t: jnp.where(
-                        first,
-                        jnp.broadcast_to(work[t][:, k : k + 1], tile),
-                        jnp.broadcast_to(work[t][:, half + k : half + k + 1], tile),
-                    )
-                    for t in range(g, count)
-                }
-            )
-        pivots = jnp.ones(tile, f32)
-        for j in range(SUB):
-            pivot = jnp.broadcast_to(columns[j][g][j : j + 1, :], tile)
-            pivots = jnp.where(sub == j, pivot, pivots)
-            inverse = inverse_of(pivot)
-            row = jnp.broadcast_to(work[g][j : j + 1, :], tile)
-            heads = {m: jnp.broadcast_to(columns[m][g][j : j + 1, :], tile) for m in range(j + 1, SUB)}
+            pivot = head[j, j]
+            if j:
+                pivots = jnp.where(sub == j, pivot, pivots)
+            guess = pl.reciprocal(pivot, approx=True)
+            mend = 2.0 - pivot * guess
+            inverse = guess * mend
+            for l in range(j + 1, SUB):
+                for m in range(l, SUB):
+                    head[m, l] = head[m, l] - (head[l, j] * head[m, j]) * guess * mend
+            own = [down(part, j) for part in work[g]]
+            own_block = down(block[g], j)
             for t in range(g, count):
-                factor = columns[j][t] * inverse
+                factor = ready[j][t] * inverse
                 if t == g:
                     factor = jnp.where(sub > j, factor, 0.0)
                 for m in range(j + 1, SUB):
-                    columns[m][t] = columns[m][t] - factor * heads[m]
-                work[t] = work[t] - factor * row
-        done.append(work[g] * lax.rsqrt(pivots))
+                    ready[m][t] = ready[m][t] - factor * head[m, j]
+                if t > g:
+                    for k, column in enumerate(ahead):
+                        column[t] = column[t] - factor * down(ready[j][g + 1], k)
+                block[t] = block[t] - factor * own_block
+                work[t] = [part - factor * spread for part, spread in zip(work[t], own)]
+        scale = lax.rsqrt(pivots)
+        done.append(jnp.concatenate([part * scale for part in work[g]], axis=1))
+        ready = ahead
     return jnp.concatenate(done, axis=0)
 
 
@@ -98,46 +114,42 @@
     return jnp.concatenate([terms[i] for i in order], axis=axis)
 
 
-def invert_factors(grams, size):
-    wide = (PANEL, 4 * PANEL)
-    lane = lax.broadcasted_iota(jnp.int32, wide, 1)
-    sub = lax.broadcasted_iota(jnp.int32, wide, 0)
-    inverse_part = lane % (2 * PANEL) >= PANEL
-    eyes = (lane % (2 * PANEL) == sub + PANEL).astype(f32)
-    row_lane = lax.broadcasted_iota(jnp.int32, (PANEL, size), 1)
-    row_sub = lax.broadcasted_iota(jnp.int32, (PANEL, size), 0)
-    all_lane = lax.broadcasted_iota(jnp.int32, (size, size), 1)
-    zero = jnp.zeros((PANEL, size), f32)
+def laced(pair):
+    size = pair[0].shape[1]
+    return jnp.concatenate([part[:, at : at + HALF] for at in range(0, size, HALF) for part in pair], axis=1)
+
+
+def unlaced(both, side):
+    size = both.shape[1]
+    return jnp.concatenate([both[:, at : at + HALF] for at in range(side * HALF, size, LANES)], axis=1)
+
+
+def invert_factors(gram, size):
+    def columns(rows):
+        lane = lax.broadcasted_iota(jnp.int32, (rows, 2 * size), 1)
+        return (lane // LANES) * HALF + lane % HALF, lane % LANES < HALF
+
+    row_column, _ = columns(PANEL)
+    row_sub = lax.broadcasted_iota(jnp.int32, (PANEL, 2 * size), 0)
+    part_column, part_first = columns(HALF)
 
     def step(index, carry):
         start = pl.multiple_of(index * PANEL, PANEL)
         stop = start + PANEL
-        rows = [gram[pl.ds(start, PANEL), :] for gram in grams]
-        blocks = []
-        for side in range(2):
-            block = rows[side][:, 0 : 4 * PANEL]
-            for at in range(4 * PANEL, size, 4 * PANEL):
-                block = jnp.where(start >= at, rows[side][:, at : at + 4 * PANEL], block)
-            blocks.append(pltpu.roll(block, lax.rem(2 * PANEL * side + 4 * size - start, 4 * PANEL), 1))
-        panel = jnp.where(inverse_part, eyes, jnp.where(lane < 2 * PANEL, blocks[0], blocks[1]))
-        inverse = jnp.where(inverse_part, panel_inverse(panel, PANEL), 0.0)
-        inverse = jnp.concatenate(
-            [jnp.where(lane < 2 * PANEL, inverse, 0.0), jnp.where(lane >= 2 * PANEL, inverse, 0.0)], axis=0
-        )
-        within = (row_lane >= start) & (row_lane < stop)
-        eye = (row_lane - start == row_sub).astype(f32)
-        rows = [jnp.where(within, eye, part) for part in rows]
-        left = split(inverse)
-        right = split(jnp.concatenate([zero, rows[0], zero, rows[1]], axis=0))
-        done = dot16(stacked(left, LEFT, 1), stacked(right, RIGHT, 0), 1, 0)
-        terms = split(done)
-        for side, gram in enumerate(grams):
-            own = slice(side * PANEL, (side + 1) * PANEL)
-            right = [term[own, :] for term in terms]
-            left = [jnp.where(row_lane >= stop, term, jnp.zeros_like(term)) for term in right]
-            change = dot16(stacked(left, LEFT, 0), stacked(right, RIGHT, 0), 0, 0)
-            gram[...] = jnp.where((all_lane >= start) & (all_lane < stop), 0.0, gram[...]) - change
-            gram[pl.ds(start, PANEL), :] = done[own, :]
+        lanes = pl.ds(pl.multiple_of(lax.div(start, HALF) * LANES, LANES), LANES)
+        block = pltpu.roll(gram[pl.ds(start, PANEL), lanes], lax.rem(LANES - lax.rem(start, HALF), LANES), 1)
+        eye = (row_column - start == row_sub).astype(f32)
+        within = (row_column >= start) & (row_column < stop)
+        rows = eliminate(block, jnp.where(within, eye, gram[pl.ds(start, PANEL), :]))
+        right = split(rows)
+        left = [jnp.where(row_column >= stop, term, jnp.zeros_like(term)) for term in right]
+        change = dot16(stacked(left, LEFT, 0), stacked(right, RIGHT, 0), 0, 0)
+        for part in range(size // HALF):
+            at = part * LANES
+            own = jnp.where(part_first, change[at : at + HALF, :], change[at + HALF : at + LANES, :])
+            held = pl.ds(part * HALF, HALF)
+            gram[held, :] = jnp.where((part_column >= start) & (part_column < stop), 0.0, gram[held, :]) - own
+        gram[pl.ds(start, PANEL), :] = rows
         return carry
 
     lax.fori_loop(0, size // PANEL, step, 0)
@@ -156,18 +168,17 @@
 def rotate(refs, outs, scratch, sems):
     top_ref, low_ref = refs
     low_out, inv_out, mix_out = outs
-    cross_ref, norm_ref, gram1, gram2, new_ref, inv_ref, mix_ref = scratch
+    cross_ref, norm_ref, gram, new_ref, inv_ref, mix_ref = scratch
     indiv, size = top_ref.shape
     norm_top = dot(norm_ref[0:SUB, :], jnp.ones((SUB, size), f32), 0, 0)
     norm_low = norm_ref[SUB : SUB + 1, :]
     coupling = 2.0 * cross_ref[...] / (norm_top + norm_low + epsilon)
     eye = identity(size)
-    gram1[...] = eye + dot(coupling, coupling, 1, 1)
-    gram2[...] = eye + dot(coupling, coupling, 0, 0)
-    invert_factors((gram1, gram2), size)
+    gram[...] = laced((eye + dot(coupling, coupling, 1, 1), eye + dot(coupling, coupling, 0, 0)))
+    invert_factors(gram, size)
     below = lax.broadcasted_iota(jnp.int32, (size, size), 0) >= lax.broadcasted_iota(jnp.int32, (size, size), 1)
-    inverse1 = jnp.where(below, gram1[...], 0.0)
-    inverse2 = jnp.where(below, gram2[...], 0.0)
+    inverse1 = jnp.where(below, unlaced(gram[...], 0), 0.0)
+    inverse2 = jnp.where(below, unlaced(gram[...], 1), 0.0)
     from_top = dot(coupling, inverse2, 1, 1).astype(jnp.bfloat16)
     from_low = inverse2.astype(jnp.bfloat16)
     count = indiv // CHUNK
@@ -208,8 +219,7 @@
         block,
         pltpu.VMEM((size, size), f32),
         pltpu.VMEM((2 * SUB, size), f32),
-        pltpu.VMEM((size, size), f32),
-        pltpu.VMEM((size, size), f32),
+        pltpu.VMEM((size, 2 * size), f32),
         block,
         small,
         small,
@@ -222,27 +232,41 @@
     return pl.CostEstimate(flops=40 * indiv * size * size, bytes_accessed=16 * indiv * size, transcendentals=0)
 
 
-def round_kernel(top_hbm, low_hbm, low_out, inv_out, mix_out, top_ref, low_ref, cross_ref, norm_ref, *rest):
+def start_low(lows, copy_of):
+    for core, low_hbm in enumerate(lows):
+        if len(lows) == 1:
+            copy_of(low_hbm).start()
+        else:
+
+            @pl.when(lax.axis_index("group") % 2 == core)
+            def _():
+                copy_of(low_hbm).start()
+
+
+def round_kernel(lows, top_hbm, *refs):
+    lows, refs = refs[:lows], refs[lows:]
+    low_out, inv_out, mix_out, top_ref, low_ref, cross_ref, norm_ref, *rest = refs
     *scratch, sems, in_sems = rest
     indiv, size = top_ref.shape
     count = indiv // CHUNK
 
-    def fetched(step):
-        rows = pl.ds(pl.multiple_of(step * CHUNK, CHUNK), CHUNK)
-        return [
-            pltpu.make_async_copy(top_hbm.at[rows, :], top_ref.at[rows, :], in_sems.at[2 * step]),
-            pltpu.make_async_copy(low_hbm.at[rows, :], low_ref.at[rows, :], in_sems.at[2 * step + 1]),
-        ]
+    def fetch_top(step):
+        rows = pl.ds(pl.multiple_of(step * CHUNK, CHUNK), CHUNK)
+        return pltpu.make_async_copy(top_hbm.at[rows, :], top_ref.at[rows, :], in_sems.at[2 * step])
+
+    def fetch_low(step, low_hbm=lows[0]):
+        rows = pl.ds(pl.multiple_of(step * CHUNK, CHUNK), CHUNK)
+        return pltpu.make_async_copy(low_hbm.at[rows, :], low_ref.at[rows, :], in_sems.at[2 * step + 1])
 
     for step in range(count):
-        for copy in fetched(step):
-            copy.start()
+        fetch_top(step).start()
+        start_low(lows, functools.partial(fetch_low, step))
     cross_ref[...] = jnp.zeros_like(cross_ref)
     norm_ref[...] = jnp.zeros_like(norm_ref)
 
     def accumulate(step, carry):
-        for copy in fetched(step):
-            copy.wait()
+        fetch_top(step).wait()
+        fetch_low(step).wait()
         take_grams(pl.ds(pl.multiple_of(step * CHUNK, CHUNK), CHUNK), top_ref, low_ref, cross_ref, norm_ref)
         return carry
 
@@ -250,20 +274,20 @@
     rotate((top_ref, low_ref), (low_out, inv_out, mix_out), (cross_ref, norm_ref, *scratch), sems)
 
 
-def rotate_low(top, low):
+def rotate_low(top, lows):
     indiv, size = top.shape
     square = jax.ShapeDtypeStruct((size, size), jnp.bfloat16)
     anywhere = pl.BlockSpec(memory_space=pl.ANY)
     return pl.pallas_call(
-        round_kernel,
-        in_specs=[anywhere] * 2,
+        functools.partial(round_kernel, len(lows)),
+        in_specs=[anywhere] * (1 + len(lows)),
         out_specs=[anywhere] * 3,
         out_shape=[jax.ShapeDtypeStruct((indiv, size), jnp.bfloat16), square, square],
         scratch_shapes=scratch_of(indiv, size),
         compiler_params=pltpu.CompilerParams(vmem_limit_bytes=16 * 2**20),
         cost_estimate=cost(indiv, size),
         name="rotate_low",
-    )(top, low)
+    )(top, *lows)
 
 
 def offsets_of(dest):
@@ -285,7 +309,7 @@
         out_ref[...] = counts_ref[...].astype(out_ref.dtype)
 
 
-def picked(genotypes, dest, wants):
+def picked(genotypes, dest, wants, room):
     indiv, size = genotypes.shape[0], genotypes.shape[1] // 2
     steps = 4
     in_specs, out_specs, shapes = [], [], []
@@ -307,14 +331,14 @@
             num_scalar_prefetch=1, grid=(steps,), in_specs=in_specs, out_specs=out_specs
         ),
         out_shape=shapes,
-        compiler_params=pltpu.CompilerParams(vmem_limit_bytes=16 * 2**20),
+        compiler_params=pltpu.CompilerParams(vmem_limit_bytes=room * 2**20),
         name="pick_blocks",
     )(dest, *[genotypes] * len(wants))
 
 
 def first_kernel(wholes, halves, dest, *refs):
     sources = refs[: wholes + halves]
-    held = 5 if halves else 0
+    held = 4 if halves else 0
     low_out, inv_out, mix_out, top_scaled, low_scaled = refs[wholes + halves + held : wholes + halves + held + 5]
     top_ref, low_ref, cross_ref, norm_ref, *rest = refs[wholes + halves + held + 5 :]
     *scratch, sems, in_sems = rest
@@ -353,13 +377,13 @@
                 pltpu.make_async_copy(sources[0].at[rows, :], target.at[rows, :], in_sems.at[2 * side + part]).wait()
 
             def add(step, sums):
-                values = target[pl.ds(pl.multiple_of(step * CHUNK, CHUNK), CHUNK), :].astype(f32)
+                values = target[pl.ds(pl.multiple_of(step * PIECE, PIECE), PIECE), :].astype(f32)
                 return (
                     sums[0] + jnp.sum(values, axis=0, keepdims=True),
                     sums[1] + jnp.sum(values * values, axis=0, keepdims=True),
                 )
 
-            total, squares = lax.fori_loop(0, count, add, (jnp.zeros((1, size), f32),) * 2)
+            total, squares = lax.fori_loop(0, indiv // PIECE, add, (jnp.zeros((1, size), f32),) * 2)
             whole = total.astype(jnp.int32)
             spread = indiv * squares.astype(jnp.int32) - whole * whole
             variance = spread.astype(f32) * (1.0 / (indiv * indiv))
@@ -401,7 +425,7 @@
         in_specs=[pl.BlockSpec(memory_space=pltpu.SMEM)] + [anywhere] * (len(sources) + len(held)),
         out_specs=[anywhere] * 5,
         out_shape=[block, square, square, block, block],
-        input_output_aliases={1 + len(sources) + i: i for i in range(len(held))},
+        input_output_aliases={1 + len(sources) + i: 1 + i for i in range(len(held))},
         scratch_shapes=scratch,
         compiler_params=pltpu.CompilerParams(vmem_limit_bytes=16 * 2**20),
         cost_estimate=cost(indiv, size),
@@ -409,7 +433,9 @@
     )(dest, *sources, *held)
 
 
-def top_kernel(top_hbm, low_hbm, inv_hbm, mix_hbm, out_hbm, top_ref, low_ref, inv_ref, mix_ref, new_ref, sems):
+def top_kernel(lows, top_hbm, *refs):
+    lows, refs = refs[:lows], refs[lows:]
+    inv_hbm, mix_hbm, out_hbm, top_ref, low_ref, inv_ref, mix_ref, new_ref, sems = refs
     indiv, size = top_ref.shape
     count = indiv // CHUNK
     small = [
@@ -419,26 +445,27 @@
     for copy in small:
         copy.start()
 
-    def fetched(step):
-        rows = pl.ds(pl.multiple_of(step * CHUNK, CHUNK), CHUNK)
-        return [
-            pltpu.make_async_copy(top_hbm.at[rows, :], top_ref.at[rows, :], sems.at[3 * step]),
-            pltpu.make_async_copy(low_hbm.at[rows, :], low_ref.at[rows, :], sems.at[3 * step + 1]),
-        ]
+    def fetch_top(step):
+        rows = pl.ds(pl.multiple_of(step * CHUNK, CHUNK), CHUNK)
+        return pltpu.make_async_copy(top_hbm.at[rows, :], top_ref.at[rows, :], sems.at[3 * step])
+
+    def fetch_low(step, low_hbm=lows[0]):
+        rows = pl.ds(pl.multiple_of(step * CHUNK, CHUNK), CHUNK)
+        return pltpu.make_async_copy(low_hbm.at[rows, :], low_ref.at[rows, :], sems.at[3 * step + 1])
 
     def sent(step):
         rows = pl.ds(pl.multiple_of(step * CHUNK, CHUNK), CHUNK)
         return pltpu.make_async_copy(new_ref.at[rows, :], out_hbm.at[rows, 0:size], sems.at[3 * step + 2])
 
     for step in range(count):
-        for copy in fetched(step):
-            copy.start()
+        fetch_top(step).start()
+        start_low(lows, functools.partial(fetch_low, step))
     for copy in small:
         copy.wait()
 
     def apply(step, carry):
-        for copy in fetched(step):
-            copy.wait()
+        fetch_top(step).wait()
+        fetch_low(step).wait()
         rows = pl.ds(pl.multiple_of(step * CHUNK, CHUNK), CHUNK)
         new_ref[rows, :] = (
             dot16(top_ref[rows, :], inv_ref[...], 1, 1) + dot16(low_ref[rows, :], mix_ref[...], 1, 1)
@@ -451,14 +478,14 @@
         sent(step).wait()
 
 
-def rotate_top(top, low, inverse, mix, blocks=1):
+def rotate_top(top, lows, inverse, mix, blocks=1):
     indiv, size = top.shape
     anywhere = pl.BlockSpec(memory_space=pl.ANY)
     block = pltpu.VMEM((indiv, size), jnp.bfloat16)
     small = pltpu.VMEM((size, size), jnp.bfloat16)
     return pl.pallas_call(
-        top_kernel,
-        in_specs=[anywhere] * 4,
+        functools.partial(top_kernel, len(lows)),
+        in_specs=[anywhere] * (3 + len(lows)),
         out_specs=anywhere,
         out_shape=jax.ShapeDtypeStruct((indiv, blocks * size), jnp.bfloat16),
         scratch_shapes=[block, block, small, small, block, pltpu.SemaphoreType.DMA((3 * (indiv // CHUNK) + 2,))],
@@ -467,15 +494,15 @@
             flops=4 * indiv * size * size, bytes_accessed=6 * indiv * size, transcendentals=0
         ),
         name="rotate_top",
-    )(top, low, inverse, mix)
+    )(top, *lows, inverse, mix)
 
 
 def place_kernel(low_hbm, held_ref, out_hbm, low_ref, sems):
     indiv, size = low_ref.shape
-    count = indiv // CHUNK
+    count = indiv // PIECE
     into, out = [], []
     for step in range(count):
-        rows = pl.ds(step * CHUNK, CHUNK)
+        rows = pl.ds(step * PIECE, PIECE)
         into.append(pltpu.make_async_copy(low_hbm.at[rows, :], low_ref.at[rows, :], sems.at[2 * step]))
         out.append(
             pltpu.make_async_copy(low_ref.at[rows, :], out_hbm.at[rows, size : 2 * size], sems.at[2 * step + 1])
@@ -499,13 +526,23 @@
         input_output_aliases={1: 0},
         scratch_shapes=[
             pltpu.VMEM((indiv, size), jnp.bfloat16),
-            pltpu.SemaphoreType.DMA((2 * (indiv // CHUNK),)),
+            pltpu.SemaphoreType.DMA((2 * (indiv // PIECE),)),
         ],
         compiler_params=pltpu.CompilerParams(vmem_limit_bytes=4 * 2**20),
         name="place_low",
     )(low, held)
 
 
+def next_pair(array, core):
+    groups, pairs = lax.axis_size("group"), lax.axis_size("pair")
+    hops = []
+    for group in range(groups):
+        for pair in range(pairs):
+            to = (pair + 1) % pairs if group % 2 == core else pair
+            hops.append((group * pairs + pair, group * pairs + to))
+    return lax.ppermute(array, ("group", "pair"), hops)
+
+
 def regrouped_first_round(genotypes, dest_group):
     num_groups = lax.axis_size("group")
     core = lax.axis_index("group") % 2
@@ -524,6 +561,7 @@
         genotypes,
         dest_group,
         [lambda o: (by_core(jnp.where(present(o, 2), 2, 3), jnp.where(present(o, 1), 1, 2)),)],
+        56,
     )
     cross_one = sent(cross, lambda chip: [(chip + 1, far(chip)), (chip, chip + 1)])
     cross_zero = sent(cross, lambda chip: [(chip, far(chip)), (chip + 1, chip + 1)])
@@ -537,6 +575,7 @@
             lambda o: (by_core(3, 2), by_core(1, 0)),
             lambda o: (by_core(3, 2), by_core(0, 1)),
         ],
+        16,
     )
     lent = sent(lent, lambda chip: [(chip, chip + 1), (chip + 1, chip)])
     near = sent(near, lambda chip: [(chip, chip + 1), (chip + 1, chip)])
@@ -546,20 +585,23 @@
     lower = sent(last, lambda chip: [(chip + 1, far(chip) + 1), (chip, chip)])
     passed = jnp.where(present(offsets, 2), cross_one, cross_zero)
     passed = sent(passed, lambda chip: [(chip, chip + 1), (chip + 1, chip)])
-    held = list(first_round(dest_group, (own, near, cross_one, cross_zero)))
-    upper, lower, held[1] = lax.optimization_barrier((upper, lower, held[1]))
-    return first_round(dest_group, (own, near, passed), (upper, lower), held)
+    low_zero, *held = first_round(dest_group, (own, near, cross_one, cross_zero))
+    low_zero, held[0] = lax.optimization_barrier((low_zero, held[0]))
+    low_zero = next_pair(low_zero, 0)
+    upper, lower, held[0] = lax.optimization_barrier((upper, lower, held[0]))
+    low_one, *held = first_round(dest_group, (own, near, passed), (upper, lower), held)
+    return (low_zero, next_pair(low_one, 1)), *held
 
 
 def body(genotypes, dest_group):
-    low_new, inverse, mix, top, low = regrouped_first_round(genotypes, dest_group)
+    low_next, inverse, mix, top, low = regrouped_first_round(genotypes, dest_group)
+    top = rotate_top(top, (low,), inverse, mix)
     for cycle_round in range(1, ROUNDS):
-        low_next = passed_along(low_new, "pair", 1)
-        top = rotate_top(top, low, inverse, mix)
-        low = low_next
-        low_new, inverse, mix = rotate_low(top, low)
-    low_next = passed_along(low_new, "pair", 1)
-    return place_low(low_next, rotate_top(top, low, inverse, mix, 2))
+        low_new, inverse, mix = rotate_low(top, low_next)
+        low, low_next = low_next, (passed_along(low_new, "pair", 1),)
+        if cycle_round < ROUNDS - 1:
+            top = rotate_top(top, low, inverse, mix)
+    return place_low(low_next[0], rotate_top(top, low, inverse, mix, 2))
 
 
 def solution(mesh):

time: 237 us -> 226 us (0.954)
  Pallas kernels: 80.9 us -> 66.4 us
    ppermute x0 -> x2, waiting for transfers between devices: none -> 26.5 us  [next_pair(): return lax.ppermute(array, ('group', 'pair'), hops)]
    ppermute x3 -> x2, waiting for transfers between devices: 73.5 us -> 52.9 us  [passed_along(): lax.ppermute(array, axis, [(i, (i + by) % size) for i in range(size)])]
    pallas_call x5, Pallas kernels: 49.3 us -> 36.6 us  [the longest x2 28.8 us: rotate_low(): pl.pallas_call(functools.partial(round_kernel, len(lows)), in_specs=[anyw...]
    ppermute x0 -> x2, starting transfers between devices: none -> 5.42 us  [next_pair(): return lax.ppermute(array, ('group', 'pair'), hops)]
    ppermute x7, waiting for transfers between devices: 59.1 us -> 53.8 us  [sent(): lax.ppermute(array, 'group', [hop for chip in range(0, num_groups, 2) for...]
    pallas_call x2, Pallas kernels: 23.6 us -> 19.4 us  [first_round(): pl.pallas_call(functools.partial(first_kernel, len(wholes), len(halves)),...]
    ppermute x3 -> x2, starting transfers between devices: 3.97 us -> 0.12 us  [passed_along(): lax.ppermute(array, axis, [(i, (i + by) % size) for i in range(size)])]
    unnamed x10 -> x8, local copies, waits for them, and re-layouts: 5.4 us -> 4.74 us
  transfers between devices with their start and end apart: 10 -> 11, of which waited for: 6 -> 6; matrix products, arithmetic and copies ran while one was open for 0% -> 1% of each run, Pallas kernels for 7% -> 14%
where the time goes in v5:
time: 226 us; the launch traced here: 225 us
  waiting for transfers between devices  133 us (59%)
  Pallas kernels  66.4 us (29%)
  starting transfers between devices  15.6 us (7%)
  local copies, waits for them, and re-layouts  5.41 us (2%)
  between operations  2.98 us (1%)
    ppermute x7, waiting for transfers between devices, sent(): lax.ppermute(array, 'group', [hop for chip in range(0, num_groups, 2) for...  53.8 us
    ppermute x2, waiting for transfers between devices, passed_along(): lax.ppermute(array, axis, [(i, (i + by) % size) for i in range(size)])  52.9 us
    pallas_call x2, Pallas kernels, rotate_low(): pl.pallas_call(functools.partial(round_kernel, len(lows)), in_specs=[anyw...  28.8 us
    ppermute x2, waiting for transfers between devices, next_pair(): return lax.ppermute(array, ('group', 'pair'), hops)  26.5 us
    pallas_call x2, Pallas kernels, first_round(): pl.pallas_call(functools.partial(first_kernel, len(wholes), len(halves)),...  19.4 us
    ppermute x7, starting transfers between devices, sent(): lax.ppermute(array, 'group', [hop for chip in range(0, num_groups, 2) for...  10 us
    pallas_call x2, Pallas kernels, picked(): pl.pallas_call(cast_kernel, grid_spec=pltpu.PrefetchScalarGridSpec(num_sc...  8.82 us
    pallas_call x3, Pallas kernels, rotate_top(): pl.pallas_call(functools.partial(top_kernel, len(lows)), in_specs=[anywhe...  7.87 us
  transfers between devices with their start and end apart: 11, of which 6 were waited for; matrix products, arithmetic and copies ran while one was open for 1% of the time, Pallas kernels for 14%

profile of v5, /device:TPU:1, one launch (start us, length us, event | category | flops | bytes accessed | tf_op | source)
XLA Modules:
  0.0 225.2 jit_solution(9981097760066363283)
XLA Ops:
  0.0 5.1 %pick_blocks.2 = bf16[4096,256]{1,0:T(8,128)(2,1)} custom-call(s32[64]{0:T(128)} %dest.7, s32[4096,512]{1,0:T(8,128)} %refs_3_), custom_call_target="tpu_custom_call" | custom-call | tf_op jit(solution)/shard_map/pick_blocks/pallas_call | solution.py:328
  5.1 2.2 collective-permute-start.3
  7.3 2.4 %collective-permute-start.2 = (bf16[4096,256]{1,0:T(8,128)(2,1)}, bf16[4096,256]{1,0:T(8,128)(2,1)}, u32[]{:S(2)}, u32[]{:S(2)}) collective-permute-start(bf16[4096,256]{1,0:T(8,128)(2,1)} %pick_blocks.2), channel_id=1, source_target_pairs={{8,16},{0,8},{24,0},{16,24},{9,17},{1,9},{25,1},{17,25},{10,18},{2... | collective-permute-start | bytes 6291464 | tf_op jit(solution)/shard_map/ppermute | solution.py:555
  9.7 3.4 %copy-done = s32[4096,512]{1,0:T(8,128)S(1)} copy-done((s32[4096,512]{1,0:T(8,128)S(1)}, s32[4096,512]{1,0:T(8,128)}, u32[]{:S(2)}) %copy-start) | copy-done | bytes 8388632
  13.0 3.8 %pick_blocks.3 = (bf16[4096,256]{1,0:T(8,128)(2,1)}, bf16[4096,256]{1,0:T(8,128)(2,1)S(1)}, bf16[2048,256]{1,0:T(8,128)(2,1)}, bf16[2048,256]{1,0:T(8,128)(2,1)S(1)}) custom-call(s32[64]{0:T(128)S(1)} %copy-done.1, s32[4096,512]{1,0:T(8,128)S(1)} %copy-done, s32[4096,512]{1,0:T(8,128)S(1)} %copy-done, s32[4096,512]{1,0:T(8,128)S(1)} %copy-done, ...), custom_call_target="tpu_custom_call" | custom-call | tf_op jit(solution)/shard_map/pick_blocks/pallas_call | solution.py:328
  16.8 1.4 copy-done.2
  22.0 1.4 broadcast_select_fusion.1
  23.4 31.6 %collective-permute-done.2.refs_2_ = bf16[4096,256]{1,0:T(8,128)(2,1)} collective-permute-done((bf16[4096,256]{1,0:T(8,128)(2,1)}, bf16[4096,256]{1,0:T(8,128)(2,1)}, u32[]{:S(2)}, u32[]{:S(2)}) %collective-permute-start.2) | collective-permute-done | bytes 2097184 | tf_op jit(solution)/shard_map/ppermute | solution.py:555
  55.4 1.8 collective-permute-start.4
  57.2 3.0 %collective-permute-start.6 = (bf16[2048,256]{1,0:T(8,128)(2,1)S(1)}, bf16[2048,256]{1,0:T(8,128)(2,1)S(1)}, u32[]{:S(2)}, u32[]{:S(2)}) collective-permute-start(bf16[2048,256]{1,0:T(8,128)(2,1)S(1)} %broadcast_select_fusion.1), channel_id=1, source_target_pairs={{8,24},{0,0},{24,8},{16,16},{9,25},{1,1},{25,9},{17,17},{10,26},{2... | collective-permute-start | bytes 3145736 | tf_op jit(solution)/shard_map/ppermute | solution.py:555
  61.0 0.8 collective-permute-start.7
  61.8 20.4 %collective-permute-done.6.refs_4_ = bf16[2048,256]{1,0:T(8,128)(2,1)S(1)} collective-permute-done((bf16[2048,256]{1,0:T(8,128)(2,1)S(1)}, bf16[2048,256]{1,0:T(8,128)(2,1)S(1)}, u32[]{:S(2)}, u32[]{:S(2)}) %collective-permute-start.6) | collective-permute-done | bytes 1048608 | tf_op jit(solution)/shard_map/ppermute | solution.py:555
  82.2 1.7 collective-permute-done.5.refs_3_
  84.0 18.7 %first_round.3 = (bf16[4096,256]{1,0:T(8,128)(2,1)S(1)}, bf16[256,256]{1,0:T(8,128)(2,1)S(1)}, bf16[256,256]{1,0:T(8,128)(2,1)S(1)}, bf16[4096,256]{1,0:T(8,128)(2,1)S(1)}, bf16[4096,256]{1,0:T(8,128)(2,1)S(1)}) custom-call(s32[64]{0:T(128)S(1)} %copy-done.1, ...), custom_call_target="tpu_custom_call", output_to_operand_aliasing={{1}: (6, {}), {2}: (7, {}), {3}: (8, {}), {4}: (9, {})} | custom-call | flops 10737418240 | bytes 16777216 | tf_op jit(solution)/shard_map/first_round/pallas_call | solution.py:423
  102.7 4.6 %collective-permute-start.8 = (bf16[4096,256]{1,0:T(8,128)(2,1)S(1)}, bf16[4096,256]{1,0:T(8,128)(2,1)S(1)}, u32[]{:S(2)}, u32[]{:S(2)}) collective-permute-start(bf16[4096,256]{1,0:T(8,128)(2,1)S(1)} %get-tuple-element.56), channel_id=1, source_target_pairs={{0,0},{1,1},{2,2},{3,3},{4,4},{5,5},{6,6},{7,7},{8,9},{9,10},{10,1... | collective-permute-start | bytes 6291464 | tf_op jit(solution)/shard_map/ppermute | solution.py:543
  107.3 2.3 %rotate_top.3.top_hbm = bf16[4096,256]{1,0:T(8,128)(2,1)S(1)} custom-call(bf16[4096,256]{1,0:T(8,128)(2,1)S(1)} %get-tuple-element.51.top_hbm, bf16[4096,256]{1,0:T(8,128)(2,1)S(1)} %get-tuple-element.52.refs_0_, bf16[256,256]{1,0:T(8,128)(2,1)S(1)} %get-tuple-element.53.refs_1_, bf16[256,256]{1,0:T(8,128)(2,1)S(1)} %get-tuple-element.54.refs_2_), custom_call_target="tpu_custom_call" | custom-call | flops 1073741824 | bytes 6291456 | tf_op jit(solution)/shard_map/rotate_top/pallas_call | solution.py:486
  109.7 26.5 %collective-permute-done.8.refs_1_ = bf16[4096,256]{1,0:T(8,128)(2,1)S(1)} collective-permute-done((bf16[4096,256]{1,0:T(8,128)(2,1)S(1)}, bf16[4096,256]{1,0:T(8,128)(2,1)S(1)}, u32[]{:S(2)}, u32[]{:S(2)}) %collective-permute-start.8) | collective-permute-done | bytes 2097184 | tf_op jit(solution)/shard_map/ppermute | solution.py:543
  136.2 14.4 %rotate_low.2 = (bf16[4096,256]{1,0:T(8,128)(2,1)S(1)}, bf16[256,256]{1,0:T(8,128)(2,1)S(1)}, bf16[256,256]{1,0:T(8,128)(2,1)S(1)}) custom-call(bf16[4096,256]{1,0:T(8,128)(2,1)S(1)} %rotate_top.3.top_hbm, bf16[4096,256]{1,0:T(8,128)(2,1)S(1)} %collective-permute-done.7.refs_0_, bf16[4096,256]{1,0:T(8,128)(2,1)S(1)} %collective-permute-done.8.refs_1_), custom_call_target="tpu_custom_call" | custom-call | flops 10737418240 | bytes 16777216 | tf_op jit(solution)/shard_map/rotate_low/pallas_call | solution.py:281
  150.6 2.4 %rotate_top.4.top_hbm = bf16[4096,256]{1,0:T(8,128)(2,1)S(1)} custom-call(bf16[4096,256]{1,0:T(8,128)(2,1)S(1)} %rotate_top.3.top_hbm, bf16[4096,256]{1,0:T(8,128)(2,1)S(1)} %collective-permute-done.7.refs_0_, bf16[4096,256]{1,0:T(8,128)(2,1)S(1)} %collective-permute-done.8.refs_1_, bf16[256,256]{1,0:T(8,128)(2,1)S(1)} %get-tuple-element.57.refs_2_, ...), custom_call_target="tpu_custom_call" | custom-call | flops 1073741824 | bytes 6291456 | tf_op jit(solution)/shard_map/rotate_top/pallas_call | solution.py:486
  153.0 27.3 %collective-permute-done.9.refs_0_ = bf16[4096,256]{1,0:T(8,128)(2,1)S(1)} collective-permute-done((bf16[4096,256]{1,0:T(8,128)(2,1)S(1)}, bf16[4096,256]{1,0:T(8,128)(2,1)S(1)}, u32[]{:S(2)}, u32[]{:S(2)}) %collective-permute-start.9) | collective-permute-done | bytes 2097184 | tf_op jit(solution)/shard_map/ppermute | solution.py:24
  180.3 14.4 %rotate_low.3 = (bf16[4096,256]{1,0:T(8,128)(2,1)S(1)}, bf16[256,256]{1,0:T(8,128)(2,1)S(1)}, bf16[256,256]{1,0:T(8,128)(2,1)S(1)}) custom-call(bf16[4096,256]{1,0:T(8,128)(2,1)S(1)} %rotate_top.4.top_hbm, bf16[4096,256]{1,0:T(8,128)(2,1)S(1)} %collective-permute-done.9.refs_0_), custom_call_target="tpu_custom_call" | custom-call | flops 10737418240 | bytes 16777216 | tf_op jit(solution)/shard_map/rotate_low/pallas_call | solution.py:281
  194.7 3.1 %rotate_top.5.held_ref = bf16[4096,512]{1,0:T(8,128)(2,1)} custom-call(bf16[4096,256]{1,0:T(8,128)(2,1)S(1)} %rotate_top.4.top_hbm, bf16[4096,256]{1,0:T(8,128)(2,1)S(1)} %collective-permute-done.9.refs_0_, bf16[256,256]{1,0:T(8,128)(2,1)S(1)} %get-tuple-element.61.refs_1_, bf16[256,256]{1,0:T(8,128)(2,1)S(1)} %get-tuple-element.62.refs_2_), custom_call_target="tpu_custom_call" | custom-call | flops 1073741824 | bytes 6291456 | tf_op jit(solution)/shard_map/rotate_top/pallas_call | solution.py:486
  197.9 25.6 %collective-permute-done.10.low_hbm = bf16[4096,256]{1,0:T(8,128)(2,1)S(1)} collective-permute-done((bf16[4096,256]{1,0:T(8,128)(2,1)S(1)}, bf16[4096,256]{1,0:T(8,128)(2,1)S(1)}, u32[]{:S(2)}, u32[]{:S(2)}) %collective-permute-start.10) | collective-permute-done | bytes 2097184 | tf_op jit(solution)/shard_map/ppermute | solution.py:24
  223.5 1.6 place_low.1
  (19 shorter events, 2.4 us)
Async XLA Ops:
  0.0 9.7 %copy-start.1 = (s32[64]{0:T(128)S(1)}, s32[64]{0:T(128)}, u32[]{:S(2)}) copy-start(s32[64]{0:T(128)} %dest.7) | copy-start | bytes 772
  5.1 18.3 %collective-permute-start.3 = (bf16[4096,256]{1,0:T(8,128)(2,1)}, bf16[4096,256]{1,0:T(8,128)(2,1)S(1)}, u32[]{:S(2)}, u32[]{:S(2)}) collective-permute-start(bf16[4096,256]{1,0:T(8,128)(2,1)} %pick_blocks.2), channel_id=1, source_target_pairs={{0,16},{8,8},{16,0},{24,24},{1,17},{9,9},{17,1},{25,25},{2,18},{10... | collective-permute-start | bytes 6291464 | tf_op jit(solution)/shard_map/ppermute | solution.py:555
  7.3 47.7 %collective-permute-start.2 = (bf16[4096,256]{1,0:T(8,128)(2,1)}, bf16[4096,256]{1,0:T(8,128)(2,1)}, u32[]{:S(2)}, u32[]{:S(2)}) collective-permute-start(bf16[4096,256]{1,0:T(8,128)(2,1)} %pick_blocks.2), channel_id=1, source_target_pairs={{8,16},{0,8},{24,0},{16,24},{9,17},{1,9},{25,1},{17,25},{10,18},{2... | collective-permute-start | bytes 6291464 | tf_op jit(solution)/shard_map/ppermute | solution.py:555
  9.7 3.4 %copy-start = (s32[4096,512]{1,0:T(8,128)S(1)}, s32[4096,512]{1,0:T(8,128)}, u32[]{:S(2)}) copy-start(s32[4096,512]{1,0:T(8,128)} %refs_3_) | copy-start | bytes 25165828
  16.8 1.4 copy-start.2
  18.2 3.8 %collective-permute-start.1 = (bf16[2048,256]{1,0:T(8,128)(2,1)}, bf16[2048,256]{1,0:T(8,128)(2,1)}, u32[]{:S(2)}, u32[]{:S(2)}) collective-permute-start(bf16[2048,256]{1,0:T(8,128)(2,1)} %get-tuple-element.38), channel_id=1, source_target_pairs={{0,8},{8,0},{16,24},{24,16},{1,9},{9,1},{17,25},{25,17},{2,10},{10... | collective-permute-start | bytes 3145736 | tf_op jit(solution)/shard_map/ppermute | solution.py:555
  18.6 41.7 %collective-permute-start = (bf16[4096,256]{1,0:T(8,128)(2,1)}, bf16[4096,256]{1,0:T(8,128)(2,1)}, u32[]{:S(2)}, u32[]{:S(2)}) collective-permute-start(bf16[4096,256]{1,0:T(8,128)(2,1)} %get-tuple-element.36), channel_id=1, source_target_pairs={{0,8},{8,0},{16,24},{24,16},{1,9},{9,1},{17,25},{25,17},{2,10},{10... | collective-permute-start | bytes 6291464 | tf_op jit(solution)/shard_map/ppermute | solution.py:555
  55.0 5.3 %copy-start.3 = (bf16[4096,256]{1,0:T(8,128)(2,1)S(1)}, bf16[4096,256]{1,0:T(8,128)(2,1)}, u32[]{:S(2)}) copy-start(bf16[4096,256]{1,0:T(8,128)(2,1)} %copy-done.2) | copy-start | bytes 6291460
  55.4 28.6 %collective-permute-start.4 = (bf16[4096,256]{1,0:T(8,128)(2,1)S(1)}, bf16[4096,256]{1,0:T(8,128)(2,1)S(1)}, u32[]{:S(2)}, u32[]{:S(2)}) collective-permute-start(bf16[4096,256]{1,0:T(8,128)(2,1)S(1)} %broadcast_select_fusion), channel_id=1, source_target_pairs={{0,8},{8,0},{16,24},{24,16},{1,9},{9,1},{17,25},{25,17},{2,10},{10... | collective-permute-start | bytes 6291464 | tf_op jit(solution)/shard_map/ppermute | solution.py:555
  57.2 25.0 %collective-permute-start.6 = (bf16[2048,256]{1,0:T(8,128)(2,1)S(1)}, bf16[2048,256]{1,0:T(8,128)(2,1)S(1)}, u32[]{:S(2)}, u32[]{:S(2)}) collective-permute-start(bf16[2048,256]{1,0:T(8,128)(2,1)S(1)} %broadcast_select_fusion.1), channel_id=1, source_target_pairs={{8,24},{0,0},{24,8},{16,16},{9,25},{1,1},{25,9},{17,17},{10,26},{2... | collective-permute-start | bytes 3145736 | tf_op jit(solution)/shard_map/ppermute | solution.py:555
  60.2 23.7 %collective-permute-start.5 = (bf16[2048,256]{1,0:T(8,128)(2,1)S(1)}, bf16[2048,256]{1,0:T(8,128)(2,1)S(1)}, u32[]{:S(2)}, u32[]{:S(2)}) collective-permute-start(bf16[2048,256]{1,0:T(8,128)(2,1)S(1)} %broadcast_select_fusion.1), channel_id=1, source_target_pairs={{0,24},{8,0},{16,8},{24,16},{1,25},{9,1},{17,9},{25,17},{2,26},{10... | collective-permute-start | bytes 3145736 | tf_op jit(solution)/shard_map/ppermute | solution.py:555
  61.0 48.7 %collective-permute-start.7 = (bf16[4096,256]{1,0:T(8,128)(2,1)S(1)}, bf16[4096,256]{1,0:T(8,128)(2,1)S(1)}, u32[]{:S(2)}, u32[]{:S(2)}) collective-permute-start(bf16[4096,256]{1,0:T(8,128)(2,1)S(1)} %get-tuple-element.55), channel_id=1, source_target_pairs={{0,1},{1,2},{2,3},{3,4},{4,5},{5,6},{6,7},{7,0},{8,8},{9,9},{10,10... | collective-permute-start | bytes 6291464 | tf_op jit(solution)/shard_map/ppermute | solution.py:543
  102.7 33.5 %collective-permute-start.8 = (bf16[4096,256]{1,0:T(8,128)(2,1)S(1)}, bf16[4096,256]{1,0:T(8,128)(2,1)S(1)}, u32[]{:S(2)}, u32[]{:S(2)}) collective-permute-start(bf16[4096,256]{1,0:T(8,128)(2,1)S(1)} %get-tuple-element.56), channel_id=1, source_target_pairs={{0,0},{1,1},{2,2},{3,3},{4,4},{5,5},{6,6},{7,7},{8,9},{9,10},{10,1... | collective-permute-start | bytes 6291464 | tf_op jit(solution)/shard_map/ppermute | solution.py:543
  150.6 29.7 %collective-permute-start.9 = (bf16[4096,256]{1,0:T(8,128)(2,1)S(1)}, bf16[4096,256]{1,0:T(8,128)(2,1)S(1)}, u32[]{:S(2)}, u32[]{:S(2)}) collective-permute-start(bf16[4096,256]{1,0:T(8,128)(2,1)S(1)} %get-tuple-element.59), channel_id=1, source_target_pairs={{0,1},{1,2},{2,3},{3,4},{4,5},{5,6},{6,7},{7,0},{8,9},{9,10},{10,1... | collective-permute-start | bytes 6291464 | tf_op jit(solution)/shard_map/ppermute | solution.py:24
  194.7 28.8 %collective-permute-start.10 = (bf16[4096,256]{1,0:T(8,128)(2,1)S(1)}, bf16[4096,256]{1,0:T(8,128)(2,1)S(1)}, u32[]{:S(2)}, u32[]{:S(2)}) collective-permute-start(bf16[4096,256]{1,0:T(8,128)(2,1)S(1)} %get-tuple-element.60), channel_id=1, source_target_pairs={{0,1},{1,2},{2,3},{3,4},{4,5},{5,6},{6,7},{7,0},{8,9},{9,10},{10,1... | collective-permute-start | bytes 6291464 | tf_op jit(solution)/shard_map/ppermute | solution.py:24

commit v6 on v5

--- a/solution.py
+++ b/solution.py
@@ -132,6 +132,7 @@
     row_column, _ = columns(PANEL)
     row_sub = lax.broadcasted_iota(jnp.int32, (PANEL, 2 * size), 0)
     part_column, part_first = columns(HALF)
+    part_sub = lax.broadcasted_iota(jnp.int32, (HALF, 2 * size), 0)
 
     def step(index, carry):
         start = pl.multiple_of(index * PANEL, PANEL)
@@ -141,15 +142,20 @@
         eye = (row_column - start == row_sub).astype(f32)
         within = (row_column >= start) & (row_column < stop)
         rows = eliminate(block, jnp.where(within, eye, gram[pl.ds(start, PANEL), :]))
-        right = split(rows)
-        left = [jnp.where(row_column >= stop, term, jnp.zeros_like(term)) for term in right]
-        change = dot16(stacked(left, LEFT, 0), stacked(right, RIGHT, 0), 0, 0)
-        for part in range(size // HALF):
-            at = part * LANES
-            own = jnp.where(part_first, change[at : at + HALF, :], change[at + HALF : at + LANES, :])
-            held = pl.ds(part * HALF, HALF)
-            gram[held, :] = jnp.where((part_column >= start) & (part_column < stop), 0.0, gram[held, :]) - own
         gram[pl.ds(start, PANEL), :] = rows
+
+        @pl.when(stop < size)
+        def _():
+            right = split(rows)
+            left = [jnp.where(row_column >= stop, term, jnp.zeros_like(term)) for term in right]
+            change = dot16(stacked(left, LEFT, 0), stacked(right, RIGHT, 0), 0, 0)
+            done = (part_column >= start) & (part_column < stop)
+            for part in range(size // HALF):
+                at = part * LANES
+                own = jnp.where(part_first, change[at : at + HALF, :], change[at + HALF : at + LANES, :])
+                held = pl.ds(part * HALF, HALF)
+                gram[held, :] = jnp.where(done & (part * HALF + part_sub >= stop), 0.0, gram[held, :]) - own
+
         return carry
 
     lax.fori_loop(0, size // PANEL, step, 0)
@@ -303,13 +309,60 @@
     return jnp.where(offsets[1] == value, 1, 0)
 
 
+def cross_kernel(dest, counts_hbm, out_hbm, counts_ref, cast_ref, sems):
+    indiv, size = cast_ref.shape
+    steps = indiv // PIECE
+    offsets = offsets_of(dest)
+    core = lax.axis_index("group") % 2
+    zero = jnp.where(present(offsets, 2), 2, 3)
+    one = jnp.where(present(offsets, 1), 1, 2)
+    column = pl.multiple_of(side_with(offsets, jnp.where(core == 0, zero, one)) * size, size)
+
+    def fetched(step):
+        rows = pl.ds(step * PIECE, PIECE)
+        return pltpu.make_async_copy(
+            counts_hbm.at[rows, pl.ds(column, size)], counts_ref.at[rows, :], sems.at[2 * step]
+        )
+
+    def sent(step):
+        rows = pl.ds(step * PIECE, PIECE)
+        return pltpu.make_async_copy(cast_ref.at[rows, :], out_hbm.at[rows, :], sems.at[2 * step + 1])
+
+    for step in range(steps):
+        fetched(step).start()
+    for step in range(steps):
+        rows = pl.ds(step * PIECE, PIECE)
+        fetched(step).wait()
+        cast_ref[rows, :] = counts_ref[rows, :].astype(cast_ref.dtype)
+        sent(step).start()
+    for step in range(steps):
+        sent(step).wait()
+
+
+def picked_cross(genotypes, dest):
+    indiv, size = genotypes.shape[0], genotypes.shape[1] // 2
+    return pl.pallas_call(
+        cross_kernel,
+        in_specs=[pl.BlockSpec(memory_space=pltpu.SMEM), pl.BlockSpec(memory_space=pl.ANY)],
+        out_specs=pl.BlockSpec(memory_space=pl.ANY),
+        out_shape=jax.ShapeDtypeStruct((indiv, size), jnp.bfloat16),
+        scratch_shapes=[
+            pltpu.VMEM((indiv, size), jnp.int32),
+            pltpu.VMEM((indiv, size), jnp.bfloat16),
+            pltpu.SemaphoreType.DMA((2 * (indiv // PIECE),)),
+        ],
+        compiler_params=pltpu.CompilerParams(vmem_limit_bytes=56 * 2**20),
+        name="pick_cross",
+    )(dest, genotypes)
+
+
 def cast_kernel(dest, *refs):
     count = len(refs) // 2
     for counts_ref, out_ref in zip(refs[:count], refs[count:]):
         out_ref[...] = counts_ref[...].astype(out_ref.dtype)
 
 
-def picked(genotypes, dest, wants, room):
+def picked(genotypes, dest, wants):
     indiv, size = genotypes.shape[0], genotypes.shape[1] // 2
     steps = 4
     in_specs, out_specs, shapes = [], [], []
@@ -331,7 +384,7 @@
             num_scalar_prefetch=1, grid=(steps,), in_specs=in_specs, out_specs=out_specs
         ),
         out_shape=shapes,
-        compiler_params=pltpu.CompilerParams(vmem_limit_bytes=room * 2**20),
+        compiler_params=pltpu.CompilerParams(vmem_limit_bytes=16 * 2**20),
         name="pick_blocks",
     )(dest, *[genotypes] * len(wants))
 
@@ -370,20 +423,24 @@
 
         cross_ref[...] = jnp.zeros_like(cross_ref)
         norm_ref[...] = jnp.zeros_like(norm_ref)
-        scales = []
         for side, target in enumerate((top_ref, low_ref)):
             for part in range(2):
                 rows = pl.ds(part * half, half)
                 pltpu.make_async_copy(sources[0].at[rows, :], target.at[rows, :], in_sems.at[2 * side + part]).wait()
 
-            def add(step, sums):
-                values = target[pl.ds(pl.multiple_of(step * PIECE, PIECE), PIECE), :].astype(f32)
-                return (
-                    sums[0] + jnp.sum(values, axis=0, keepdims=True),
-                    sums[1] + jnp.sum(values * values, axis=0, keepdims=True),
-                )
-
-            total, squares = lax.fori_loop(0, indiv // PIECE, add, (jnp.zeros((1, size), f32),) * 2)
+        def add(step, sums):
+            rows = pl.ds(pl.multiple_of(step * PIECE, PIECE), PIECE)
+            new = []
+            for side, target in enumerate((top_ref, low_ref)):
+                values = target[rows, :].astype(f32).reshape(PIECE // SUB, SUB, size)
+                new += [sums[2 * side] + jnp.sum(values, axis=0)]
+                new += [sums[2 * side + 1] + jnp.sum(values * values, axis=0)]
+            return tuple(new)
+
+        sums = lax.fori_loop(0, indiv // PIECE, add, (jnp.zeros((SUB, size), f32),) * 4)
+        sums = [jnp.sum(part, axis=0, keepdims=True) for part in sums]
+        scales = []
+        for total, squares in (sums[0:2], sums[2:4]):
             whole = total.astype(jnp.int32)
             spread = indiv * squares.astype(jnp.int32) - whole * whole
             variance = spread.astype(f32) * (1.0 / (indiv * indiv))
@@ -557,12 +614,7 @@
     def far(chip):
         return (chip + 2) % num_groups
 
-    (cross,) = picked(
-        genotypes,
-        dest_group,
-        [lambda o: (by_core(jnp.where(present(o, 2), 2, 3), jnp.where(present(o, 1), 1, 2)),)],
-        56,
-    )
+    cross = picked_cross(genotypes, dest_group)
     cross_one = sent(cross, lambda chip: [(chip + 1, far(chip)), (chip, chip + 1)])
     cross_zero = sent(cross, lambda chip: [(chip, far(chip)), (chip + 1, chip + 1)])
     table, _ = lax.optimization_barrier((genotypes, cross))
@@ -575,7 +627,6 @@
             lambda o: (by_core(3, 2), by_core(1, 0)),
             lambda o: (by_core(3, 2), by_core(0, 1)),
         ],
-        16,
     )
     lent = sent(lent, lambda chip: [(chip, chip + 1), (chip + 1, chip)])
     near = sent(near, lambda chip: [(chip, chip + 1), (chip + 1, chip)])

time: 226 us -> 224 us (level)
  starting transfers between devices: 15.6 us -> 21.2 us
  waiting for transfers between devices: 133 us -> 128 us
  Pallas kernels: 66.4 us -> 63.6 us
    pallas_call x2 -> x1, Pallas kernels: 8.82 us -> 3.76 us  [picked(): pl.pallas_call(cast_kernel, grid_spec=pltpu.PrefetchScalarGridSpec(num_sc...]
    ppermute x2, starting transfers between devices: 0.12 us -> 4.51 us  [passed_along(): lax.ppermute(array, axis, [(i, (i + by) % size) for i in range(size)])]
    ppermute x2, waiting for transfers between devices: 52.9 us -> 48.7 us  [passed_along(): lax.ppermute(array, axis, [(i, (i + by) % size) for i in range(size)])]
    pallas_call x0 -> x1, Pallas kernels: none -> 4.11 us  [picked_cross(): pl.pallas_call(cross_kernel, in_specs=[pl.BlockSpec(memory_space=pltpu.SM...]
where the time goes in v6:
time: 224 us; the launch traced here: 223 us
  waiting for transfers between devices  128 us (57%)
  Pallas kernels  63.6 us (28%)
  starting transfers between devices  21.2 us (9%)
  local copies, waits for them, and re-layouts  5.41 us (2%)
  between operations  2.97 us (1%)
    ppermute x7, waiting for transfers between devices, sent(): lax.ppermute(array, 'group', [hop for chip in range(0, num_groups, 2) for...  53.8 us
    ppermute x2, waiting for transfers between devices, passed_along(): lax.ppermute(array, axis, [(i, (i + by) % size) for i in range(size)])  48.7 us
    pallas_call x2, Pallas kernels, rotate_low(): pl.pallas_call(functools.partial(round_kernel, len(lows)), in_specs=[anyw...  27.8 us
    ppermute x2, waiting for transfers between devices, next_pair(): return lax.ppermute(array, ('group', 'pair'), hops)  25.5 us
    pallas_call x2, Pallas kernels, first_round(): pl.pallas_call(functools.partial(first_kernel, len(wholes), len(halves)),...  18.6 us
    ppermute x7, starting transfers between devices, sent(): lax.ppermute(array, 'group', [hop for chip in range(0, num_groups, 2) for...  10 us
    pallas_call x3, Pallas kernels, rotate_top(): pl.pallas_call(functools.partial(top_kernel, len(lows)), in_specs=[anywhe...  7.8 us
    ppermute x2, starting transfers between devices, next_pair(): return lax.ppermute(array, ('group', 'pair'), hops)  6.62 us
  transfers between devices with their start and end apart: 11, of which 6 were waited for; matrix products, arithmetic and copies ran while one was open for 1% of the time, Pallas kernels for 14%

profile of v6, /device:TPU:1, one launch (start us, length us, event | category | flops | bytes accessed | tf_op | source)
XLA Modules:
  0.0 222.9 jit_solution(13860497090148225034)
XLA Ops:
  0.0 4.1 %pick_cross.1 = bf16[4096,256]{1,0:T(8,128)(2,1)} custom-call(s32[64]{0:T(128)} %dest.7, s32[4096,512]{1,0:T(8,128)} %refs_3_), custom_call_target="tpu_custom_call" | custom-call | tf_op jit(solution)/shard_map/pick_cross/pallas_call | solution.py:344
  4.1 2.2 %collective-permute-start.3 = (bf16[4096,256]{1,0:T(8,128)(2,1)}, bf16[4096,256]{1,0:T(8,128)(2,1)S(1)}, u32[]{:S(2)}, u32[]{:S(2)}) collective-permute-start(bf16[4096,256]{1,0:T(8,128)(2,1)} %pick_cross.1), channel_id=1, source_target_pairs={{0,16},{8,8},{16,0},{24,24},{1,17},{9,9},{17,1},{25,25},{2,18},{10... | collective-permute-start | bytes 6291464 | tf_op jit(solution)/shard_map/ppermute | solution.py:612
  6.4 2.4 %collective-permute-start.2 = (bf16[4096,256]{1,0:T(8,128)(2,1)}, bf16[4096,256]{1,0:T(8,128)(2,1)}, u32[]{:S(2)}, u32[]{:S(2)}) collective-permute-start(bf16[4096,256]{1,0:T(8,128)(2,1)} %pick_cross.1), channel_id=1, source_target_pairs={{8,16},{0,8},{24,0},{16,24},{9,17},{1,9},{25,1},{17,25},{10,18},{2... | collective-permute-start | bytes 6291464 | tf_op jit(solution)/shard_map/ppermute | solution.py:612
  8.7 3.4 %copy-done = s32[4096,512]{1,0:T(8,128)S(1)} copy-done((s32[4096,512]{1,0:T(8,128)S(1)}, s32[4096,512]{1,0:T(8,128)}, u32[]{:S(2)}) %copy-start) | copy-done | bytes 8388632
  12.1 3.8 %pick_blocks.1 = (bf16[4096,256]{1,0:T(8,128)(2,1)}, bf16[4096,256]{1,0:T(8,128)(2,1)S(1)}, bf16[2048,256]{1,0:T(8,128)(2,1)}, bf16[2048,256]{1,0:T(8,128)(2,1)S(1)}) custom-call(s32[64]{0:T(128)S(1)} %copy-done.1, s32[4096,512]{1,0:T(8,128)S(1)} %copy-done, s32[4096,512]{1,0:T(8,128)S(1)} %copy-done, s32[4096,512]{1,0:T(8,128)S(1)} %copy-done, ...), custom_call_target="tpu_custom_call" | custom-call | tf_op jit(solution)/shard_map/pick_blocks/pallas_call | solution.py:381
  21.1 1.4 broadcast_select_fusion.1
  22.4 31.6 %collective-permute-done.2.refs_2_ = bf16[4096,256]{1,0:T(8,128)(2,1)} collective-permute-done((bf16[4096,256]{1,0:T(8,128)(2,1)}, bf16[4096,256]{1,0:T(8,128)(2,1)}, u32[]{:S(2)}, u32[]{:S(2)}) %collective-permute-start.2) | collective-permute-done | bytes 2097184 | tf_op jit(solution)/shard_map/ppermute | solution.py:612
  54.4 1.8 collective-permute-start.4
  56.3 3.0 %collective-permute-start.6 = (bf16[2048,256]{1,0:T(8,128)(2,1)S(1)}, bf16[2048,256]{1,0:T(8,128)(2,1)S(1)}, u32[]{:S(2)}, u32[]{:S(2)}) collective-permute-start(bf16[2048,256]{1,0:T(8,128)(2,1)S(1)} %broadcast_select_fusion.1), channel_id=1, source_target_pairs={{8,24},{0,0},{24,8},{16,16},{9,25},{1,1},{25,9},{17,17},{10,26},{2... | collective-permute-start | bytes 3145736 | tf_op jit(solution)/shard_map/ppermute | solution.py:612
  60.9 20.4 %collective-permute-done.6.refs_4_ = bf16[2048,256]{1,0:T(8,128)(2,1)S(1)} collective-permute-done((bf16[2048,256]{1,0:T(8,128)(2,1)S(1)}, bf16[2048,256]{1,0:T(8,128)(2,1)S(1)}, u32[]{:S(2)}, u32[]{:S(2)}) %collective-permute-start.6) | collective-permute-done | bytes 1048608 | tf_op jit(solution)/shard_map/ppermute | solution.py:612
  81.3 1.7 collective-permute-done.5.refs_3_
  83.0 17.9 %first_round.3 = (bf16[4096,256]{1,0:T(8,128)(2,1)S(1)}, bf16[256,256]{1,0:T(8,128)(2,1)S(1)}, bf16[256,256]{1,0:T(8,128)(2,1)S(1)}, bf16[4096,256]{1,0:T(8,128)(2,1)S(1)}, bf16[4096,256]{1,0:T(8,128)(2,1)S(1)}) custom-call(s32[64]{0:T(128)S(1)} %copy-done.1, ...), custom_call_target="tpu_custom_call", output_to_operand_aliasing={{1}: (6, {}), {2}: (7, {}), {3}: (8, {}), {4}: (9, {})} | custom-call | flops 10737418240 | bytes 16777216 | tf_op jit(solution)/shard_map/first_round/pallas_call | solution.py:480
  100.9 5.8 %collective-permute-start.8 = (bf16[4096,256]{1,0:T(8,128)(2,1)S(1)}, bf16[4096,256]{1,0:T(8,128)(2,1)S(1)}, u32[]{:S(2)}, u32[]{:S(2)}) collective-permute-start(bf16[4096,256]{1,0:T(8,128)(2,1)S(1)} %get-tuple-element.56), channel_id=1, source_target_pairs={{0,0},{1,1},{2,2},{3,3},{4,4},{5,5},{6,6},{7,7},{8,9},{9,10},{10,1... | collective-permute-start | bytes 6291464 | tf_op jit(solution)/shard_map/ppermute | solution.py:600
  106.7 2.3 %rotate_top.3.top_hbm = bf16[4096,256]{1,0:T(8,128)(2,1)S(1)} custom-call(bf16[4096,256]{1,0:T(8,128)(2,1)S(1)} %get-tuple-element.51.top_hbm, bf16[4096,256]{1,0:T(8,128)(2,1)S(1)} %get-tuple-element.52.refs_0_, bf16[256,256]{1,0:T(8,128)(2,1)S(1)} %get-tuple-element.53.refs_1_, bf16[256,256]{1,0:T(8,128)(2,1)S(1)} %get-tuple-element.54.refs_2_), custom_call_target="tpu_custom_call" | custom-call | flops 1073741824 | bytes 6291456 | tf_op jit(solution)/shard_map/rotate_top/pallas_call | solution.py:543
  109.1 25.5 %collective-permute-done.8.refs_1_ = bf16[4096,256]{1,0:T(8,128)(2,1)S(1)} collective-permute-done((bf16[4096,256]{1,0:T(8,128)(2,1)S(1)}, bf16[4096,256]{1,0:T(8,128)(2,1)S(1)}, u32[]{:S(2)}, u32[]{:S(2)}) %collective-permute-start.8) | collective-permute-done | bytes 2097184 | tf_op jit(solution)/shard_map/ppermute | solution.py:600
  134.6 13.9 %rotate_low.2 = (bf16[4096,256]{1,0:T(8,128)(2,1)S(1)}, bf16[256,256]{1,0:T(8,128)(2,1)S(1)}, bf16[256,256]{1,0:T(8,128)(2,1)S(1)}) custom-call(bf16[4096,256]{1,0:T(8,128)(2,1)S(1)} %rotate_top.3.top_hbm, bf16[4096,256]{1,0:T(8,128)(2,1)S(1)} %collective-permute-done.7.refs_0_, bf16[4096,256]{1,0:T(8,128)(2,1)S(1)} %collective-permute-done.8.refs_1_), custom_call_target="tpu_custom_call" | custom-call | flops 10737418240 | bytes 16777216 | tf_op jit(solution)/shard_map/rotate_low/pallas_call | solution.py:287
  148.6 2.3 %collective-permute-start.9 = (bf16[4096,256]{1,0:T(8,128)(2,1)S(1)}, bf16[4096,256]{1,0:T(8,128)(2,1)S(1)}, u32[]{:S(2)}, u32[]{:S(2)}) collective-permute-start(bf16[4096,256]{1,0:T(8,128)(2,1)S(1)} %get-tuple-element.59), channel_id=1, source_target_pairs={{0,1},{1,2},{2,3},{3,4},{4,5},{5,6},{6,7},{7,0},{8,9},{9,10},{10,1... | collective-permute-start | bytes 6291464 | tf_op jit(solution)/shard_map/ppermute | solution.py:24
  150.8 2.3 %rotate_top.4.top_hbm = bf16[4096,256]{1,0:T(8,128)(2,1)S(1)} custom-call(bf16[4096,256]{1,0:T(8,128)(2,1)S(1)} %rotate_top.3.top_hbm, bf16[4096,256]{1,0:T(8,128)(2,1)S(1)} %collective-permute-done.7.refs_0_, bf16[4096,256]{1,0:T(8,128)(2,1)S(1)} %collective-permute-done.8.refs_1_, bf16[256,256]{1,0:T(8,128)(2,1)S(1)} %get-tuple-element.57.refs_2_, ...), custom_call_target="tpu_custom_call" | custom-call | flops 1073741824 | bytes 6291456 | tf_op jit(solution)/shard_map/rotate_top/pallas_call | solution.py:543
  153.2 25.6 %collective-permute-done.9.refs_0_ = bf16[4096,256]{1,0:T(8,128)(2,1)S(1)} collective-permute-done((bf16[4096,256]{1,0:T(8,128)(2,1)S(1)}, bf16[4096,256]{1,0:T(8,128)(2,1)S(1)}, u32[]{:S(2)}, u32[]{:S(2)}) %collective-permute-start.9) | collective-permute-done | bytes 2097184 | tf_op jit(solution)/shard_map/ppermute | solution.py:24
  178.8 13.9 %rotate_low.3 = (bf16[4096,256]{1,0:T(8,128)(2,1)S(1)}, bf16[256,256]{1,0:T(8,128)(2,1)S(1)}, bf16[256,256]{1,0:T(8,128)(2,1)S(1)}) custom-call(bf16[4096,256]{1,0:T(8,128)(2,1)S(1)} %rotate_top.4.top_hbm, bf16[4096,256]{1,0:T(8,128)(2,1)S(1)} %collective-permute-done.9.refs_0_), custom_call_target="tpu_custom_call" | custom-call | flops 10737418240 | bytes 16777216 | tf_op jit(solution)/shard_map/rotate_low/pallas_call | solution.py:287
  192.7 2.2 %collective-permute-start.10 = (bf16[4096,256]{1,0:T(8,128)(2,1)S(1)}, bf16[4096,256]{1,0:T(8,128)(2,1)S(1)}, u32[]{:S(2)}, u32[]{:S(2)}) collective-permute-start(bf16[4096,256]{1,0:T(8,128)(2,1)S(1)} %get-tuple-element.60), channel_id=1, source_target_pairs={{0,1},{1,2},{2,3},{3,4},{4,5},{5,6},{6,7},{7,0},{8,9},{9,10},{10,1... | collective-permute-start | bytes 6291464 | tf_op jit(solution)/shard_map/ppermute | solution.py:24
  194.9 3.1 %rotate_top.5.held_ref = bf16[4096,512]{1,0:T(8,128)(2,1)} custom-call(bf16[4096,256]{1,0:T(8,128)(2,1)S(1)} %rotate_top.4.top_hbm, bf16[4096,256]{1,0:T(8,128)(2,1)S(1)} %collective-permute-done.9.refs_0_, bf16[256,256]{1,0:T(8,128)(2,1)S(1)} %get-tuple-element.61.refs_1_, bf16[256,256]{1,0:T(8,128)(2,1)S(1)} %get-tuple-element.62.refs_2_), custom_call_target="tpu_custom_call" | custom-call | flops 1073741824 | bytes 6291456 | tf_op jit(solution)/shard_map/rotate_top/pallas_call | solution.py:543
  198.0 23.1 %collective-permute-done.10.low_hbm = bf16[4096,256]{1,0:T(8,128)(2,1)S(1)} collective-permute-done((bf16[4096,256]{1,0:T(8,128)(2,1)S(1)}, bf16[4096,256]{1,0:T(8,128)(2,1)S(1)}, u32[]{:S(2)}, u32[]{:S(2)}) %collective-permute-start.10) | collective-permute-done | bytes 2097184 | tf_op jit(solution)/shard_map/ppermute | solution.py:24
  221.1 1.6 place_low.1
  (19 shorter events, 4.4 us)
Async XLA Ops:
  0.0 8.7 %copy-start.1 = (s32[64]{0:T(128)S(1)}, s32[64]{0:T(128)}, u32[]{:S(2)}) copy-start(s32[64]{0:T(128)} %dest.7) | copy-start | bytes 772
  4.1 18.3 %collective-permute-start.3 = (bf16[4096,256]{1,0:T(8,128)(2,1)}, bf16[4096,256]{1,0:T(8,128)(2,1)S(1)}, u32[]{:S(2)}, u32[]{:S(2)}) collective-permute-start(bf16[4096,256]{1,0:T(8,128)(2,1)} %pick_cross.1), channel_id=1, source_target_pairs={{0,16},{8,8},{16,0},{24,24},{1,17},{9,9},{17,1},{25,25},{2,18},{10... | collective-permute-start | bytes 6291464 | tf_op jit(solution)/shard_map/ppermute | solution.py:612
  6.4 47.7 %collective-permute-start.2 = (bf16[4096,256]{1,0:T(8,128)(2,1)}, bf16[4096,256]{1,0:T(8,128)(2,1)}, u32[]{:S(2)}, u32[]{:S(2)}) collective-permute-start(bf16[4096,256]{1,0:T(8,128)(2,1)} %pick_cross.1), channel_id=1, source_target_pairs={{8,16},{0,8},{24,0},{16,24},{9,17},{1,9},{25,1},{17,25},{10,18},{2... | collective-permute-start | bytes 6291464 | tf_op jit(solution)/shard_map/ppermute | solution.py:612
  8.7 3.4 %copy-start = (s32[4096,512]{1,0:T(8,128)S(1)}, s32[4096,512]{1,0:T(8,128)}, u32[]{:S(2)}) copy-start(s32[4096,512]{1,0:T(8,128)} %refs_3_) | copy-start | bytes 25165828
  15.9 1.4 copy-start.2
  17.2 3.8 %collective-permute-start.1 = (bf16[2048,256]{1,0:T(8,128)(2,1)}, bf16[2048,256]{1,0:T(8,128)(2,1)}, u32[]{:S(2)}, u32[]{:S(2)}) collective-permute-start(bf16[2048,256]{1,0:T(8,128)(2,1)} %get-tuple-element.38), channel_id=1, source_target_pairs={{0,8},{8,0},{16,24},{24,16},{1,9},{9,1},{17,25},{25,17},{2,10},{10... | collective-permute-start | bytes 3145736 | tf_op jit(solution)/shard_map/ppermute | solution.py:612
  17.6 41.7 %collective-permute-start = (bf16[4096,256]{1,0:T(8,128)(2,1)}, bf16[4096,256]{1,0:T(8,128)(2,1)}, u32[]{:S(2)}, u32[]{:S(2)}) collective-permute-start(bf16[4096,256]{1,0:T(8,128)(2,1)} %get-tuple-element.36), channel_id=1, source_target_pairs={{0,8},{8,0},{16,24},{24,16},{1,9},{9,1},{17,25},{25,17},{2,10},{10... | collective-permute-start | bytes 6291464 | tf_op jit(solution)/shard_map/ppermute | solution.py:612
  54.1 5.3 %copy-start.3 = (bf16[4096,256]{1,0:T(8,128)(2,1)S(1)}, bf16[4096,256]{1,0:T(8,128)(2,1)}, u32[]{:S(2)}) copy-start(bf16[4096,256]{1,0:T(8,128)(2,1)} %copy-done.2) | copy-start | bytes 6291460
  54.4 28.6 %collective-permute-start.4 = (bf16[4096,256]{1,0:T(8,128)(2,1)S(1)}, bf16[4096,256]{1,0:T(8,128)(2,1)S(1)}, u32[]{:S(2)}, u32[]{:S(2)}) collective-permute-start(bf16[4096,256]{1,0:T(8,128)(2,1)S(1)} %broadcast_select_fusion), channel_id=1, source_target_pairs={{0,8},{8,0},{16,24},{24,16},{1,9},{9,1},{17,25},{25,17},{2,10},{10... | collective-permute-start | bytes 6291464 | tf_op jit(solution)/shard_map/ppermute | solution.py:612
  56.3 25.0 %collective-permute-start.6 = (bf16[2048,256]{1,0:T(8,128)(2,1)S(1)}, bf16[2048,256]{1,0:T(8,128)(2,1)S(1)}, u32[]{:S(2)}, u32[]{:S(2)}) collective-permute-start(bf16[2048,256]{1,0:T(8,128)(2,1)S(1)} %broadcast_select_fusion.1), channel_id=1, source_target_pairs={{8,24},{0,0},{24,8},{16,16},{9,25},{1,1},{25,9},{17,17},{10,26},{2... | collective-permute-start | bytes 3145736 | tf_op jit(solution)/shard_map/ppermute | solution.py:612
  59.3 23.7 %collective-permute-start.5 = (bf16[2048,256]{1,0:T(8,128)(2,1)S(1)}, bf16[2048,256]{1,0:T(8,128)(2,1)S(1)}, u32[]{:S(2)}, u32[]{:S(2)}) collective-permute-start(bf16[2048,256]{1,0:T(8,128)(2,1)S(1)} %broadcast_select_fusion.1), channel_id=1, source_target_pairs={{0,24},{8,0},{16,8},{24,16},{1,25},{9,1},{17,9},{25,17},{2,26},{10... | collective-permute-start | bytes 3145736 | tf_op jit(solution)/shard_map/ppermute | solution.py:612
  60.1 49.0 %collective-permute-start.7 = (bf16[4096,256]{1,0:T(8,128)(2,1)S(1)}, bf16[4096,256]{1,0:T(8,128)(2,1)S(1)}, u32[]{:S(2)}, u32[]{:S(2)}) collective-permute-start(bf16[4096,256]{1,0:T(8,128)(2,1)S(1)} %get-tuple-element.55), channel_id=1, source_target_pairs={{0,1},{1,2},{2,3},{3,4},{4,5},{5,6},{6,7},{7,0},{8,8},{9,9},{10,10... | collective-permute-start | bytes 6291464 | tf_op jit(solution)/shard_map/ppermute | solution.py:600
  100.9 33.7 %collective-permute-start.8 = (bf16[4096,256]{1,0:T(8,128)(2,1)S(1)}, bf16[4096,256]{1,0:T(8,128)(2,1)S(1)}, u32[]{:S(2)}, u32[]{:S(2)}) collective-permute-start(bf16[4096,256]{1,0:T(8,128)(2,1)S(1)} %get-tuple-element.56), channel_id=1, source_target_pairs={{0,0},{1,1},{2,2},{3,3},{4,4},{5,5},{6,6},{7,7},{8,9},{9,10},{10,1... | collective-permute-start | bytes 6291464 | tf_op jit(solution)/shard_map/ppermute | solution.py:600
  148.6 30.2 %collective-permute-start.9 = (bf16[4096,256]{1,0:T(8,128)(2,1)S(1)}, bf16[4096,256]{1,0:T(8,128)(2,1)S(1)}, u32[]{:S(2)}, u32[]{:S(2)}) collective-permute-start(bf16[4096,256]{1,0:T(8,128)(2,1)S(1)} %get-tuple-element.59), channel_id=1, source_target_pairs={{0,1},{1,2},{2,3},{3,4},{4,5},{5,6},{6,7},{7,0},{8,9},{9,10},{10,1... | collective-permute-start | bytes 6291464 | tf_op jit(solution)/shard_map/ppermute | solution.py:24
  192.7 28.5 %collective-permute-start.10 = (bf16[4096,256]{1,0:T(8,128)(2,1)S(1)}, bf16[4096,256]{1,0:T(8,128)(2,1)S(1)}, u32[]{:S(2)}, u32[]{:S(2)}) collective-permute-start(bf16[4096,256]{1,0:T(8,128)(2,1)S(1)} %get-tuple-element.60), channel_id=1, source_target_pairs={{0,1},{1,2},{2,3},{3,4},{4,5},{5,6},{6,7},{7,0},{8,9},{9,10},{10,1... | collective-permute-start | bytes 6291464 | tf_op jit(solution)/shard_map/ppermute | solution.py:24

commit v7 on v6

--- a/solution.py
+++ b/solution.py
@@ -14,6 +14,8 @@
 HALF = LANES // 2
 CHUNK = 2048
 PIECE = 512
+TALL = 16
+GROUP = 32
 
 epsilon = 1e-05
 f32 = jnp.float32
@@ -389,33 +391,32 @@
     )(dest, *[genotypes] * len(wants))
 
 
-def first_kernel(wholes, halves, dest, *refs):
-    sources = refs[: wholes + halves]
-    held = 4 if halves else 0
-    low_out, inv_out, mix_out, top_scaled, low_scaled = refs[wholes + halves + held : wholes + halves + held + 5]
-    top_ref, low_ref, cross_ref, norm_ref, *rest = refs[wholes + halves + held + 5 :]
+def first_kernel(kinds, late, dest, *refs):
+    sources = [refs[sum(kinds[:code]) : sum(kinds[: code + 1])] for code in range(len(kinds))]
+    inputs = sum(kinds) + (4 if late else 0)
+    low_out, inv_out, mix_out, top_scaled, low_scaled = refs[inputs : inputs + 5]
+    top_ref, low_ref, cross_ref, norm_ref, *rest = refs[inputs + 5 :]
     *scratch, sems, in_sems = rest
     indiv, size = top_ref.shape
     half = indiv // 2
     count = indiv // CHUNK
 
     offsets = offsets_of(dest)
-    if halves:
-        two = jnp.where(present(offsets, 1), wholes, 2)
-        codes = (0, 1, two, jnp.where(present(offsets, 2), wholes, 2))
+    if late:
+        codes = (0, 1, jnp.where(present(offsets, 1), 3, 2), jnp.where(present(offsets, 2), 3, 2))
     else:
         codes = (0, 2, 3, 1)
 
-    @pl.when(lax.axis_index("group") % 2 == (1 if halves else 0))
+    @pl.when(lax.axis_index("group") % 2 == (1 if late else 0))
     def _():
         for side, target in enumerate((top_ref, low_ref)):
             chosen = jnp.int32(codes[0])
             for offset in range(1, 4):
                 chosen = jnp.where(offsets[side] == offset, codes[offset], chosen)
-            for code in range(wholes + halves // 2):
+            for code, arrays in enumerate(sources):
                 for part in range(2):
                     rows = pl.ds(part * half, half)
-                    source = sources[code].at[rows, :] if code < wholes else sources[wholes + part]
+                    source = arrays[part] if len(arrays) == 2 else arrays[0].at[rows, :]
 
                     @pl.when(chosen == code)
                     def _():
@@ -426,18 +427,21 @@
         for side, target in enumerate((top_ref, low_ref)):
             for part in range(2):
                 rows = pl.ds(part * half, half)
-                pltpu.make_async_copy(sources[0].at[rows, :], target.at[rows, :], in_sems.at[2 * side + part]).wait()
+                pltpu.make_async_copy(sources[0][0].at[rows, :], target.at[rows, :], in_sems.at[2 * side + part]).wait()
 
         def add(step, sums):
             rows = pl.ds(pl.multiple_of(step * PIECE, PIECE), PIECE)
             new = []
             for side, target in enumerate((top_ref, low_ref)):
-                values = target[rows, :].astype(f32).reshape(PIECE // SUB, SUB, size)
-                new += [sums[2 * side] + jnp.sum(values, axis=0)]
-                new += [sums[2 * side + 1] + jnp.sum(values * values, axis=0)]
+                values = target[rows, :].reshape(PIECE // (GROUP * TALL), GROUP, TALL, size)
+                for k, terms in enumerate((values, values * values)):
+                    small = terms[:, 0]
+                    for i in range(1, GROUP):
+                        small = small + terms[:, i]
+                    new.append(sums[2 * side + k] + jnp.sum(small.astype(f32), axis=0))
             return tuple(new)
 
-        sums = lax.fori_loop(0, indiv // PIECE, add, (jnp.zeros((SUB, size), f32),) * 4)
+        sums = lax.fori_loop(0, indiv // PIECE, add, (jnp.zeros((TALL, size), f32),) * 4)
         sums = [jnp.sum(part, axis=0, keepdims=True) for part in sums]
         scales = []
         for total, squares in (sums[0:2], sums[2:4]):
@@ -469,16 +473,16 @@
                 copy.wait()
 
 
-def first_round(dest, wholes, halves=(), held=()):
-    indiv, size = wholes[0].shape
-    sources = tuple(wholes) + tuple(halves)
+def first_round(dest, arrays, held=()):
+    indiv, size = arrays[0][0].shape
+    sources = [array for source in arrays for array in source]
     block = jax.ShapeDtypeStruct((indiv, size), jnp.bfloat16)
     square = jax.ShapeDtypeStruct((size, size), jnp.bfloat16)
     anywhere = pl.BlockSpec(memory_space=pl.ANY)
     scratch = scratch_of(indiv, size)
     scratch[-1] = pltpu.SemaphoreType.DMA((2 * (indiv // CHUNK) + 4,))
     return pl.pallas_call(
-        functools.partial(first_kernel, len(wholes), len(halves)),
+        functools.partial(first_kernel, tuple(len(source) for source in arrays), bool(held)),
         in_specs=[pl.BlockSpec(memory_space=pltpu.SMEM)] + [anywhere] * (len(sources) + len(held)),
         out_specs=[anywhere] * 5,
         out_shape=[block, square, square, block, block],
@@ -634,13 +638,15 @@
     last, cross_one, cross_zero = lax.optimization_barrier((last, cross_one, cross_zero))
     upper = sent(last, lambda chip: [(chip, far(chip) + 1), (chip + 1, chip)])
     lower = sent(last, lambda chip: [(chip + 1, far(chip) + 1), (chip, chip)])
-    passed = jnp.where(present(offsets, 2), cross_one, cross_zero)
-    passed = sent(passed, lambda chip: [(chip, chip + 1), (chip + 1, chip)])
-    low_zero, *held = first_round(dest_group, (own, near, cross_one, cross_zero))
+    half = cross.shape[0] // 2
+    passed = lax.optimization_barrier(jnp.where(present(offsets, 2), cross_one, cross_zero))
+    passed = [passed[:half], passed[half:]]
+    passed = [sent(part, lambda chip: [(chip, chip + 1), (chip + 1, chip)]) for part in passed]
+    low_zero, *held = first_round(dest_group, ((own,), (near,), (cross_one,), (cross_zero,)))
     low_zero, held[0] = lax.optimization_barrier((low_zero, held[0]))
     low_zero = next_pair(low_zero, 0)
     upper, lower, held[0] = lax.optimization_barrier((upper, lower, held[0]))
-    low_one, *held = first_round(dest_group, (own, near, passed), (upper, lower), held)
+    low_one, *held = first_round(dest_group, ((own,), (near,), passed, (upper, lower)), held)
     return (low_zero, next_pair(low_one, 1)), *held
 
 

time: 224 us -> 225 us (level)
  waiting for transfers between devices: 128 us -> 137 us
  starting transfers between devices: 21.2 us -> 14.8 us
    ppermute x2, waiting for transfers between devices: 48.7 us -> 57.7 us  [passed_along(): lax.ppermute(array, axis, [(i, (i + by) % size) for i in range(size)])]
    ppermute x2, starting transfers between devices: 4.51 us -> 0.94 us  [passed_along(): lax.ppermute(array, axis, [(i, (i + by) % size) for i in range(size)])]
    ppermute x7 -> x8, waiting for transfers between devices: 53.8 us -> 52.7 us  [sent(): lax.ppermute(array, 'group', [hop for chip in range(0, num_groups, 2) for...]
    ppermute x7 -> x8, starting transfers between devices: 10 us -> 9.05 us  [sent(): lax.ppermute(array, 'group', [hop for chip in range(0, num_groups, 2) for...]
  transfers between devices with their start and end apart: 11 -> 12, of which waited for: 6 -> 6; matrix products, arithmetic and copies ran while one was open for 1% -> 1% of each run, Pallas kernels for 14% -> 13%
where the time goes in v7:
time: 225 us
  waiting for transfers between devices  137 us (61%)
  Pallas kernels  62.5 us (28%)
  starting transfers between devices  14.8 us (7%)
  local copies, waits for them, and re-layouts  5.6 us (2%)
  between operations  2.71 us (1%)
    ppermute x2, waiting for transfers between devices, passed_along(): lax.ppermute(array, axis, [(i, (i + by) % size) for i in range(size)])  57.7 us
    ppermute x8, waiting for transfers between devices, sent(): lax.ppermute(array, 'group', [hop for chip in range(0, num_groups, 2) for...  52.7 us
    pallas_call x2, Pallas kernels, rotate_low(): pl.pallas_call(functools.partial(round_kernel, len(lows)), in_specs=[anyw...  27.8 us
    ppermute x2, waiting for transfers between devices, next_pair(): return lax.ppermute(array, ('group', 'pair'), hops)  26.9 us
    pallas_call x2, Pallas kernels, first_round(): pl.pallas_call(functools.partial(first_kernel, tuple((len(source) for sou...  17.4 us
    ppermute x8, starting transfers between devices, sent(): lax.ppermute(array, 'group', [hop for chip in range(0, num_groups, 2) for...  9.05 us
    pallas_call x3, Pallas kernels, rotate_top(): pl.pallas_call(functools.partial(top_kernel, len(lows)), in_specs=[anywhe...  7.82 us
    ppermute x2, starting transfers between devices, next_pair(): return lax.ppermute(array, ('group', 'pair'), hops)  4.82 us
  transfers between devices with their start and end apart: 12, of which 6 were waited for; matrix products, arithmetic and copies ran while one was open for 1% of the time, Pallas kernels for 13%

profile of v7, /device:TPU:1, one launch (start us, length us, event | category | flops | bytes accessed | tf_op | source)
XLA Modules:
  0.0 224.6 jit_solution(17919379608081069315)
XLA Ops:
  0.0 4.1 %pick_cross.1 = bf16[4096,256]{1,0:T(8,128)(2,1)} custom-call(s32[64]{0:T(128)} %dest.7, s32[4096,512]{1,0:T(8,128)} %refs_3_), custom_call_target="tpu_custom_call" | custom-call | tf_op jit(solution)/shard_map/pick_cross/pallas_call | solution.py:346
  4.1 2.2 %collective-permute-start.3 = (bf16[4096,256]{1,0:T(8,128)(2,1)}, bf16[4096,256]{1,0:T(8,128)(2,1)S(1)}, u32[]{:S(2)}, u32[]{:S(2)}) collective-permute-start(bf16[4096,256]{1,0:T(8,128)(2,1)} %pick_cross.1), channel_id=1, source_target_pairs={{0,16},{8,8},{16,0},{24,24},{1,17},{9,9},{17,1},{25,25},{2,18},{10... | collective-permute-start | bytes 6291464 | tf_op jit(solution)/shard_map/ppermute | solution.py:616
  6.4 2.4 %collective-permute-start.2 = (bf16[4096,256]{1,0:T(8,128)(2,1)}, bf16[4096,256]{1,0:T(8,128)(2,1)}, u32[]{:S(2)}, u32[]{:S(2)}) collective-permute-start(bf16[4096,256]{1,0:T(8,128)(2,1)} %pick_cross.1), channel_id=1, source_target_pairs={{8,16},{0,8},{24,0},{16,24},{9,17},{1,9},{25,1},{17,25},{10,18},{2... | collective-permute-start | bytes 6291464 | tf_op jit(solution)/shard_map/ppermute | solution.py:616
  8.7 3.4 %copy-done = s32[4096,512]{1,0:T(8,128)S(1)} copy-done((s32[4096,512]{1,0:T(8,128)S(1)}, s32[4096,512]{1,0:T(8,128)}, u32[]{:S(2)}) %copy-start) | copy-done | bytes 8388632
  12.1 3.8 %pick_blocks.1 = (bf16[4096,256]{1,0:T(8,128)(2,1)}, bf16[4096,256]{1,0:T(8,128)(2,1)S(1)}, bf16[2048,256]{1,0:T(8,128)(2,1)}, bf16[2048,256]{1,0:T(8,128)(2,1)S(1)}) custom-call(s32[64]{0:T(128)S(1)} %copy-done.1, s32[4096,512]{1,0:T(8,128)S(1)} %copy-done, s32[4096,512]{1,0:T(8,128)S(1)} %copy-done, s32[4096,512]{1,0:T(8,128)S(1)} %copy-done, ...), custom_call_target="tpu_custom_call" | custom-call | tf_op jit(solution)/shard_map/pick_blocks/pallas_call | solution.py:383
  15.9 1.3 copy-done.2
  20.8 1.4 broadcast_select_fusion.1
  22.1 32.0 %collective-permute-done.2.refs_2_ = bf16[4096,256]{1,0:T(8,128)(2,1)} collective-permute-done((bf16[4096,256]{1,0:T(8,128)(2,1)}, bf16[4096,256]{1,0:T(8,128)(2,1)}, u32[]{:S(2)}, u32[]{:S(2)}) %collective-permute-start.2) | collective-permute-done | bytes 2097184 | tf_op jit(solution)/shard_map/ppermute | solution.py:616
  54.1 2.5 %collective-permute-start.7 = (bf16[2048,256]{1,0:T(8,128)(2,1)S(1)}, bf16[2048,256]{1,0:T(8,128)(2,1)S(1)}, u32[]{:S(2)}, u32[]{:S(2)}) collective-permute-start(bf16[2048,256]{1,0:T(8,128)(2,1)S(1)} %broadcast_select_fusion.1), channel_id=1, source_target_pairs={{8,24},{0,0},{24,8},{16,16},{9,25},{1,1},{25,9},{17,17},{10,26},{2... | collective-permute-start | bytes 3145736 | tf_op jit(solution)/shard_map/ppermute | solution.py:616
  57.2 1.3 collective-permute-start.5
  60.1 19.4 %collective-permute-done.7.refs_5_ = bf16[2048,256]{1,0:T(8,128)(2,1)S(1)} collective-permute-done((bf16[2048,256]{1,0:T(8,128)(2,1)S(1)}, bf16[2048,256]{1,0:T(8,128)(2,1)S(1)}, u32[]{:S(2)}, u32[]{:S(2)}) %collective-permute-start.7) | collective-permute-done | bytes 1048608 | tf_op jit(solution)/shard_map/ppermute | solution.py:616
  79.5 1.3 collective-permute-done.6.refs_4_
  80.9 16.7 %first_round.3 = (bf16[4096,256]{1,0:T(8,128)(2,1)S(1)}, bf16[256,256]{1,0:T(8,128)(2,1)S(1)}, bf16[256,256]{1,0:T(8,128)(2,1)S(1)}, bf16[4096,256]{1,0:T(8,128)(2,1)S(1)}, bf16[4096,256]{1,0:T(8,128)(2,1)S(1)}) custom-call(s32[64]{0:T(128)S(1)} %copy-done.1, ...), custom_call_target="tpu_custom_call", output_to_operand_aliasing={{1}: (7, {}), {2}: (8, {}), {3}: (9, {}), {4}: (10, {})} | custom-call | flops 10737418240 | bytes 16777216 | tf_op jit(solution)/shard_map/first_round/pallas_call | solution.py:484
  97.6 4.0 %collective-permute-start.9 = (bf16[4096,256]{1,0:T(8,128)(2,1)S(1)}, bf16[4096,256]{1,0:T(8,128)(2,1)S(1)}, u32[]{:S(2)}, u32[]{:S(2)}) collective-permute-start(bf16[4096,256]{1,0:T(8,128)(2,1)S(1)} %get-tuple-element.56), channel_id=1, source_target_pairs={{0,0},{1,1},{2,2},{3,3},{4,4},{5,5},{6,6},{7,7},{8,9},{9,10},{10,1... | collective-permute-start | bytes 6291464 | tf_op jit(solution)/shard_map/ppermute | solution.py:604
  101.6 2.3 %rotate_top.3.top_hbm = bf16[4096,256]{1,0:T(8,128)(2,1)S(1)} custom-call(bf16[4096,256]{1,0:T(8,128)(2,1)S(1)} %get-tuple-element.51.top_hbm, bf16[4096,256]{1,0:T(8,128)(2,1)S(1)} %get-tuple-element.52.refs_0_, bf16[256,256]{1,0:T(8,128)(2,1)S(1)} %get-tuple-element.53.refs_1_, bf16[256,256]{1,0:T(8,128)(2,1)S(1)} %get-tuple-element.54.refs_2_), custom_call_target="tpu_custom_call" | custom-call | flops 1073741824 | bytes 6291456 | tf_op jit(solution)/shard_map/rotate_top/pallas_call | solution.py:547
  104.0 26.9 %collective-permute-done.9.refs_1_ = bf16[4096,256]{1,0:T(8,128)(2,1)S(1)} collective-permute-done((bf16[4096,256]{1,0:T(8,128)(2,1)S(1)}, bf16[4096,256]{1,0:T(8,128)(2,1)S(1)}, u32[]{:S(2)}, u32[]{:S(2)}) %collective-permute-start.9) | collective-permute-done | bytes 2097184 | tf_op jit(solution)/shard_map/ppermute | solution.py:604
  130.9 13.9 %rotate_low.2 = (bf16[4096,256]{1,0:T(8,128)(2,1)S(1)}, bf16[256,256]{1,0:T(8,128)(2,1)S(1)}, bf16[256,256]{1,0:T(8,128)(2,1)S(1)}) custom-call(bf16[4096,256]{1,0:T(8,128)(2,1)S(1)} %rotate_top.3.top_hbm, bf16[4096,256]{1,0:T(8,128)(2,1)S(1)} %collective-permute-done.8.refs_0_, bf16[4096,256]{1,0:T(8,128)(2,1)S(1)} %collective-permute-done.9.refs_1_), custom_call_target="tpu_custom_call" | custom-call | flops 10737418240 | bytes 16777216 | tf_op jit(solution)/shard_map/rotate_low/pallas_call | solution.py:289
  144.8 0.9 collective-permute-start.10
  145.7 2.3 %rotate_top.4.top_hbm = bf16[4096,256]{1,0:T(8,128)(2,1)S(1)} custom-call(bf16[4096,256]{1,0:T(8,128)(2,1)S(1)} %rotate_top.3.top_hbm, bf16[4096,256]{1,0:T(8,128)(2,1)S(1)} %collective-permute-done.8.refs_0_, bf16[4096,256]{1,0:T(8,128)(2,1)S(1)} %collective-permute-done.9.refs_1_, bf16[256,256]{1,0:T(8,128)(2,1)S(1)} %get-tuple-element.57.refs_2_, ...), custom_call_target="tpu_custom_call" | custom-call | flops 1073741824 | bytes 6291456 | tf_op jit(solution)/shard_map/rotate_top/pallas_call | solution.py:547
  148.1 28.3 %collective-permute-done.10.refs_0_ = bf16[4096,256]{1,0:T(8,128)(2,1)S(1)} collective-permute-done((bf16[4096,256]{1,0:T(8,128)(2,1)S(1)}, bf16[4096,256]{1,0:T(8,128)(2,1)S(1)}, u32[]{:S(2)}, u32[]{:S(2)}) %collective-permute-start.10) | collective-permute-done | bytes 2097184 | tf_op jit(solution)/shard_map/ppermute | solution.py:26
  176.4 13.9 %rotate_low.3 = (bf16[4096,256]{1,0:T(8,128)(2,1)S(1)}, bf16[256,256]{1,0:T(8,128)(2,1)S(1)}, bf16[256,256]{1,0:T(8,128)(2,1)S(1)}) custom-call(bf16[4096,256]{1,0:T(8,128)(2,1)S(1)} %rotate_top.4.top_hbm, bf16[4096,256]{1,0:T(8,128)(2,1)S(1)} %collective-permute-done.10.refs_0_), custom_call_target="tpu_custom_call" | custom-call | flops 10737418240 | bytes 16777216 | tf_op jit(solution)/shard_map/rotate_low/pallas_call | solution.py:289
  190.3 3.1 %rotate_top.5.held_ref = bf16[4096,512]{1,0:T(8,128)(2,1)} custom-call(bf16[4096,256]{1,0:T(8,128)(2,1)S(1)} %rotate_top.4.top_hbm, bf16[4096,256]{1,0:T(8,128)(2,1)S(1)} %collective-permute-done.10.refs_0_, bf16[256,256]{1,0:T(8,128)(2,1)S(1)} %get-tuple-element.61.refs_1_, bf16[256,256]{1,0:T(8,128)(2,1)S(1)} %get-tuple-element.62.refs_2_), custom_call_target="tpu_custom_call" | custom-call | flops 1073741824 | bytes 6291456 | tf_op jit(solution)/shard_map/rotate_top/pallas_call | solution.py:547
  193.5 29.4 %collective-permute-done.11.low_hbm = bf16[4096,256]{1,0:T(8,128)(2,1)S(1)} collective-permute-done((bf16[4096,256]{1,0:T(8,128)(2,1)S(1)}, bf16[4096,256]{1,0:T(8,128)(2,1)S(1)}, u32[]{:S(2)}, u32[]{:S(2)}) %collective-permute-start.11) | collective-permute-done | bytes 2097184 | tf_op jit(solution)/shard_map/ppermute | solution.py:26
  222.9 1.6 place_low.1
  (22 shorter events, 3.4 us)
Async XLA Ops:
  0.0 8.7 %copy-start.1 = (s32[64]{0:T(128)S(1)}, s32[64]{0:T(128)}, u32[]{:S(2)}) copy-start(s32[64]{0:T(128)} %dest.7) | copy-start | bytes 772
  4.1 18.0 %collective-permute-start.3 = (bf16[4096,256]{1,0:T(8,128)(2,1)}, bf16[4096,256]{1,0:T(8,128)(2,1)S(1)}, u32[]{:S(2)}, u32[]{:S(2)}) collective-permute-start(bf16[4096,256]{1,0:T(8,128)(2,1)} %pick_cross.1), channel_id=1, source_target_pairs={{0,16},{8,8},{16,0},{24,24},{1,17},{9,9},{17,1},{25,25},{2,18},{10... | collective-permute-start | bytes 6291464 | tf_op jit(solution)/shard_map/ppermute | solution.py:616
  6.4 47.7 %collective-permute-start.2 = (bf16[4096,256]{1,0:T(8,128)(2,1)}, bf16[4096,256]{1,0:T(8,128)(2,1)}, u32[]{:S(2)}, u32[]{:S(2)}) collective-permute-start(bf16[4096,256]{1,0:T(8,128)(2,1)} %pick_cross.1), channel_id=1, source_target_pairs={{8,16},{0,8},{24,0},{16,24},{9,17},{1,9},{25,1},{17,25},{10,18},{2... | collective-permute-start | bytes 6291464 | tf_op jit(solution)/shard_map/ppermute | solution.py:616
  8.7 3.4 %copy-start = (s32[4096,512]{1,0:T(8,128)S(1)}, s32[4096,512]{1,0:T(8,128)}, u32[]{:S(2)}) copy-start(s32[4096,512]{1,0:T(8,128)} %refs_3_) | copy-start | bytes 25165828
  15.9 1.3 copy-start.2
  17.2 3.5 %collective-permute-start.1 = (bf16[2048,256]{1,0:T(8,128)(2,1)}, bf16[2048,256]{1,0:T(8,128)(2,1)}, u32[]{:S(2)}, u32[]{:S(2)}) collective-permute-start(bf16[2048,256]{1,0:T(8,128)(2,1)} %get-tuple-element.38), channel_id=1, source_target_pairs={{0,8},{8,0},{16,24},{24,16},{1,9},{9,1},{17,25},{25,17},{2,10},{10... | collective-permute-start | bytes 3145736 | tf_op jit(solution)/shard_map/ppermute | solution.py:616
  17.6 40.9 %collective-permute-start = (bf16[4096,256]{1,0:T(8,128)(2,1)}, bf16[4096,256]{1,0:T(8,128)(2,1)}, u32[]{:S(2)}, u32[]{:S(2)}) collective-permute-start(bf16[4096,256]{1,0:T(8,128)(2,1)} %get-tuple-element.36), channel_id=1, source_target_pairs={{0,8},{8,0},{16,24},{24,16},{1,9},{9,1},{17,25},{25,17},{2,10},{10... | collective-permute-start | bytes 6291464 | tf_op jit(solution)/shard_map/ppermute | solution.py:616
  54.1 25.4 %collective-permute-start.7 = (bf16[2048,256]{1,0:T(8,128)(2,1)S(1)}, bf16[2048,256]{1,0:T(8,128)(2,1)S(1)}, u32[]{:S(2)}, u32[]{:S(2)}) collective-permute-start(bf16[2048,256]{1,0:T(8,128)(2,1)S(1)} %broadcast_select_fusion.1), channel_id=1, source_target_pairs={{8,24},{0,0},{24,8},{16,16},{9,25},{1,1},{25,9},{17,17},{10,26},{2... | collective-permute-start | bytes 3145736 | tf_op jit(solution)/shard_map/ppermute | solution.py:616
  56.6 24.2 %collective-permute-start.6 = (bf16[2048,256]{1,0:T(8,128)(2,1)S(1)}, bf16[2048,256]{1,0:T(8,128)(2,1)S(1)}, u32[]{:S(2)}, u32[]{:S(2)}) collective-permute-start(bf16[2048,256]{1,0:T(8,128)(2,1)S(1)} %broadcast_select_fusion.1), channel_id=1, source_target_pairs={{0,24},{8,0},{16,8},{24,16},{1,25},{9,1},{17,9},{25,17},{2,26},{10... | collective-permute-start | bytes 3145736 | tf_op jit(solution)/shard_map/ppermute | solution.py:616
  57.0 1.6 copy-start.3
  57.2 23.7 %collective-permute-start.5 = (bf16[2048,256]{1,0:T(8,128)(2,1)S(1)}, bf16[2048,256]{1,0:T(8,128)(2,1)S(1)}, u32[]{:S(2)}, u32[]{:S(2)}) collective-permute-start(bf16[2048,256]{1,0:T(8,128)(2,1)S(1)} %get-tuple-element.63), channel_id=1, source_target_pairs={{0,8},{8,0},{16,24},{24,16},{1,9},{9,1},{17,25},{25,17},{2,10},{10... | collective-permute-start | bytes 3145736 | tf_op jit(solution)/shard_map/ppermute | solution.py:616
  58.5 22.4 %collective-permute-start.4 = (bf16[2048,256]{1,0:T(8,128)(2,1)S(1)}, bf16[2048,256]{1,0:T(8,128)(2,1)S(1)}, u32[]{:S(2)}, u32[]{:S(2)}) collective-permute-start(bf16[2048,256]{1,0:T(8,128)(2,1)S(1)} %get-tuple-element.64), channel_id=1, source_target_pairs={{0,8},{8,0},{16,24},{24,16},{1,9},{9,1},{17,25},{25,17},{2,10},{10... | collective-permute-start | bytes 3145736 | tf_op jit(solution)/shard_map/ppermute | solution.py:616
  59.3 44.7 %collective-permute-start.8 = (bf16[4096,256]{1,0:T(8,128)(2,1)S(1)}, bf16[4096,256]{1,0:T(8,128)(2,1)S(1)}, u32[]{:S(2)}, u32[]{:S(2)}) collective-permute-start(bf16[4096,256]{1,0:T(8,128)(2,1)S(1)} %get-tuple-element.55), channel_id=1, source_target_pairs={{0,1},{1,2},{2,3},{3,4},{4,5},{5,6},{6,7},{7,0},{8,8},{9,9},{10,10... | collective-permute-start | bytes 6291464 | tf_op jit(solution)/shard_map/ppermute | solution.py:604
  97.6 33.3 %collective-permute-start.9 = (bf16[4096,256]{1,0:T(8,128)(2,1)S(1)}, bf16[4096,256]{1,0:T(8,128)(2,1)S(1)}, u32[]{:S(2)}, u32[]{:S(2)}) collective-permute-start(bf16[4096,256]{1,0:T(8,128)(2,1)S(1)} %get-tuple-element.56), channel_id=1, source_target_pairs={{0,0},{1,1},{2,2},{3,3},{4,4},{5,5},{6,6},{7,7},{8,9},{9,10},{10,1... | collective-permute-start | bytes 6291464 | tf_op jit(solution)/shard_map/ppermute | solution.py:604
  144.8 31.5 %collective-permute-start.10 = (bf16[4096,256]{1,0:T(8,128)(2,1)S(1)}, bf16[4096,256]{1,0:T(8,128)(2,1)S(1)}, u32[]{:S(2)}, u32[]{:S(2)}) collective-permute-start(bf16[4096,256]{1,0:T(8,128)(2,1)S(1)} %get-tuple-element.59), channel_id=1, source_target_pairs={{0,1},{1,2},{2,3},{3,4},{4,5},{5,6},{6,7},{7,0},{8,9},{9,10},{10,1... | collective-permute-start | bytes 6291464 | tf_op jit(solution)/shard_map/ppermute | solution.py:26
  190.3 32.6 %collective-permute-start.11 = (bf16[4096,256]{1,0:T(8,128)(2,1)S(1)}, bf16[4096,256]{1,0:T(8,128)(2,1)S(1)}, u32[]{:S(2)}, u32[]{:S(2)}) collective-permute-start(bf16[4096,256]{1,0:T(8,128)(2,1)S(1)} %get-tuple-element.60), channel_id=1, source_target_pairs={{0,1},{1,2},{2,3},{3,4},{4,5},{5,6},{6,7},{7,0},{8,9},{9,10},{10,1... | collective-permute-start | bytes 6291464 | tf_op jit(solution)/shard_map/ppermute | solution.py:26

commit v8 on v7

--- a/solution.py
+++ b/solution.py
@@ -461,12 +461,13 @@
             rows = pl.ds(pl.multiple_of(step * CHUNK, CHUNK), CHUNK)
             for (mean, scale), target in zip(scales, (top_ref, low_ref)):
                 target[rows, :] = ((target[rows, :].astype(f32) - mean) * scale).astype(jnp.bfloat16)
+            take_grams(rows, top_ref, low_ref, cross_ref, norm_ref)
+            return carry
+
+        lax.fori_loop(0, count, scale_rows, 0)
+        for step in range(count):
             for copy in kept(step):
                 copy.start()
-            take_grams(rows, top_ref, low_ref, cross_ref, norm_ref)
-            return carry
-
-        lax.fori_loop(0, count, scale_rows, 0)
         rotate((top_ref, low_ref), (low_out, inv_out, mix_out), (cross_ref, norm_ref, *scratch), sems)
         for step in range(count):
             for copy in kept(step):

time: 225 us -> 224 us (level)
  waiting for transfers between devices: 137 us -> 134 us
    ppermute x2, waiting for transfers between devices: 57.7 us -> 53.5 us  [passed_along(): lax.ppermute(array, axis, [(i, (i + by) % size) for i in range(size)])]
where the time goes in v8:
time: 224 us; the launch traced here: 222 us
  waiting for transfers between devices  134 us (60%)
  Pallas kernels  63.1 us (28%)
  starting transfers between devices  16.3 us (7%)
  local copies, waits for them, and re-layouts  5.6 us (2%)
  between operations  2.69 us (1%)
    ppermute x8, waiting for transfers between devices, sent(): lax.ppermute(array, 'group', [hop for chip in range(0, num_groups, 2) for...  53.9 us
    ppermute x2, waiting for transfers between devices, passed_along(): lax.ppermute(array, axis, [(i, (i + by) % size) for i in range(size)])  53.5 us
    pallas_call x2, Pallas kernels, rotate_low(): pl.pallas_call(functools.partial(round_kernel, len(lows)), in_specs=[anyw...  27.8 us
    ppermute x2, waiting for transfers between devices, next_pair(): return lax.ppermute(array, ('group', 'pair'), hops)  26.4 us
    pallas_call x2, Pallas kernels, first_round(): pl.pallas_call(functools.partial(first_kernel, tuple((len(source) for sou...  18.1 us
    ppermute x8, starting transfers between devices, sent(): lax.ppermute(array, 'group', [hop for chip in range(0, num_groups, 2) for...  9.05 us
    pallas_call x3, Pallas kernels, rotate_top(): pl.pallas_call(functools.partial(top_kernel, len(lows)), in_specs=[anywhe...  7.8 us
    ppermute x2, starting transfers between devices, next_pair(): return lax.ppermute(array, ('group', 'pair'), hops)  4.85 us
  transfers between devices with their start and end apart: 12, of which 6 were waited for; matrix products, arithmetic and copies ran while one was open for 1% of the time, Pallas kernels for 13%

profile of v8, /device:TPU:1, one launch (start us, length us, event | category | flops | bytes accessed | tf_op | source)
XLA Modules:
  0.0 222.0 jit_solution(4003936961521871703)
XLA Ops:
  0.0 4.1 %pick_cross.1 = bf16[4096,256]{1,0:T(8,128)(2,1)} custom-call(s32[64]{0:T(128)} %dest.7, s32[4096,512]{1,0:T(8,128)} %refs_3_), custom_call_target="tpu_custom_call" | custom-call | tf_op jit(solution)/shard_map/pick_cross/pallas_call | solution.py:346
  4.1 2.2 %collective-permute-start.3 = (bf16[4096,256]{1,0:T(8,128)(2,1)}, bf16[4096,256]{1,0:T(8,128)(2,1)S(1)}, u32[]{:S(2)}, u32[]{:S(2)}) collective-permute-start(bf16[4096,256]{1,0:T(8,128)(2,1)} %pick_cross.1), channel_id=1, source_target_pairs={{0,16},{8,8},{16,0},{24,24},{1,17},{9,9},{17,1},{25,25},{2,18},{10... | collective-permute-start | bytes 6291464 | tf_op jit(solution)/shard_map/ppermute | solution.py:617
  6.4 2.4 %collective-permute-start.2 = (bf16[4096,256]{1,0:T(8,128)(2,1)}, bf16[4096,256]{1,0:T(8,128)(2,1)}, u32[]{:S(2)}, u32[]{:S(2)}) collective-permute-start(bf16[4096,256]{1,0:T(8,128)(2,1)} %pick_cross.1), channel_id=1, source_target_pairs={{8,16},{0,8},{24,0},{16,24},{9,17},{1,9},{25,1},{17,25},{10,18},{2... | collective-permute-start | bytes 6291464 | tf_op jit(solution)/shard_map/ppermute | solution.py:617
  8.7 3.4 %copy-done = s32[4096,512]{1,0:T(8,128)S(1)} copy-done((s32[4096,512]{1,0:T(8,128)S(1)}, s32[4096,512]{1,0:T(8,128)}, u32[]{:S(2)}) %copy-start) | copy-done | bytes 8388632
  12.1 3.7 %pick_blocks.1 = (bf16[4096,256]{1,0:T(8,128)(2,1)}, bf16[4096,256]{1,0:T(8,128)(2,1)S(1)}, bf16[2048,256]{1,0:T(8,128)(2,1)}, bf16[2048,256]{1,0:T(8,128)(2,1)S(1)}) custom-call(s32[64]{0:T(128)S(1)} %copy-done.1, s32[4096,512]{1,0:T(8,128)S(1)} %copy-done, s32[4096,512]{1,0:T(8,128)S(1)} %copy-done, s32[4096,512]{1,0:T(8,128)S(1)} %copy-done, ...), custom_call_target="tpu_custom_call" | custom-call | tf_op jit(solution)/shard_map/pick_blocks/pallas_call | solution.py:383
  15.9 1.3 copy-done.2
  20.9 33.2 %collective-permute-done.2.refs_2_ = bf16[4096,256]{1,0:T(8,128)(2,1)} collective-permute-done((bf16[4096,256]{1,0:T(8,128)(2,1)}, bf16[4096,256]{1,0:T(8,128)(2,1)}, u32[]{:S(2)}, u32[]{:S(2)}) %collective-permute-start.2) | collective-permute-done | bytes 2097184 | tf_op jit(solution)/shard_map/ppermute | solution.py:617
  54.1 2.5 %collective-permute-start.7 = (bf16[2048,256]{1,0:T(8,128)(2,1)S(1)}, bf16[2048,256]{1,0:T(8,128)(2,1)S(1)}, u32[]{:S(2)}, u32[]{:S(2)}) collective-permute-start(bf16[2048,256]{1,0:T(8,128)(2,1)S(1)} %broadcast_select_fusion.1), channel_id=1, source_target_pairs={{8,24},{0,0},{24,8},{16,16},{9,25},{1,1},{25,9},{17,17},{10,26},{2... | collective-permute-start | bytes 3145736 | tf_op jit(solution)/shard_map/ppermute | solution.py:617
  57.2 1.3 collective-permute-start.5
  60.1 19.4 %collective-permute-done.7.refs_5_ = bf16[2048,256]{1,0:T(8,128)(2,1)S(1)} collective-permute-done((bf16[2048,256]{1,0:T(8,128)(2,1)S(1)}, bf16[2048,256]{1,0:T(8,128)(2,1)S(1)}, u32[]{:S(2)}, u32[]{:S(2)}) %collective-permute-start.7) | collective-permute-done | bytes 1048608 | tf_op jit(solution)/shard_map/ppermute | solution.py:617
  79.5 1.3 collective-permute-done.6.refs_4_
  80.9 17.4 %first_round.3 = (bf16[4096,256]{1,0:T(8,128)(2,1)S(1)}, bf16[256,256]{1,0:T(8,128)(2,1)S(1)}, bf16[256,256]{1,0:T(8,128)(2,1)S(1)}, bf16[4096,256]{1,0:T(8,128)(2,1)S(1)}, bf16[4096,256]{1,0:T(8,128)(2,1)S(1)}) custom-call(s32[64]{0:T(128)S(1)} %copy-done.1, ...), custom_call_target="tpu_custom_call", output_to_operand_aliasing={{1}: (7, {}), {2}: (8, {}), {3}: (9, {}), {4}: (10, {})} | custom-call | flops 10737418240 | bytes 16777216 | tf_op jit(solution)/shard_map/first_round/pallas_call | solution.py:485
  98.3 4.1 %collective-permute-start.9 = (bf16[4096,256]{1,0:T(8,128)(2,1)S(1)}, bf16[4096,256]{1,0:T(8,128)(2,1)S(1)}, u32[]{:S(2)}, u32[]{:S(2)}) collective-permute-start(bf16[4096,256]{1,0:T(8,128)(2,1)S(1)} %get-tuple-element.56), channel_id=1, source_target_pairs={{0,0},{1,1},{2,2},{3,3},{4,4},{5,5},{6,6},{7,7},{8,9},{9,10},{10,1... | collective-permute-start | bytes 6291464 | tf_op jit(solution)/shard_map/ppermute | solution.py:605
  102.3 2.3 %rotate_top.3.top_hbm = bf16[4096,256]{1,0:T(8,128)(2,1)S(1)} custom-call(bf16[4096,256]{1,0:T(8,128)(2,1)S(1)} %get-tuple-element.51.top_hbm, bf16[4096,256]{1,0:T(8,128)(2,1)S(1)} %get-tuple-element.52.refs_0_, bf16[256,256]{1,0:T(8,128)(2,1)S(1)} %get-tuple-element.53.refs_1_, bf16[256,256]{1,0:T(8,128)(2,1)S(1)} %get-tuple-element.54.refs_2_), custom_call_target="tpu_custom_call" | custom-call | flops 1073741824 | bytes 6291456 | tf_op jit(solution)/shard_map/rotate_top/pallas_call | solution.py:548
  104.7 26.4 %collective-permute-done.9.refs_1_ = bf16[4096,256]{1,0:T(8,128)(2,1)S(1)} collective-permute-done((bf16[4096,256]{1,0:T(8,128)(2,1)S(1)}, bf16[4096,256]{1,0:T(8,128)(2,1)S(1)}, u32[]{:S(2)}, u32[]{:S(2)}) %collective-permute-start.9) | collective-permute-done | bytes 2097184 | tf_op jit(solution)/shard_map/ppermute | solution.py:605
  131.1 13.9 %rotate_low.2 = (bf16[4096,256]{1,0:T(8,128)(2,1)S(1)}, bf16[256,256]{1,0:T(8,128)(2,1)S(1)}, bf16[256,256]{1,0:T(8,128)(2,1)S(1)}) custom-call(bf16[4096,256]{1,0:T(8,128)(2,1)S(1)} %rotate_top.3.top_hbm, bf16[4096,256]{1,0:T(8,128)(2,1)S(1)} %collective-permute-done.8.refs_0_, bf16[4096,256]{1,0:T(8,128)(2,1)S(1)} %collective-permute-done.9.refs_1_), custom_call_target="tpu_custom_call" | custom-call | flops 10737418240 | bytes 16777216 | tf_op jit(solution)/shard_map/rotate_low/pallas_call | solution.py:289
  145.0 1.2 collective-permute-start.10
  146.2 2.3 %rotate_top.4.top_hbm = bf16[4096,256]{1,0:T(8,128)(2,1)S(1)} custom-call(bf16[4096,256]{1,0:T(8,128)(2,1)S(1)} %rotate_top.3.top_hbm, bf16[4096,256]{1,0:T(8,128)(2,1)S(1)} %collective-permute-done.8.refs_0_, bf16[4096,256]{1,0:T(8,128)(2,1)S(1)} %collective-permute-done.9.refs_1_, bf16[256,256]{1,0:T(8,128)(2,1)S(1)} %get-tuple-element.57.refs_2_, ...), custom_call_target="tpu_custom_call" | custom-call | flops 1073741824 | bytes 6291456 | tf_op jit(solution)/shard_map/rotate_top/pallas_call | solution.py:548
  148.5 26.6 %collective-permute-done.10.refs_0_ = bf16[4096,256]{1,0:T(8,128)(2,1)S(1)} collective-permute-done((bf16[4096,256]{1,0:T(8,128)(2,1)S(1)}, bf16[4096,256]{1,0:T(8,128)(2,1)S(1)}, u32[]{:S(2)}, u32[]{:S(2)}) %collective-permute-start.10) | collective-permute-done | bytes 2097184 | tf_op jit(solution)/shard_map/ppermute | solution.py:26
  175.2 13.9 %rotate_low.3 = (bf16[4096,256]{1,0:T(8,128)(2,1)S(1)}, bf16[256,256]{1,0:T(8,128)(2,1)S(1)}, bf16[256,256]{1,0:T(8,128)(2,1)S(1)}) custom-call(bf16[4096,256]{1,0:T(8,128)(2,1)S(1)} %rotate_top.4.top_hbm, bf16[4096,256]{1,0:T(8,128)(2,1)S(1)} %collective-permute-done.10.refs_0_), custom_call_target="tpu_custom_call" | custom-call | flops 10737418240 | bytes 16777216 | tf_op jit(solution)/shard_map/rotate_low/pallas_call | solution.py:289
  189.1 1.2 collective-permute-start.11
  190.3 3.1 %rotate_top.5.held_ref = bf16[4096,512]{1,0:T(8,128)(2,1)} custom-call(bf16[4096,256]{1,0:T(8,128)(2,1)S(1)} %rotate_top.4.top_hbm, bf16[4096,256]{1,0:T(8,128)(2,1)S(1)} %collective-permute-done.10.refs_0_, bf16[256,256]{1,0:T(8,128)(2,1)S(1)} %get-tuple-element.61.refs_1_, bf16[256,256]{1,0:T(8,128)(2,1)S(1)} %get-tuple-element.62.refs_2_), custom_call_target="tpu_custom_call" | custom-call | flops 1073741824 | bytes 6291456 | tf_op jit(solution)/shard_map/rotate_top/pallas_call | solution.py:548
  193.4 26.8 %collective-permute-done.11.low_hbm = bf16[4096,256]{1,0:T(8,128)(2,1)S(1)} collective-permute-done((bf16[4096,256]{1,0:T(8,128)(2,1)S(1)}, bf16[4096,256]{1,0:T(8,128)(2,1)S(1)}, u32[]{:S(2)}, u32[]{:S(2)}) %collective-permute-start.11) | collective-permute-done | bytes 2097184 | tf_op jit(solution)/shard_map/ppermute | solution.py:26
  220.3 1.6 place_low.1
  (22 shorter events, 3.5 us)
Async XLA Ops:
  0.0 8.7 %copy-start.1 = (s32[64]{0:T(128)S(1)}, s32[64]{0:T(128)}, u32[]{:S(2)}) copy-start(s32[64]{0:T(128)} %dest.7) | copy-start | bytes 772
  4.1 16.8 %collective-permute-start.3 = (bf16[4096,256]{1,0:T(8,128)(2,1)}, bf16[4096,256]{1,0:T(8,128)(2,1)S(1)}, u32[]{:S(2)}, u32[]{:S(2)}) collective-permute-start(bf16[4096,256]{1,0:T(8,128)(2,1)} %pick_cross.1), channel_id=1, source_target_pairs={{0,16},{8,8},{16,0},{24,24},{1,17},{9,9},{17,1},{25,25},{2,18},{10... | collective-permute-start | bytes 6291464 | tf_op jit(solution)/shard_map/ppermute | solution.py:617
  6.4 47.7 %collective-permute-start.2 = (bf16[4096,256]{1,0:T(8,128)(2,1)}, bf16[4096,256]{1,0:T(8,128)(2,1)}, u32[]{:S(2)}, u32[]{:S(2)}) collective-permute-start(bf16[4096,256]{1,0:T(8,128)(2,1)} %pick_cross.1), channel_id=1, source_target_pairs={{8,16},{0,8},{24,0},{16,24},{9,17},{1,9},{25,1},{17,25},{10,18},{2... | collective-permute-start | bytes 6291464 | tf_op jit(solution)/shard_map/ppermute | solution.py:617
  8.7 3.4 %copy-start = (s32[4096,512]{1,0:T(8,128)S(1)}, s32[4096,512]{1,0:T(8,128)}, u32[]{:S(2)}) copy-start(s32[4096,512]{1,0:T(8,128)} %refs_3_) | copy-start | bytes 25165828
  15.9 1.3 copy-start.2
  17.2 3.5 %collective-permute-start.1 = (bf16[2048,256]{1,0:T(8,128)(2,1)}, bf16[2048,256]{1,0:T(8,128)(2,1)}, u32[]{:S(2)}, u32[]{:S(2)}) collective-permute-start(bf16[2048,256]{1,0:T(8,128)(2,1)} %get-tuple-element.38), channel_id=1, source_target_pairs={{0,8},{8,0},{16,24},{24,16},{1,9},{9,1},{17,25},{25,17},{2,10},{10... | collective-permute-start | bytes 3145736 | tf_op jit(solution)/shard_map/ppermute | solution.py:617
  17.6 40.9 %collective-permute-start = (bf16[4096,256]{1,0:T(8,128)(2,1)}, bf16[4096,256]{1,0:T(8,128)(2,1)}, u32[]{:S(2)}, u32[]{:S(2)}) collective-permute-start(bf16[4096,256]{1,0:T(8,128)(2,1)} %get-tuple-element.36), channel_id=1, source_target_pairs={{0,8},{8,0},{16,24},{24,16},{1,9},{9,1},{17,25},{25,17},{2,10},{10... | collective-permute-start | bytes 6291464 | tf_op jit(solution)/shard_map/ppermute | solution.py:617
  54.1 25.4 %collective-permute-start.7 = (bf16[2048,256]{1,0:T(8,128)(2,1)S(1)}, bf16[2048,256]{1,0:T(8,128)(2,1)S(1)}, u32[]{:S(2)}, u32[]{:S(2)}) collective-permute-start(bf16[2048,256]{1,0:T(8,128)(2,1)S(1)} %broadcast_select_fusion.1), channel_id=1, source_target_pairs={{8,24},{0,0},{24,8},{16,16},{9,25},{1,1},{25,9},{17,17},{10,26},{2... | collective-permute-start | bytes 3145736 | tf_op jit(solution)/shard_map/ppermute | solution.py:617
  56.6 24.2 %collective-permute-start.6 = (bf16[2048,256]{1,0:T(8,128)(2,1)S(1)}, bf16[2048,256]{1,0:T(8,128)(2,1)S(1)}, u32[]{:S(2)}, u32[]{:S(2)}) collective-permute-start(bf16[2048,256]{1,0:T(8,128)(2,1)S(1)} %broadcast_select_fusion.1), channel_id=1, source_target_pairs={{0,24},{8,0},{16,8},{24,16},{1,25},{9,1},{17,9},{25,17},{2,26},{10... | collective-permute-start | bytes 3145736 | tf_op jit(solution)/shard_map/ppermute | solution.py:617
  57.0 1.6 copy-start.3
  57.2 23.7 %collective-permute-start.5 = (bf16[2048,256]{1,0:T(8,128)(2,1)S(1)}, bf16[2048,256]{1,0:T(8,128)(2,1)S(1)}, u32[]{:S(2)}, u32[]{:S(2)}) collective-permute-start(bf16[2048,256]{1,0:T(8,128)(2,1)S(1)} %get-tuple-element.63), channel_id=1, source_target_pairs={{0,8},{8,0},{16,24},{24,16},{1,9},{9,1},{17,25},{25,17},{2,10},{10... | collective-permute-start | bytes 3145736 | tf_op jit(solution)/shard_map/ppermute | solution.py:617
  58.5 22.4 %collective-permute-start.4 = (bf16[2048,256]{1,0:T(8,128)(2,1)S(1)}, bf16[2048,256]{1,0:T(8,128)(2,1)S(1)}, u32[]{:S(2)}, u32[]{:S(2)}) collective-permute-start(bf16[2048,256]{1,0:T(8,128)(2,1)S(1)} %get-tuple-element.64), channel_id=1, source_target_pairs={{0,8},{8,0},{16,24},{24,16},{1,9},{9,1},{17,25},{25,17},{2,10},{10... | collective-permute-start | bytes 3145736 | tf_op jit(solution)/shard_map/ppermute | solution.py:617
  59.3 45.4 %collective-permute-start.8 = (bf16[4096,256]{1,0:T(8,128)(2,1)S(1)}, bf16[4096,256]{1,0:T(8,128)(2,1)S(1)}, u32[]{:S(2)}, u32[]{:S(2)}) collective-permute-start(bf16[4096,256]{1,0:T(8,128)(2,1)S(1)} %get-tuple-element.55), channel_id=1, source_target_pairs={{0,1},{1,2},{2,3},{3,4},{4,5},{5,6},{6,7},{7,0},{8,8},{9,9},{10,10... | collective-permute-start | bytes 6291464 | tf_op jit(solution)/shard_map/ppermute | solution.py:605
  98.3 32.8 %collective-permute-start.9 = (bf16[4096,256]{1,0:T(8,128)(2,1)S(1)}, bf16[4096,256]{1,0:T(8,128)(2,1)S(1)}, u32[]{:S(2)}, u32[]{:S(2)}) collective-permute-start(bf16[4096,256]{1,0:T(8,128)(2,1)S(1)} %get-tuple-element.56), channel_id=1, source_target_pairs={{0,0},{1,1},{2,2},{3,3},{4,4},{5,5},{6,6},{7,7},{8,9},{9,10},{10,1... | collective-permute-start | bytes 6291464 | tf_op jit(solution)/shard_map/ppermute | solution.py:605
  145.0 30.1 %collective-permute-start.10 = (bf16[4096,256]{1,0:T(8,128)(2,1)S(1)}, bf16[4096,256]{1,0:T(8,128)(2,1)S(1)}, u32[]{:S(2)}, u32[]{:S(2)}) collective-permute-start(bf16[4096,256]{1,0:T(8,128)(2,1)S(1)} %get-tuple-element.59), channel_id=1, source_target_pairs={{0,1},{1,2},{2,3},{3,4},{4,5},{5,6},{6,7},{7,0},{8,9},{9,10},{10,1... | collective-permute-start | bytes 6291464 | tf_op jit(solution)/shard_map/ppermute | solution.py:26
  189.1 31.2 %collective-permute-start.11 = (bf16[4096,256]{1,0:T(8,128)(2,1)S(1)}, bf16[4096,256]{1,0:T(8,128)(2,1)S(1)}, u32[]{:S(2)}, u32[]{:S(2)}) collective-permute-start(bf16[4096,256]{1,0:T(8,128)(2,1)S(1)} %get-tuple-element.60), channel_id=1, source_target_pairs={{0,1},{1,2},{2,3},{3,4},{4,5},{5,6},{6,7},{7,0},{8,9},{9,10},{10,1... | collective-permute-start | bytes 6291464 | tf_op jit(solution)/shard_map/ppermute | solution.py:26
